TPU v7x, 512 devices: a whole 4x4x16 slice. The times are simulated.
512 devices in a mesh: section: 2 (over core), batch: 8 (over z_hi, y), chan: 32 (over z_lo, x).
Axes of the slice: x: 4, y: 4, z: 16 (z_hi: 2, z_lo: 8; z = z_hi * 8 + z_lo), core: 2. Of those that a mesh axis runs over, the one named last changes fastest.
Arguments:
- activations: bfloat16 [2, 1, 64, 64, 1024], P('section', None, 'batch'), may hold values from -14 to 14
- kernel_a: bfloat16 [3, 3, 1024, 1024], P(None, None, None, 'chan'), may hold values from -0.0625 to 0.0625
- gain_a: float32 [1024], P('chan'), may hold values from 0.1 to 1.9
- bias_a: float32 [1024], P('chan'), may hold values from -0.5 to 0.5
- w_up: bfloat16 [1024, 4096], P(None, 'chan'), may hold values from -0.1875 to 0.1875
- gain_b: float32 [4096], P('chan'), may hold values from 0.1 to 1.9
- bias_b: float32 [4096], P('chan'), may hold values from -0.5 to 0.5
- w_down: bfloat16 [4096, 1024], P('chan'), may hold values from -0.09375 to 0.09375
- grad_out: bfloat16 [2, 1, 64, 64, 1024], P('section', None, 'batch', None, 'chan'), may hold values from -6 to 6
Outputs:
- block_output: bfloat16 [2, 1, 64, 64, 1024], P('section', None, 'batch', None, 'chan')
- grad_x: bfloat16 [2, 1, 64, 64, 1024], P('section', None, 'batch', None, 'chan')
- grad_kernel_a: float32 [3, 3, 1024, 1024], P(None, None, None, 'chan')
- grad_gain_a: float32 [1024], P('chan')
- grad_bias_a: float32 [1024], P('chan')
- grad_w_up: float32 [1024, 4096], P(None, 'chan')
- grad_gain_b: float32 [4096], P('chan')
- grad_bias_b: float32 [4096], P('chan')
- grad_w_down: float32 [4096, 1024], P('chan')
All inputs are finite; a program needn't handle non-finite values.
Results may differ from a plain program's by a relative error of at most 0.034.
The roundings to bfloat16 on the way count: a program that leaves them out, or rounds other values in their place, can miss the bound.
Values may be sent and summed in bfloat16 or wider, within the bound.
No kernel may reach another device: no remote copies, remote signals or barrier semaphores. Data moves between devices by JAX's collectives and lax.ppermute only.
A program may use at most 64 MiB of HBM per device.

v0:
```python
import jax
import jax.numpy as jnp
from jax import lax
from jax.sharding import PartitionSpec as P

EPSILON = 1e-05


def with_halo(array, sides, width):
    for axis, dim in sides:
        peers, length = (lax.axis_size(axis), array.shape[dim])
        up = [(i, (i + 1) % peers) for i in range(peers - 1)]
        down = [(j, i) for i, j in up]
        last = lax.slice_in_dim(array, length - width, length, axis=dim)
        initial = lax.slice_in_dim(array, 0, width, axis=dim)
        before = lax.ppermute(last, axis, up)
        after = lax.ppermute(initial, axis, down)
        array = jnp.concatenate([before, array, after], axis=dim)
    return array


def conv_taps(padded, kernel, height, columns):
    summed = jnp.zeros((padded.shape[0] * height * columns, kernel.shape[3]), jnp.float32)
    for tap_row in range(3):
        for tap_col in range(3):
            window = padded[:, tap_row : tap_row + height, tap_col : tap_col + columns, :].reshape(
                -1, kernel.shape[2]
            )
            summed = summed + jnp.dot(
                window, kernel[tap_row, tap_col], preferred_element_type=jnp.float32
            )
    return summed


def body(activations, kernel_a, gain_a, bias_a, w_up, gain_b, bias_b, w_down, grad_out):
    images = activations.shape[1]
    row_count = activations.shape[2]
    columns = activations.shape[3]
    channels = activations.shape[4]
    width_local = kernel_a.shape[3]
    pixel_count = images * row_count * lax.axis_size("batch") * columns
    local_pixels = images * row_count * columns
    source_rows = activations[0]
    halo_source = with_halo(source_rows, (("batch", 1),), 1)
    padded_input = jnp.pad(halo_source, ((0, 0), (0, 0), (1, 1), (0, 0)))
    conv_a = conv_taps(padded_input, kernel_a, row_count, columns)
    sums_a = lax.psum((jnp.sum(conv_a, 0), jnp.sum(conv_a * conv_a, 0)), "batch")
    mean_a = sums_a[0] / pixel_count
    var_a = sums_a[1] / pixel_count - mean_a * mean_a
    scale_a = lax.rsqrt(var_a + EPSILON)
    norm_a = (conv_a - mean_a) * scale_a
    pre_a = gain_a * norm_a + bias_a
    first_channel = lax.axis_index("chan") * width_local
    source_own = lax.dynamic_slice_in_dim(
        source_rows.reshape(local_pixels, channels), first_channel, width_local, 1
    )
    stream_own = (source_own.astype(jnp.float32) + jnp.maximum(pre_a, 0.0)).astype(jnp.bfloat16)
    cotan_own = grad_out[0].reshape(local_pixels, width_local)
    stream_full = lax.all_gather(stream_own, "chan", axis=1, tiled=True)
    hidden = jnp.dot(stream_full, w_up, preferred_element_type=jnp.float32)
    sums_b = lax.psum((jnp.sum(hidden, 0), jnp.sum(hidden * hidden, 0)), "batch")
    mean_b = sums_b[0] / pixel_count
    var_b = sums_b[1] / pixel_count - mean_b * mean_b
    scale_b = lax.rsqrt(var_b + EPSILON)
    norm_b = (hidden - mean_b) * scale_b
    pre_b = gain_b * norm_b + bias_b
    activated = jnp.maximum(pre_b, 0.0).astype(jnp.bfloat16)
    down_term = jnp.dot(activated, w_down, preferred_element_type=jnp.float32)
    down_out = lax.psum_scatter(
        down_term.astype(jnp.bfloat16), "chan", scatter_dimension=1, tiled=True
    ).astype(jnp.float32)
    out_own = (stream_own.astype(jnp.float32) + down_out).astype(jnp.bfloat16)
    cotan_full = lax.all_gather(cotan_own, "chan", axis=1, tiled=True)
    back_hidden = lax.dot_general(
        cotan_full, w_down, (((1,), (1,)), ((), ())), preferred_element_type=jnp.float32
    )
    down_grad = lax.dot_general(
        activated, cotan_full, (((0,), (0,)), ((), ())), preferred_element_type=jnp.float32
    )
    masked_b = jnp.where(pre_b > 0, back_hidden, 0.0)
    local_first_b = jnp.sum(masked_b, 0)
    local_second_b = jnp.sum(masked_b * norm_b, 0)
    back_sums_b = lax.psum((local_first_b, local_second_b), "batch")
    delta_u = (
        gain_b
        * scale_b
        * (masked_b - back_sums_b[0] / pixel_count - norm_b * back_sums_b[1] / pixel_count)
    ).astype(jnp.bfloat16)
    up_grad = lax.dot_general(
        stream_full, delta_u, (((0,), (0,)), ((), ())), preferred_element_type=jnp.float32
    )
    grads_b = (
        lax.psum(up_grad.astype(jnp.bfloat16), ("section", "batch")).astype(jnp.float32),
        lax.psum(down_grad.astype(jnp.bfloat16), ("section", "batch")).astype(jnp.float32),
        lax.psum(local_first_b.astype(jnp.bfloat16), ("section", "batch")).astype(jnp.float32),
        lax.psum(local_second_b.astype(jnp.bfloat16), ("section", "batch")).astype(jnp.float32),
    )
    up_term = lax.dot_general(
        delta_u, w_up, (((1,), (1,)), ((), ())), preferred_element_type=jnp.float32
    )
    grad_y = cotan_own.astype(jnp.float32) + lax.psum_scatter(
        up_term.astype(jnp.bfloat16), "chan", scatter_dimension=1, tiled=True
    ).astype(jnp.float32)
    masked_a = jnp.where(pre_a > 0, grad_y, 0.0)
    local_first_a = jnp.sum(masked_a, 0)
    local_second_a = jnp.sum(masked_a * norm_a, 0)
    back_sums_a = lax.psum((local_first_a, local_second_a), "batch")
    delta_a = (
        gain_a
        * scale_a
        * (masked_a - back_sums_a[0] / pixel_count - norm_a * back_sums_a[1] / pixel_count)
    ).astype(jnp.bfloat16)
    tap_grads = []
    for tap_row in range(3):
        for tap_col in range(3):
            window = padded_input[
                :, tap_row : tap_row + row_count, tap_col : tap_col + columns, :
            ].reshape(-1, channels)
            tap_grads.append(
                lax.dot_general(
                    window, delta_a, (((0,), (0,)), ((), ())), preferred_element_type=jnp.float32
                )
            )
    kernel_local = jnp.stack(tap_grads).reshape(3, 3, channels, width_local)
    delta_halo = with_halo(
        delta_a.reshape(images, row_count, columns, width_local), (("batch", 1),), 1
    )
    delta_pad = jnp.pad(delta_halo, ((0, 0), (0, 0), (1, 1), (0, 0)))
    back_conv = jnp.zeros((local_pixels, channels), jnp.float32)
    for tap_row in range(3):
        for tap_col in range(3):
            window = delta_pad[
                :, 2 - tap_row : 2 - tap_row + row_count, 2 - tap_col : 2 - tap_col + columns, :
            ].reshape(-1, width_local)
            back_conv = back_conv + lax.dot_general(
                window,
                kernel_a[tap_row, tap_col],
                (((1,), (1,)), ((), ())),
                preferred_element_type=jnp.float32,
            )
    conv_back = lax.psum_scatter(
        back_conv.astype(jnp.bfloat16), "chan", scatter_dimension=1, tiled=True
    ).astype(jnp.float32)
    grad_x_own = (grad_y + conv_back).astype(jnp.bfloat16)
    grads_a = (
        lax.psum(kernel_local.astype(jnp.bfloat16), ("section", "batch")).astype(jnp.float32),
        lax.psum(local_first_a.astype(jnp.bfloat16), ("section", "batch")).astype(jnp.float32),
        lax.psum(local_second_a.astype(jnp.bfloat16), ("section", "batch")).astype(jnp.float32),
    )
    shard_shape = (1, images, row_count, columns, width_local)
    return (
        out_own.reshape(shard_shape),
        grad_x_own.reshape(shard_shape),
        grads_a[0],
        grads_a[2],
        grads_a[1],
        grads_b[0],
        grads_b[3],
        grads_b[2],
        grads_b[1],
    )


def solution(mesh):
    placed = (
        P("section", None, "batch", None, None),
        P(None, None, None, "chan"),
        P("chan"),
        P("chan"),
        P(None, "chan"),
        P("chan"),
        P("chan"),
        P("chan", None),
        P("section", None, "batch", None, "chan"),
    )
    return jax.shard_map(
        body,
        mesh=mesh,
        in_specs=placed,
        out_specs=(
            P("section", None, "batch", None, "chan"),
            P("section", None, "batch", None, "chan"),
            P(None, None, None, "chan"),
            P("chan"),
            P("chan"),
            P(None, "chan"),
            P("chan"),
            P("chan"),
            P("chan", None),
        ),
        check_vma=False,
    )
```

profile of v0, /device:TPU:1, one launch (start us, length us, event | category | flops | bytes accessed | tf_op | source)
XLA Modules:
  0.0 1567.8 jit_solution(1932201732105232681)
XLA Ops:
  7.2 1.1 fusion.104
  8.3 4.0 collective-permute-start
  12.4 1.3 collective-permute-start.1
  13.7 1.0 constant_dynamic-slice_fusion
  14.8 1.7 fusion.49
  16.5 1.6 collective-permute-done.1
  20.0 0.8 fusion.103
  23.0 0.5 fusion.102
  23.6 45.1 %all-reduce.5 = (f32[32]{0:T(128)S(1)}, f32[32]{0:T(128)S(1)}) all-reduce(f32[32]{0:T(128)S(1)} %get-tuple-element.34, f32[32]{0:T(128)S(1)} %get-tuple-element.33), channel_id=1, replica_groups=mesh['section'=2,'batch'=8,'chan'=32] {'batch'}, use_global_device_ids=true, to_apply=%region_3.4 | all-reduce | flops 64 | bytes 512 | tf_op jit(solution)/shard_map/psum | solution.py:47
  68.7 0.5 fusion.98
  69.2 0.7 add_convert_fusion.3
  70.0 0.9 copy.23
  70.9 0.7 reshape_squeeze.7
  71.7 220.7 %all-gather.3.cloned.1.call-done = bf16[512,1024]{0,1:T(8,128)(2,1)} async-done(((bf16[512,32]{0,1:T(8,128)(2,1)}), bf16[512,1024]{0,1:T(8,128)(2,1)}) %all-gather.3.cloned.1.call-update) | async-done | bytes 1048592 | tf_op jit(solution)/shard_map/all_gather | solution.py:59
  292.4 2.4 fusion.100
  294.8 40.8 %all-reduce.4 = (f32[128]{0:T(128)S(1)}, f32[128]{0:T(128)S(1)}) all-reduce(f32[128]{0:T(128)S(1)} %get-tuple-element.30, f32[128]{0:T(128)S(1)} %get-tuple-element.29), channel_id=1, replica_groups=mesh['section'=2,'batch'=8,'chan'=32] {'batch'}, use_global_device_ids=true, to_apply=%region_7.8 | all-reduce | flops 256 | bytes 2048 | tf_op jit(solution)/shard_map/psum | solution.py:61
  335.6 1.2 fusion.97
  336.8 177.7 %all-gather.5.cloned.1.call-done = bf16[512,1024]{0,1:T(8,128)(2,1)} async-done(((bf16[512,32]{0,1:T(8,128)(2,1)}), bf16[512,1024]{0,1:T(8,128)(2,1)}) %all-gather.5.cloned.1.call-update) | async-done | bytes 1048592 | tf_op jit(solution)/shard_map/all_gather | solution.py:73
  514.5 2.5 fusion.99
  517.1 41.3 %all-reduce.3 = (f32[128]{0:T(128)}, f32[128]{0:T(128)S(1)}) all-reduce(f32[128]{0:T(128)S(1)} %get-tuple-element.28, f32[128]{0:T(128)S(1)} %get-tuple-element.27), channel_id=1, replica_groups=mesh['section'=2,'batch'=8,'chan'=32] {'batch'}, use_global_device_ids=true, to_apply=%region_12.13 | all-reduce | flops 256 | bytes 2048 | tf_op jit(solution)/shard_map/psum | solution.py:83
  558.4 1.1 multiply_convert_fusion
  559.5 1.5 convolution_convert_fusion
  561.1 2.5 convolution_convert_fusion.1
  563.7 2.5 convolution_convert_fusion.2
  566.2 2.4 convolution_convert_fusion.3
  568.6 223.1 %reduce-scatter.6.cloned.1.call-done = bf16[512,32]{0,1:T(8,128)(2,1)} async-done(((bf16[512,1024]{0,1:T(8,128)(2,1)}), bf16[512,32]{0,1:T(8,128)(2,1)}) %reduce-scatter.6.cloned.1.call-update) | async-done | bytes 32784 | tf_op jit(solution)/shard_map/reduce_scatter | solution.py:101
  791.7 1.1 fusion.101
  792.8 35.4 %all-reduce.2 = (f32[32]{0:T(128)S(1)}, f32[32]{0:T(128)S(1)}) all-reduce(f32[32]{0:T(128)S(1)} %get-tuple-element.32, f32[32]{0:T(128)S(1)} %get-tuple-element.31), channel_id=1, replica_groups=mesh['section'=2,'batch'=8,'chan'=32] {'batch'}, use_global_device_ids=true, to_apply=%region_17.18 | all-reduce | flops 64 | bytes 512 | tf_op jit(solution)/shard_map/psum | solution.py:107
  828.2 0.9 multiply_convert_fusion.1
  829.1 2.1 fusion.9
  831.4 2.3 fusion.11
  833.7 0.6 fusion.106
  834.3 1.3 collective-permute-start.2
  835.6 1.3 collective-permute-start.3
  836.9 2.1 fusion.13
  839.0 0.9 fusion.15
  839.9 0.9 fusion.7
  840.8 0.9 fusion.17
  841.8 0.9 fusion.19
  842.7 0.9 fusion.21
  843.6 2.7 fusion.47
  846.2 0.9 fusion.23
  848.4 1.8 fusion.33
  850.3 1.9 fusion.55
  852.1 1.8 fusion.51
  854.0 1.8 fusion.44
  855.8 1.8 fusion.40
  857.6 1.8 fusion.63
  860.2 1.1 copy-done.12
  861.4 6.3 add_convert_fusion
  867.8 160.2 %reduce-scatter.4.cloned.1.call-done = bf16[512,32]{0,1:T(8,128)(2,1)} async-done(((bf16[512,1024]{0,1:T(8,128)(2,1)}), bf16[512,32]{0,1:T(8,128)(2,1)}) %reduce-scatter.4.cloned.1.call-update) | async-done | bytes 32784 | tf_op jit(solution)/shard_map/reduce_scatter | solution.py:69
  1027.9 0.8 add_convert_fusion.2
  1028.8 0.6 copy.24
  1029.5 93.2 %all-reduce.6 = (bf16[32]{0:T(256)(128)(2,1)S(1)}, bf16[32]{0:T(256)(128)(2,1)S(1)}, bf16[128]{0:T(256)(128)(2,1)S(1)}, bf16[128]{0:T(256)(128)(2,1)S(1)}) all-reduce(bf16[32]{0:T(256)(128)(2,1)S(1)} %convert_element_type.109, ...), channel_id=1, replica_groups=mesh['section'=2,'batch'=8,'chan'=32] {'section','batch'}, use_global_device_ids=true, to_apply=%region_20.21 | all-reduce | flops 320 | bytes 1280 | tf_op jit(solution)/shard_map/psum | solution.py:148
  1122.6 0.5 convert_element_type.110
  1123.2 0.5 convert_element_type.112
  1124.2 0.5 convert_element_type.118
  1124.7 216.2 %all-reduce.10.cloned.1.call-done = (bf16[3,3,1024,32]{2,3,1,0:T(8,128)(2,1)}, bf16[1024,128]{1,0:T(8,128)(2,1)}, bf16[128,1024]{1,0:T(8,128)(2,1)}) async-done(((bf16[3,3,1024,32]{2,3,1,0:T(8,128)(2,1)}, bf16[1024,128]{1,0:T(8,128)(2,1)}, bf16[128,1024]{1,0:T(8,128)(2,1)}), (bf16[3,3,1024,32]{2,3,1,0:T(8,128)(2,1)}, bf16[1024,128]{1,0:T(8,128)(2,1)}, ...) | async-done | bytes 1114128 | tf_op jit(solution)/shard_map/psum | solution.py:146
  1340.9 1.8 convert_element_type.114
  1342.7 1.8 convert_element_type.120
  1344.5 2.2 convert_element_type.108
  1346.7 212.7 %reduce-scatter.8.cloned.1.call-done = bf16[512,32]{0,1:T(8,128)(2,1)} async-done(((bf16[512,1024]{0,1:T(8,128)(2,1)}), bf16[512,32]{0,1:T(8,128)(2,1)}) %reduce-scatter.8.cloned.1.call-update) | async-done | bytes 32784 | tf_op jit(solution)/shard_map/reduce_scatter | solution.py:141
  1559.4 0.8 add_convert_fusion.1
  1560.3 0.6 copy.25
  (104 shorter events, 7.4 us)
Async XLA Ops:
  7.2 285.2 %copy-start = (bf16[1024,128]{1,0:T(8,128)(2,1)S(1)}, bf16[1024,128]{1,0:T(8,128)(2,1)}, u32[]{:S(2)}) copy-start(bf16[1024,128]{1,0:T(8,128)(2,1)} %param.13) | copy-start | bytes 786436
  7.2 10.9 copy-start.1
  7.2 285.2 %all-gather.3.cloned.1.call-start = ((), (), s32[]{:S(2)}) async-start(), calls=%async_computation.3 | async-start | bytes 1081344 | tf_op jit(solution)/shard_map/all_gather | solution.py:59
  8.3 8.2 collective-permute-start
  12.4 5.7 collective-permute-start.1
  14.8 3.5 copy-start.13
  18.3 1.0 copy-start.8
  18.3 1.3 copy-start.10
  20.8 1.8 copy-start.4
  20.8 1.8 copy-start.6
  20.8 1.8 copy-start.7
  20.8 2.2 copy-start.2
  22.1 46.6 %copy-start.19 = (f32[32]{0:T(128)S(1)}, f32[32]{0:T(128)}, u32[]{:S(2)}) copy-start(f32[32]{0:T(128)} %param.11) | copy-start | bytes 388
  22.1 47.1 %copy-start.20 = (f32[32]{0:T(128)S(1)}, f32[32]{0:T(128)}, u32[]{:S(2)}) copy-start(f32[32]{0:T(128)} %param.12) | copy-start | bytes 388
  23.6 534.8 %copy-start.15 = (f32[512,32]{0,1:T(8,128)}, f32[512,32]{0,1:T(8,128)S(1)}, u32[]{:S(2)}) copy-start(f32[512,32]{0,1:T(8,128)S(1)} %get-tuple-element.77) | copy-start | bytes 196612
  70.0 444.5 %all-gather.5.cloned.1.call-start = ((), (), s32[]{:S(2)}) async-start(), calls=%async_computation.5 | async-start | bytes 1081344 | tf_op jit(solution)/shard_map/all_gather | solution.py:73
  71.6 720.0 %reduce-scatter.6.cloned.1.call-start = ((), (), s32[]{:S(2)}) async-start(), calls=%async_computation.6 | async-start | bytes 1081344 | tf_op jit(solution)/shard_map/reduce_scatter | solution.py:101
  517.1 41.3 %copy-start.25 = (f32[128]{0:T(128)}, f32[128]{0:T(128)S(1)}, u32[]{:S(2)}) copy-start(f32[128]{0:T(128)S(1)} %get-tuple-element.28) | copy-start | bytes 1540
  517.1 41.4 %copy-start.27 = (f32[128]{0:T(128)}, f32[128]{0:T(128)S(1)}, u32[]{:S(2)}) copy-start(f32[128]{0:T(128)S(1)} %get-tuple-element.27) | copy-start | bytes 1540
  561.1 466.9 %reduce-scatter.4.cloned.1.call-start = ((), (), s32[]{:S(2)}) async-start(), calls=%async_computation.4 | async-start | bytes 1081344 | tf_op jit(solution)/shard_map/reduce_scatter | solution.py:69
  563.6 777.3 %all-reduce.10.cloned.1.call-start = ((), (), s32[]{:S(2)}) async-start(), calls=%async_computation.8 | async-start | bytes 2228224 | tf_op jit(solution)/shard_map/psum | solution.py:146
  792.8 35.4 %copy-start.21 = (f32[32]{0:T(128)}, f32[32]{0:T(128)S(1)}, u32[]{:S(2)}) copy-start(f32[32]{0:T(128)S(1)} %get-tuple-element.32) | copy-start | bytes 388
  792.8 35.4 %copy-start.23 = (f32[32]{0:T(128)}, f32[32]{0:T(128)S(1)}, u32[]{:S(2)}) copy-start(f32[32]{0:T(128)S(1)} %get-tuple-element.31) | copy-start | bytes 388
  831.4 7.7 copy-start.5
  831.4 9.5 copy-start.3
  834.3 13.1 collective-permute-start.2
  835.6 11.8 collective-permute-start.3
  839.0 3.6 copy-start.9
  846.2 2.2 copy-start.14
  847.2 712.2 %reduce-scatter.8.cloned.1.call-start = ((), (), s32[]{:S(2)}) async-start(), calls=%async_computation.7 | async-start | bytes 1081344 | tf_op jit(solution)/shard_map/reduce_scatter | solution.py:141
  857.6 2.6 copy-start.11
  859.7 1.6 copy-start.12
  861.3 6.3 copy-start.28
  861.3 6.4 copy-start.26
  861.3 6.4 copy-start.24
  861.3 6.4 copy-start.22
  861.3 166.6 %copy-start.17 = (bf16[512,32]{0,1:T(8,128)(2,1)S(1)}, bf16[512,32]{0,1:T(8,128)(2,1)}, u32[]{:S(2)}) copy-start(bf16[512,32]{0,1:T(8,128)(2,1)} %add_convert_fusion.3) | copy-start | bytes 98308
  867.7 691.7 %copy-start.16 = (bf16[512,32]{0,1:T(8,128)(2,1)S(1)}, bf16[512,32]{0,1:T(8,128)(2,1)}, u32[]{:S(2)}) copy-start(bf16[512,32]{0,1:T(8,128)(2,1)} %reshape_squeeze.7) | copy-start | bytes 98308
  867.7 691.7 %copy-start.18 = (bf16[512,32]{0,1:T(8,128)(2,1)S(1)}, bf16[512,32]{0,1:T(8,128)(2,1)}, u32[]{:S(2)}) copy-start(bf16[512,32]{0,1:T(8,128)(2,1)} %reduce-scatter.6.cloned.1.call-done) | copy-start | bytes 98308
Sparse Core Ops, SparseCore 0:
  70.1 222.2 all-gather.2
  294.4 220.0 all-gather.4
  561.2 230.4 reduce-scatter.5
  795.1 232.7 reduce-scatter.3
  1032.1 308.8 all-reduce.9
  1343.6 215.7 reduce-scatter.7
where the time goes:
time: 1590 us; the launch traced here: 1570 us
  waiting for transfers between devices  1210 us (76%)
  blocking collectives  256 us (16%)
  matrix products  51.4 us (3%)
    reduce_scatter x1, waiting for transfers between devices, body(): lax.psum_scatter(up_term.astype(jnp.bfloat16), 'chan', scatter_dimension=...  223 us
    all_gather x1, waiting for transfers between devices, body(): stream_full = lax.all_gather(stream_own, 'chan', axis=1, tiled=True)  221 us
    psum x1, waiting for transfers between devices, body(): lax.psum(kernel_local.astype(jnp.bfloat16), ('section', 'batch'))  216 us
    reduce_scatter x1, waiting for transfers between devices, body(): lax.psum_scatter(back_conv.astype(jnp.bfloat16), 'chan', scatter_dimensio...  213 us
    all_gather x1, waiting for transfers between devices, body(): cotan_full = lax.all_gather(cotan_own, 'chan', axis=1, tiled=True)  178 us
    reduce_scatter x1, waiting for transfers between devices, body(): lax.psum_scatter(down_term.astype(jnp.bfloat16), 'chan', scatter_dimensio...  160 us
    psum x1, blocking collectives, body(): lax.psum(local_second_a.astype(jnp.bfloat16), ('section', 'batch'))  93.2 us
    psum x1, blocking collectives, body(): lax.psum((jnp.sum(conv_a, 0), jnp.sum(conv_a * conv_a, 0)), 'batch')  45.1 us
  transfers between devices with their start and end apart: 10, of which 7 were waited for; matrix products, arithmetic and copies ran while one was open for 4% of the time, Pallas kernels for 0%

commit v1 on v0

v1 whole, which is shorter than its diff:
```python
import jax
import jax.numpy as jnp
from jax import lax
from jax.sharding import PartitionSpec as P

EPSILON = 1e-05
F32 = jnp.float32
BF16 = jnp.bfloat16
NX = 4


def x_groups(n):
    return [[NX * z + i for i in range(NX)] for z in range(n // NX)]


def z_groups(n):
    return [[NX * z + i for z in range(n // NX)] for i in range(NX)]


def copies(value, n):
    return jnp.broadcast_to(value[None], (n,) + value.shape)


def gather_chan(own):
    n = lax.axis_size("chan")
    nz = n // NX
    line = lax.all_to_all(copies(own, nz), "chan", 0, 0, axis_index_groups=z_groups(n))
    line = line.reshape(nz * own.shape[0], own.shape[1])
    full = lax.all_to_all(copies(line, NX), "chan", 0, 0, axis_index_groups=x_groups(n))
    return full.reshape(n * own.shape[0], own.shape[1])


def scatter_chan(term):
    n = lax.axis_size("chan")
    nz = n // NX
    rows, cols = term.shape
    part = term.astype(BF16).reshape(NX, rows // NX, cols)
    part = lax.all_to_all(part, "chan", 0, 0, axis_index_groups=x_groups(n))
    part = jnp.sum(part.astype(F32), 0).astype(BF16).reshape(nz, rows // n, cols)
    part = lax.all_to_all(part, "chan", 0, 0, axis_index_groups=z_groups(n))
    return jnp.sum(part.astype(F32), 0)


def sum_batch(value):
    n = lax.axis_size("batch")
    return jnp.sum(lax.all_to_all(copies(value, n), "batch", 0, 0), 0)


def by_xz(array, n):
    block = array.shape[0] // n
    split = array.reshape(n // NX, NX, block, *array.shape[1:])
    return jnp.swapaxes(split, 0, 1).reshape(array.shape)


def by_zx(array, n):
    block = array.shape[0] // n
    split = array.reshape(NX, n // NX, block, *array.shape[1:])
    return jnp.swapaxes(split, 0, 1).reshape(array.shape)


def other_section(value):
    return lax.ppermute(value, "section", [(0, 1), (1, 0)])


def sum_grads(grad):
    rows, cols = grad.shape
    half = rows // 2
    ny = 4
    nb = lax.axis_size("batch")
    me = lax.axis_index("section")
    mine = lax.dynamic_slice_in_dim(grad, me * half, half, 0)
    theirs = lax.dynamic_slice_in_dim(grad, (1 - me) * half, half, 0)
    part = (mine.astype(F32) + other_section(theirs).astype(F32)).astype(BF16)
    y_groups = [[ny * z + i for i in range(ny)] for z in range(nb // ny)]
    part = part.reshape(ny, half // ny, cols)
    part = lax.all_to_all(part, "batch", 0, 0, axis_index_groups=y_groups)
    part = jnp.sum(part.astype(F32), 0).astype(BF16)
    across = lax.ppermute(part, "batch", [(i, (i + ny) % nb) for i in range(nb)])
    part = (part.astype(F32) + across.astype(F32)).astype(BF16)
    part = lax.all_to_all(copies(part, ny), "batch", 0, 0, axis_index_groups=y_groups)
    part = part.reshape(half, cols)
    rest = other_section(part)
    first = jnp.where(me == 0, part, rest)
    second = jnp.where(me == 0, rest, part)
    return jnp.concatenate([first, second], 0)


def halo(array, axis):
    n = lax.axis_size("batch")
    up = [(i, i + 1) for i in range(n - 1)]
    down = [(j, i) for i, j in up]
    length = array.shape[axis]
    before = lax.ppermute(lax.slice_in_dim(array, length - 1, length, axis=axis), "batch", up)
    after = lax.ppermute(lax.slice_in_dim(array, 0, 1, axis=axis), "batch", down)
    return jnp.concatenate([before, array, after], axis=axis)


def body(activations, kernel_a, gain_a, bias_a, w_up, gain_b, bias_b, w_down, grad_out):
    rows, columns, channels = activations.shape[2:]
    width = kernel_a.shape[3]
    n_chan = lax.axis_size("chan")
    local = rows * columns
    pixel_count = local * lax.axis_size("batch")
    gain_a, bias_a = gain_a[:, None], bias_a[:, None]
    gain_b, bias_b = gain_b[:, None], bias_b[:, None]

    x_own = activations[0, 0]
    taps = kernel_a.transpose(0, 1, 3, 2).reshape(9 * width, channels)
    x_halo = halo(x_own, 0).reshape((rows + 2) * columns, channels)
    cotan_own = grad_out[0, 0].transpose(2, 0, 1).reshape(width, local)
    up_rows = by_xz(w_up, n_chan)
    down_rows = by_xz(w_down.T, n_chan)

    partial = lax.dot_general(taps, x_halo, (((1,), (1,)), ((), ())), preferred_element_type=F32)
    partial = partial.reshape(3, 3, width, rows + 2, columns)
    conv_a = jnp.zeros((width, rows, columns), F32)
    for tap_row in range(3):
        for tap_col in range(3):
            piece = partial[tap_row, tap_col, :, tap_row : tap_row + rows]
            if tap_col == 0:
                piece = jnp.pad(piece[:, :, :-1], ((0, 0), (0, 0), (1, 0)))
            if tap_col == 2:
                piece = jnp.pad(piece[:, :, 1:], ((0, 0), (0, 0), (0, 1)))
            conv_a = conv_a + piece
    conv_a = conv_a.reshape(width, local)
    sums_a = sum_batch(jnp.stack([jnp.sum(conv_a, 1), jnp.sum(conv_a * conv_a, 1)]))
    mean_a = sums_a[0][:, None] / pixel_count
    var_a = sums_a[1][:, None] / pixel_count - mean_a * mean_a
    scale_a = lax.rsqrt(var_a + EPSILON)
    norm_a = (conv_a - mean_a) * scale_a
    pre_a = gain_a * norm_a + bias_a
    source_own = lax.dynamic_slice_in_dim(
        x_own.reshape(local, channels), lax.axis_index("chan") * width, width, 1
    ).T
    stream_own = (source_own.astype(F32) + jnp.maximum(pre_a, 0.0)).astype(BF16)

    cotan_full = gather_chan(cotan_own)
    stream_full = gather_chan(stream_own)
    hidden = lax.dot_general(
        up_rows, stream_full, (((0,), (0,)), ((), ())), preferred_element_type=F32
    )
    sums_b = sum_batch(jnp.stack([jnp.sum(hidden, 1), jnp.sum(hidden * hidden, 1)]))
    mean_b = sums_b[0][:, None] / pixel_count
    var_b = sums_b[1][:, None] / pixel_count - mean_b * mean_b
    scale_b = lax.rsqrt(var_b + EPSILON)
    norm_b = (hidden - mean_b) * scale_b
    pre_b = gain_b * norm_b + bias_b
    activated = jnp.maximum(pre_b, 0.0).astype(BF16)

    back_hidden = lax.dot_general(
        down_rows, cotan_full, (((0,), (0,)), ((), ())), preferred_element_type=F32
    )
    masked_b = jnp.where(pre_b > 0, back_hidden, 0.0)
    back_b = sum_batch(jnp.stack([jnp.sum(masked_b, 1), jnp.sum(masked_b * norm_b, 1)]))
    delta_u = (
        gain_b
        * scale_b
        * (
            masked_b
            - back_b[0][:, None] / pixel_count
            - norm_b * back_b[1][:, None] / pixel_count
        )
    ).astype(BF16)
    up_term = jnp.dot(up_rows, delta_u, preferred_element_type=F32)
    grad_y = cotan_own.astype(F32) + scatter_chan(up_term)

    masked_a = jnp.where(pre_a > 0, grad_y, 0.0)
    back_a = sum_batch(jnp.stack([jnp.sum(masked_a, 1), jnp.sum(masked_a * norm_a, 1)]))
    delta_a = (
        gain_a
        * scale_a
        * (
            masked_a
            - back_a[0][:, None] / pixel_count
            - norm_a * back_a[1][:, None] / pixel_count
        )
    ).astype(BF16)
    delta_halo = halo(delta_a.reshape(width, rows, columns), 1)
    delta_pad = jnp.pad(delta_halo, ((0, 0), (0, 0), (1, 1)))
    windows = jnp.stack(
        [
            delta_pad[:, 2 - tap_row : 2 - tap_row + rows, 2 - tap_col : 2 - tap_col + columns]
            for tap_row in range(3)
            for tap_col in range(3)
        ]
    ).reshape(9 * width, local)
    back_conv = lax.dot_general(
        taps, windows, (((0,), (0,)), ((), ())), preferred_element_type=F32
    )
    conv_back = scatter_chan(by_xz(back_conv.astype(BF16), n_chan))
    grad_x = (grad_y + conv_back).astype(BF16)

    down_term = jnp.dot(down_rows, activated, preferred_element_type=F32)
    out_own = (stream_own.astype(F32) + scatter_chan(down_term)).astype(BF16)

    up_grad = lax.dot_general(
        stream_full, delta_u, (((1,), (1,)), ((), ())), preferred_element_type=F32
    )
    down_grad = lax.dot_general(
        cotan_full, activated, (((1,), (1,)), ((), ())), preferred_element_type=F32
    )
    kernel_grad = jnp.dot(windows, x_own.reshape(local, channels), preferred_element_type=F32)
    units = up_grad.shape[1]
    kernel_rows = kernel_grad.reshape(-1, units)
    grads = jnp.concatenate(
        [up_grad.astype(BF16), down_grad.astype(BF16), kernel_rows.astype(BF16)], 0
    )
    grads = sum_grads(grads)
    up_total = by_zx(grads[:channels].astype(F32), n_chan)
    down_total = by_zx(grads[channels : 2 * channels].astype(F32), n_chan).T
    kernel_total = grads[2 * channels :].astype(F32).reshape(3, 3, width, channels)
    kernel_total = kernel_total.transpose(0, 1, 3, 2)
    vectors = jnp.concatenate([back_a, back_b], 1)
    vectors = vectors + other_section(vectors)

    def placed(own):
        return own.reshape(width, rows, columns).transpose(1, 2, 0)[None, None]

    return (
        placed(out_own),
        placed(grad_x),
        kernel_total,
        vectors[1, :width],
        vectors[0, :width],
        up_total,
        vectors[1, width:],
        vectors[0, width:],
        down_total,
    )


def solution(mesh):
    placed = (
        P("section", None, "batch", None, None),
        P(None, None, None, "chan"),
        P("chan"),
        P("chan"),
        P(None, "chan"),
        P("chan"),
        P("chan"),
        P("chan", None),
        P("section", None, "batch", None, "chan"),
    )
    return jax.shard_map(
        body,
        mesh=mesh,
        in_specs=placed,
        out_specs=(
            P("section", None, "batch", None, "chan"),
            P("section", None, "batch", None, "chan"),
            P(None, None, None, "chan"),
            P("chan"),
            P("chan"),
            P(None, "chan"),
            P("chan"),
            P("chan"),
            P("chan", None),
        ),
        check_vma=False,
    )
```

time: 1590 us -> 383 us (0.24)
  waiting for transfers between devices: 1210 us -> 104 us
  blocking collectives: 256 us -> 69.9 us
  starting transfers between devices: 8.33 us -> 139 us
  matrix products: 51.4 us -> 11.5 us
  local copies, waits for them, and re-layouts: 9.48 us -> 33.9 us
    reduce_scatter x3 -> x0, waiting for transfers between devices: 596 us -> none  [the longest x1 223 us: body(): lax.psum_scatter(up_term.astype(jnp.bfloat16), 'chan', scatter_dimension=...]
    all_gather x2 -> x0, waiting for transfers between devices: 398 us -> none  [the longest x1 221 us: body(): stream_full = lax.all_gather(stream_own, 'chan', axis=1, tiled=True)]
    psum x5 -> x0, blocking collectives: 256 us -> none  [the longest x1 93.2 us: body(): lax.psum(local_second_a.astype(jnp.bfloat16), ('section', 'batch'))]
    psum x1 -> x0, waiting for transfers between devices: 216 us -> none  [body(): lax.psum(kernel_local.astype(jnp.bfloat16), ('section', 'batch'))]
    all_to_all x0 -> x12, starting transfers between devices: none -> 110 us  [the longest x3 34.5 us: scatter_chan(): part = lax.all_to_all(part, 'chan', 0, 0, axis_index_groups=z_groups(n))]
    all_to_all x0 -> x12, waiting for transfers between devices: none -> 84.8 us  [the longest x3 26.5 us: scatter_chan(): part = lax.all_to_all(part, 'chan', 0, 0, axis_index_groups=z_groups(n))]
    all_to_all x0 -> x4, blocking collectives: none -> 69.9 us  [the longest x2 32.2 us: sum_batch(): return jnp.sum(lax.all_to_all(copies(value, n), 'batch', 0, 0), 0)]
    dot_general x33 -> x9, matrix products: 51.4 us -> 11.5 us  [the longest x1 1.89 us: body(): lax.dot_general(down_rows, cotan_full, (((0,), (0,)), ((), ())), preferre...]
  transfers between devices with their start and end apart: 10 -> 20, of which waited for: 7 -> 14; matrix products, arithmetic and copies ran while one was open for 4% -> 10% of each run, Pallas kernels for 0% -> 0%
where the time goes in v1:
time: 383 us; the launch traced here: 376 us
  starting transfers between devices  139 us (36%)
  waiting for transfers between devices  104 us (27%)
  blocking collectives  69.9 us (18%)
  local copies, waits for them, and re-layouts  33.9 us (9%)
  other arithmetic  16.7 us (4%)
  matrix products  11.5 us (3%)
    all_to_all x3, starting transfers between devices, scatter_chan(): part = lax.all_to_all(part, 'chan', 0, 0, axis_index_groups=z_groups(n))  34.5 us
    all_to_all x2, blocking collectives, sum_batch(): return jnp.sum(lax.all_to_all(copies(value, n), 'batch', 0, 0), 0)  32.2 us
    all_to_all x2, starting transfers between devices, sum_batch(): return jnp.sum(lax.all_to_all(copies(value, n), 'batch', 0, 0), 0)  30.3 us
    all_to_all x3, waiting for transfers between devices, scatter_chan(): part = lax.all_to_all(part, 'chan', 0, 0, axis_index_groups=z_groups(n))  26.5 us
    all_to_all x1, blocking collectives, gather_chan(): lax.all_to_all(copies(own, nz), 'chan', 0, 0, axis_index_groups=z_groups(n))  24.8 us
    all_to_all x2, waiting for transfers between devices, sum_batch(): return jnp.sum(lax.all_to_all(copies(value, n), 'batch', 0, 0), 0)  22.3 us
    ppermute x3, starting transfers between devices, other_section(): return lax.ppermute(value, 'section', [(0, 1), (1, 0)])  17.5 us
    all_to_all x2, waiting for transfers between devices, gather_chan(): lax.all_to_all(copies(line, NX), 'chan', 0, 0, axis_index_groups=x_groups...  15.6 us
  transfers between devices with their start and end apart: 20, of which 14 were waited for; matrix products, arithmetic and copies ran while one was open for 10% of the time, Pallas kernels for 0%

profile of v1, /device:TPU:1, one launch (start us, length us, event | category | flops | bytes accessed | tf_op | source)
XLA Modules:
  0.0 376.0 jit_solution(9648443088631448594)
XLA Ops:
  0.7 1.0 slice_bitcast_fusion.10
  1.7 4.0 %collective-permute-start = (bf16[1,64,1024]{2,1,0:T(8,128)(2,1)S(1)}, bf16[1,64,1024]{2,1,0:T(8,128)(2,1)S(1)}, u32[]{:S(2)}, u32[]{:S(2)}) collective-permute-start(bf16[1,64,1024]{2,1,0:T(8,128)(2,1)S(1)} %get-tuple-element.90), channel_id=1, source_target_pairs={{0,32},{32,64},{64,96},{96,128},{128,160},{160,192},{192,224},{1,3... | collective-permute-start | bytes 393224 | tf_op jit(solution)/shard_map/ppermute | solution.py:93
  5.8 1.3 collective-permute-start.1
  7.7 3.8 %collective-permute-done.1 = bf16[1,64,1024]{2,1,0:T(8,128)(2,1)S(1)} collective-permute-done((bf16[1,64,1024]{2,1,0:T(8,128)(2,1)S(1)}, bf16[1,64,1024]{2,1,0:T(8,128)(2,1)S(1)}, u32[]{:S(2)}, u32[]{:S(2)}) %collective-permute-start.1) | collective-permute-done | bytes 131104 | tf_op jit(solution)/shard_map/ppermute | solution.py:94
  11.5 1.4 pad_maximum_fusion
  12.9 1.6 convolution_bitcast_fusion
  14.4 1.6 reshape.278
  17.9 27.0 %all-to-all-start = ((f32[8,2,32]{2,1,0:T(2,128)}), f32[8,2,32]{2,1,0:T(2,128)S(1)}, u32[]{:S(2)}, u32[]{:S(2)}) async-start(f32[8,2,32]{2,1,0:T(2,128)} %broadcast_in_dim.31), calls=%async_computation | async-start | bytes 16384 | tf_op jit(solution)/shard_map/all_to_all | solution.py:46
  44.9 1.0 constant_dynamic-slice_fusion.1
  46.1 12.6 %all-to-all-done = f32[8,2,32]{2,1,0:T(2,128)S(1)} async-done(((f32[8,2,32]{2,1,0:T(2,128)}), f32[8,2,32]{2,1,0:T(2,128)S(1)}, u32[]{:S(2)}, u32[]{:S(2)}) %all-to-all-start) | async-done | bytes 2080 | tf_op jit(solution)/shard_map/all_to_all | solution.py:46
  59.4 24.8 %all_to_all.80 = bf16[8,32,512]{2,1,0:T(8,128)(2,1)S(1)} all-to-all(bf16[8,32,512]{2,1,0:T(8,128)(2,1)S(1)} %broadcast_in_dim.33), channel_id=1, replica_groups={{0,4,8,12,16,20,24,28},{1,5,9,13,17,21,25,29},{2,6,10,14,18,22,26,30},{..., dimensions={0} | all-to-all | bytes 524288 | tf_op jit(solution)/shard_map/all_to_all | solution.py:27
  84.2 1.1 broadcast_in_dim.35
  85.3 4.1 %all-to-all-start.2 = ((bf16[4,256,512]{2,1,0:T(8,128)(2,1)}), bf16[4,256,512]{2,1,0:T(8,128)(2,1)S(1)}, u32[]{:S(2)}, u32[]{:S(2)}) async-start(bf16[4,256,512]{2,1,0:T(8,128)(2,1)} %broadcast_in_dim.35), calls=%async_computation.2 | async-start | bytes 2097152 | tf_op jit(solution)/shard_map/all_to_all | solution.py:29
  89.6 9.6 %all-to-all-done.2 = bf16[4,256,512]{2,1,0:T(8,128)(2,1)S(1)} async-done(((bf16[4,256,512]{2,1,0:T(8,128)(2,1)}), bf16[4,256,512]{2,1,0:T(8,128)(2,1)S(1)}, u32[]{:S(2)}, u32[]{:S(2)}) %all-to-all-start.2) | async-done | bytes 1048608 | tf_op jit(solution)/shard_map/all_to_all | solution.py:29
  99.9 11.8 %all-to-all-start.6 = ((bf16[8,32,512]{2,1,0:T(8,128)(2,1)}), bf16[8,32,512]{2,1,0:T(8,128)(2,1)S(1)}, u32[]{:S(2)}, u32[]{:S(2)}) async-start(bf16[8,32,512]{2,1,0:T(8,128)(2,1)} %broadcast_in_dim.39), calls=%async_computation.6 | async-start | bytes 524288 | tf_op jit(solution)/shard_map/all_to_all | solution.py:27
  112.2 11.4 %all-to-all-done.6 = bf16[8,32,512]{2,1,0:T(8,128)(2,1)S(1)} async-done(((bf16[8,32,512]{2,1,0:T(8,128)(2,1)}), bf16[8,32,512]{2,1,0:T(8,128)(2,1)S(1)}, u32[]{:S(2)}, u32[]{:S(2)}) %all-to-all-start.6) | async-done | bytes 262176 | tf_op jit(solution)/shard_map/all_to_all | solution.py:27
  123.6 16.1 %all_to_all.81 = f32[8,2,128]{2,1,0:T(2,128)S(1)} all-to-all(f32[8,2,128]{2,1,0:T(2,128)S(1)} %broadcast_in_dim.36), channel_id=1, replica_groups=mesh['section'=2,'batch'=8,'chan'=32] {'batch'}, dimensions={0} | all-to-all | bytes 16384 | tf_op jit(solution)/shard_map/all_to_all | solution.py:46
  139.7 1.1 broadcast_in_dim.41
  140.7 3.6 all-to-all-start.7
  146.8 1.3 fusion.38
  148.1 6.0 %all-to-all-done.7 = bf16[4,256,512]{2,1,0:T(8,128)(2,1)S(1)} async-done(((bf16[4,256,512]{2,1,0:T(8,128)(2,1)}), bf16[4,256,512]{2,1,0:T(8,128)(2,1)S(1)}, u32[]{:S(2)}, u32[]{:S(2)}) %all-to-all-start.7) | async-done | bytes 1048608 | tf_op jit(solution)/shard_map/all_to_all | solution.py:29
  154.1 1.9 fusion.43
  156.0 16.1 %all_to_all.82 = f32[8,2,128]{2,1,0:T(2,128)S(1)} all-to-all(f32[8,2,128]{2,1,0:T(2,128)S(1)} %broadcast_in_dim.42), channel_id=1, replica_groups=mesh['section'=2,'batch'=8,'chan'=32] {'batch'}, dimensions={0} | all-to-all | bytes 16384 | tf_op jit(solution)/shard_map/all_to_all | solution.py:46
  172.2 1.0 fusion.8
  174.0 12.9 %all_to_all.83 = bf16[4,256,512]{1,2,0:T(8,128)(2,1)} all-to-all(bf16[4,256,512]{1,2,0:T(8,128)(2,1)S(1)} %bitcast.267), channel_id=1, replica_groups={{0,1,2,3},{4,5,6,7},{8,9,10,11},{12,13,14,15},{16,17,18,19},{20,21,22,2..., dimensions={0} | all-to-all | bytes 2097152 | tf_op jit(solution)/shard_map/all_to_all | solution.py:38
  186.8 1.5 reduce_sum.198
  189.2 11.6 %all-to-all-start.10 = ((bf16[8,32,512]{2,1,0:T(8,128)(2,1)}), bf16[8,32,512]{2,1,0:T(8,128)(2,1)}, u32[]{:S(2)}, u32[]{:S(2)}) async-start(bf16[8,32,512]{2,1,0:T(8,128)(2,1)} %bitcast.278), calls=%async_computation.10 | async-start | bytes 524288 | tf_op jit(solution)/shard_map/all_to_all | solution.py:40
  200.8 1.9 fusion.1
  202.7 10.2 %all-to-all-done.10 = bf16[8,32,512]{2,1,0:T(8,128)(2,1)} async-done(((bf16[8,32,512]{2,1,0:T(8,128)(2,1)}), bf16[8,32,512]{2,1,0:T(8,128)(2,1)}, u32[]{:S(2)}, u32[]{:S(2)}) %all-to-all-start.10) | async-done | bytes 262176 | tf_op jit(solution)/shard_map/all_to_all | solution.py:40
  213.9 2.2 fusion.45
  216.7 3.3 all-to-all-start.11
  220.1 1.1 convolution_convert_fusion.1
  221.2 1.8 copy.158
  223.0 1.0 copy.187
  224.0 9.7 %all-to-all-done.11 = f32[8,2,32]{2,1,0:T(2,128)S(1)} async-done(((f32[8,2,32]{2,1,0:T(2,128)}), f32[8,2,32]{2,1,0:T(2,128)S(1)}, u32[]{:S(2)}, u32[]{:S(2)}) %all-to-all-start.11) | async-done | bytes 2080 | tf_op jit(solution)/shard_map/all_to_all | solution.py:46
  233.7 3.5 all-to-all-start.4
  237.6 2.2 collective-permute-start.2
  239.8 1.3 collective-permute-start.3
  241.1 1.1 convolution_convert_fusion.5
  242.3 2.0 collective-permute-done.3
  250.5 1.4 reshape.291
  252.7 1.3 convolution_convert_fusion.3
  254.0 1.3 convert_element_type.140
  255.3 1.1 pad_maximum_fusion.1
  257.3 11.7 %collective-permute-start.4 = (bf16[2176,128]{1,0:T(8,128)(2,1)}, bf16[2176,128]{1,0:T(8,128)(2,1)}, u32[]{:S(2)}, u32[]{:S(2)}) collective-permute-start(bf16[2176,128]{1,0:T(8,128)(2,1)} %constant_dynamic-slice_fusion), channel_id=1, source_target_pairs={{0,256},{256,0},{1,257},{257,1},{2,258},{258,2},{3,259},{259,3},{4... | collective-permute-start | bytes 1671176 | tf_op jit(solution)/shard_map/ppermute | solution.py:62
  270.1 4.1 %all-to-all-start.5 = ((bf16[8,32,512]{2,1,0:T(8,128)(2,1)}), bf16[8,32,512]{2,1,0:T(8,128)(2,1)S(1)}, u32[]{:S(2)}, u32[]{:S(2)}) async-start(bf16[8,32,512]{2,1,0:T(8,128)(2,1)} %bitcast.37), calls=%async_computation.5 | async-start | bytes 524288 | tf_op jit(solution)/shard_map/all_to_all | solution.py:40
  274.3 2.1 add_convert_fusion
  276.3 12.6 %all-to-all-done.5 = bf16[8,32,512]{2,1,0:T(8,128)(2,1)S(1)} async-done(((bf16[8,32,512]{2,1,0:T(8,128)(2,1)}), bf16[8,32,512]{2,1,0:T(8,128)(2,1)S(1)}, u32[]{:S(2)}, u32[]{:S(2)}) %all-to-all-start.5) | async-done | bytes 262176 | tf_op jit(solution)/shard_map/all_to_all | solution.py:40
  288.9 14.5 %all-to-all-start.14 = ((bf16[4,544,128]{2,1,0:T(8,128)(2,1)}), bf16[4,544,128]{2,1,0:T(8,128)(2,1)S(1)}, u32[]{:S(2)}, u32[]{:S(2)}) async-start(bf16[4,544,128]{2,1,0:T(8,128)(2,1)} %bitcast.73), calls=%async_computation.14 | async-start | bytes 1114112 | tf_op jit(solution)/shard_map/all_to_all | solution.py:76
  303.4 1.7 fusion
  305.1 1.5 copy.156
  306.6 1.0 copy.157
  307.6 2.9 all-to-all-done.14
  310.6 4.5 %all-to-all-start.12 = ((bf16[4,256,512]{2,1,0:T(8,128)(2,1)}), bf16[4,256,512]{2,1,0:T(8,128)(2,1)S(1)}, u32[]{:S(2)}, u32[]{:S(2)}) async-start(bf16[4,256,512]{2,1,0:T(8,128)(2,1)} %bitcast.68), calls=%async_computation.12 | async-start | bytes 2097152 | tf_op jit(solution)/shard_map/all_to_all | solution.py:38
  315.1 1.9 collective-permute-start.5
  317.0 12.9 %collective-permute-done.5 = bf16[544,128]{1,0:T(8,128)(2,1)S(1)} collective-permute-done((bf16[544,128]{1,0:T(8,128)(2,1)S(1)}, bf16[544,128]{1,0:T(8,128)(2,1)S(1)}, u32[]{:S(2)}, u32[]{:S(2)}) %collective-permute-start.5) | collective-permute-done | bytes 139296 | tf_op jit(solution)/shard_map/ppermute | solution.py:78
  330.8 3.5 all-to-all-start.15
  335.3 6.1 %all-to-all-done.15 = bf16[4,544,128]{2,1,0:T(8,128)(2,1)S(1)} async-done(((bf16[4,544,128]{2,1,0:T(8,128)(2,1)}), bf16[4,544,128]{2,1,0:T(8,128)(2,1)S(1)}, u32[]{:S(2)}, u32[]{:S(2)}) %all-to-all-start.15) | async-done | bytes 557088 | tf_op jit(solution)/shard_map/all_to_all | solution.py:80
  341.4 18.7 %all-to-all-start.13 = ((bf16[8,32,512]{2,1,0:T(8,128)(2,1)}), bf16[8,32,512]{2,1,0:T(8,128)(2,1)S(1)}, u32[]{:S(2)}, u32[]{:S(2)}) async-start(bf16[8,32,512]{2,1,0:T(8,128)(2,1)} %bitcast.69), calls=%async_computation.13 | async-start | bytes 524288 | tf_op jit(solution)/shard_map/all_to_all | solution.py:40
  360.2 3.5 collective-permute-start.7
  365.1 2.2 collective-permute-start.6
  368.0 3.8 %all-to-all-done.13 = bf16[8,32,512]{2,1,0:T(8,128)(2,1)S(1)} async-done(((bf16[8,32,512]{2,1,0:T(8,128)(2,1)}), bf16[8,32,512]{2,1,0:T(8,128)(2,1)S(1)}, u32[]{:S(2)}, u32[]{:S(2)}) %all-to-all-start.13) | async-done | bytes 262176 | tf_op jit(solution)/shard_map/all_to_all | solution.py:40
  372.8 1.2 reshape.304
  375.0 1.0 copy.163
  (135 shorter events, 25.6 us)
Async XLA Ops:
  0.6 12.2 %copy-start = (bf16[3,3,1024,32]{2,3,1,0:T(8,128)(2,1)S(1)}, bf16[3,3,1024,32]{2,3,1,0:T(8,128)(2,1)}, u32[]{:S(2)}) copy-start(bf16[3,3,1024,32]{2,3,1,0:T(8,128)(2,1)} %param.10) | copy-start | bytes 1769476
  1.7 6.0 %collective-permute-start = (bf16[1,64,1024]{2,1,0:T(8,128)(2,1)S(1)}, bf16[1,64,1024]{2,1,0:T(8,128)(2,1)S(1)}, u32[]{:S(2)}, u32[]{:S(2)}) collective-permute-start(bf16[1,64,1024]{2,1,0:T(8,128)(2,1)S(1)} %get-tuple-element.90), channel_id=1, source_target_pairs={{0,32},{32,64},{64,96},{96,128},{128,160},{160,192},{192,224},{1,3... | collective-permute-start | bytes 393224 | tf_op jit(solution)/shard_map/ppermute | solution.py:93
  5.8 5.7 %collective-permute-start.1 = (bf16[1,64,1024]{2,1,0:T(8,128)(2,1)S(1)}, bf16[1,64,1024]{2,1,0:T(8,128)(2,1)S(1)}, u32[]{:S(2)}, u32[]{:S(2)}) collective-permute-start(bf16[1,64,1024]{2,1,0:T(8,128)(2,1)S(1)} %get-tuple-element.91), channel_id=1, source_target_pairs={{32,0},{64,32},{96,64},{128,96},{160,128},{192,160},{224,192},{33,... | collective-permute-start | bytes 393224 | tf_op jit(solution)/shard_map/ppermute | solution.py:94
  16.2 42.6 %copy-start.22 = (f32[32]{0:T(128)S(1)}, f32[32]{0:T(128)}, u32[]{:S(2)}) copy-start(f32[32]{0:T(128)} %param.11) | copy-start | bytes 388
  16.2 43.1 %copy-start.24 = (f32[32]{0:T(128)S(1)}, f32[32]{0:T(128)}, u32[]{:S(2)}) copy-start(f32[32]{0:T(128)} %param.12) | copy-start | bytes 388
  17.3 68.0 %copy-start.2 = (f32[32,8,64]{2,1,0:T(8,128)}, f32[32,8,64]{2,1,0:T(8,128)S(1)}, u32[]{:S(2)}) copy-start(f32[32,8,64]{2,1,0:T(8,128)S(1)} %get-tuple-element.81) | copy-start | bytes 196612
  17.9 40.8 %all-to-all-start = ((f32[8,2,32]{2,1,0:T(2,128)}), f32[8,2,32]{2,1,0:T(2,128)S(1)}, u32[]{:S(2)}, u32[]{:S(2)}) async-start(f32[8,2,32]{2,1,0:T(2,128)} %broadcast_in_dim.31), calls=%async_computation | async-start | bytes 16384 | tf_op jit(solution)/shard_map/all_to_all | solution.py:46
  58.7 26.5 %copy-start.20 = (f32[32]{0:T(128)}, f32[32]{0:T(128)S(1)}, u32[]{:S(2)}) copy-start(f32[32]{0:T(128)S(1)} %multiply_bitcast_fusion.3) | copy-start | bytes 388
  59.3 26.0 %copy-start.14 = (f32[32]{0:T(128)}, f32[32]{0:T(128)S(1)}, u32[]{:S(2)}) copy-start(f32[32]{0:T(128)S(1)} %get-tuple-element.101) | copy-start | bytes 388
  59.4 24.8 %copy-start.10 = (bf16[32,512]{1,0:T(8,128)(2,1)}, bf16[32,512]{1,0:T(8,128)(2,1)S(1)}, u32[]{:S(2)}) copy-start(bf16[32,512]{1,0:T(8,128)(2,1)S(1)} %fusion.35) | copy-start | bytes 98308
  85.3 4.2 %copy-start.8 = (bf16[1,1,8,64,32]{3,4,2,1,0:T(8,128)(2,1)S(1)}, bf16[1,1,8,64,32]{3,4,2,1,0:T(8,128)(2,1)}, u32[]{:S(2)}) copy-start(bf16[1,1,8,64,32]{3,4,2,1,0:T(8,128)(2,1)} %param.17) | copy-start | bytes 98308
  85.3 26.4 %copy-start.12 = (bf16[1024,128]{1,0:T(8,128)(2,1)S(1)}, bf16[1024,128]{1,0:T(8,128)(2,1)}, u32[]{:S(2)}) copy-start(bf16[1024,128]{1,0:T(8,128)(2,1)} %param.13) | copy-start | bytes 786436
  85.3 13.9 %all-to-all-start.2 = ((bf16[4,256,512]{2,1,0:T(8,128)(2,1)}), bf16[4,256,512]{2,1,0:T(8,128)(2,1)S(1)}, u32[]{:S(2)}, u32[]{:S(2)}) async-start(bf16[4,256,512]{2,1,0:T(8,128)(2,1)} %broadcast_in_dim.35), calls=%async_computation.2 | async-start | bytes 2097152 | tf_op jit(solution)/shard_map/all_to_all | solution.py:29
  99.9 23.7 %all-to-all-start.6 = ((bf16[8,32,512]{2,1,0:T(8,128)(2,1)}), bf16[8,32,512]{2,1,0:T(8,128)(2,1)S(1)}, u32[]{:S(2)}, u32[]{:S(2)}) async-start(bf16[8,32,512]{2,1,0:T(8,128)(2,1)} %broadcast_in_dim.39), calls=%async_computation.6 | async-start | bytes 524288 | tf_op jit(solution)/shard_map/all_to_all | solution.py:27
  140.7 3.7 copy-start.13
  140.7 6.1 %copy-start.17 = (f32[128]{0:T(128)S(1)}, f32[128]{0:T(128)}, u32[]{:S(2)}) copy-start(f32[128]{0:T(128)} %param.14) | copy-start | bytes 1540
  140.7 13.4 %all-to-all-start.7 = ((bf16[4,256,512]{2,1,0:T(8,128)(2,1)}), bf16[4,256,512]{2,1,0:T(8,128)(2,1)S(1)}, u32[]{:S(2)}, u32[]{:S(2)}) async-start(bf16[4,256,512]{2,1,0:T(8,128)(2,1)} %broadcast_in_dim.41), calls=%async_computation.7 | async-start | bytes 2097152 | tf_op jit(solution)/shard_map/all_to_all | solution.py:29
  146.2 0.6 copy-start.23
  146.8 9.2 %copy-start.19 = (f32[128]{0:T(128)}, f32[128]{0:T(128)S(1)}, u32[]{:S(2)}) copy-start(f32[128]{0:T(128)S(1)} %multiply_bitcast_fusion.2) | copy-start | bytes 1540
  173.2 0.7 copy-start.6
  186.8 14.0 %copy-start.18 = (f32[128]{0:T(128)S(1)}, f32[128]{0:T(128)}, u32[]{:S(2)}) copy-start(f32[128]{0:T(128)} %param.14) | copy-start | bytes 1540
  189.2 24.7 %copy-start.3 = (f32[32,8,64]{2,1,0:T(8,128)S(1)}, f32[32,8,64]{2,1,0:T(8,128)}, u32[]{:S(2)}) copy-start(f32[32,8,64]{2,1,0:T(8,128)} %copy-done.2) | copy-start | bytes 196612
  189.2 24.7 %copy-start.15 = (f32[32]{0:T(128)S(1)}, f32[32]{0:T(128)}, u32[]{:S(2)}) copy-start(f32[32]{0:T(128)} %copy-done.14) | copy-start | bytes 388
  189.2 23.7 %all-to-all-start.10 = ((bf16[8,32,512]{2,1,0:T(8,128)(2,1)}), bf16[8,32,512]{2,1,0:T(8,128)(2,1)}, u32[]{:S(2)}, u32[]{:S(2)}) async-start(bf16[8,32,512]{2,1,0:T(8,128)(2,1)} %bitcast.278), calls=%async_computation.10 | async-start | bytes 524288 | tf_op jit(solution)/shard_map/all_to_all | solution.py:40
  216.7 17.0 %all-to-all-start.11 = ((f32[8,2,32]{2,1,0:T(2,128)}), f32[8,2,32]{2,1,0:T(2,128)S(1)}, u32[]{:S(2)}, u32[]{:S(2)}) async-start(f32[8,2,32]{2,1,0:T(2,128)} %broadcast_in_dim.82), calls=%async_computation.11 | async-start | bytes 16384 | tf_op jit(solution)/shard_map/all_to_all | solution.py:46
  224.0 13.3 %copy-start.9 = (f32[32,8,64]{2,1,0:T(8,128)S(1)}, f32[32,8,64]{2,1,0:T(8,128)}, u32[]{:S(2)}) copy-start(f32[32,8,64]{2,1,0:T(8,128)} %get-tuple-element.80) | copy-start | bytes 196612
  224.0 13.3 %copy-start.16 = (f32[32]{0:T(128)S(1)}, f32[32]{0:T(128)}, u32[]{:S(2)}) copy-start(f32[32]{0:T(128)} %copy-done.14) | copy-start | bytes 388
  224.0 13.3 %copy-start.21 = (f32[32]{0:T(128)S(1)}, f32[32]{0:T(128)}, u32[]{:S(2)}) copy-start(f32[32]{0:T(128)} %copy-done.20) | copy-start | bytes 388
  224.0 13.3 %copy-start.25 = (f32[32]{0:T(128)S(1)}, f32[32]{0:T(128)}, u32[]{:S(2)}) copy-start(f32[32]{0:T(128)} %get-tuple-element.100) | copy-start | bytes 388
  224.0 17.1 %copy-start.7 = (bf16[128,512]{0,1:T(8,128)(2,1)S(1)}, bf16[128,512]{0,1:T(8,128)(2,1)}, u32[]{:S(2)}) copy-start(bf16[128,512]{0,1:T(8,128)(2,1)} %copy-done.6) | copy-start | bytes 393220
  233.7 35.3 %all-to-all-start.4 = ((bf16[4,256,512]{1,2,0:T(8,128)(2,1)}), bf16[4,256,512]{1,2,0:T(8,128)(2,1)S(1)}, u32[]{:S(2)}, u32[]{:S(2)}) async-start(bf16[4,256,512]{1,2,0:T(8,128)(2,1)} %bitcast.250), calls=%async_computation.4 | async-start | bytes 2097152 | tf_op jit(solution)/shard_map/all_to_all | solution.py:38
  237.6 4.7 %collective-permute-start.2 = (bf16[32,1,64]{2,1,0:T(2,128)(2,1)S(1)}, bf16[32,1,64]{2,1,0:T(2,128)(2,1)S(1)}, u32[]{:S(2)}, u32[]{:S(2)}) collective-permute-start(bf16[32,1,64]{2,1,0:T(2,128)(2,1)S(1)} %get-tuple-element.94), channel_id=1, source_target_pairs={{0,32},{32,64},{64,96},{96,128},{128,160},{160,192},{192,224},{1,3... | collective-permute-start | bytes 12296 | tf_op jit(solution)/shard_map/ppermute | solution.py:93
  239.8 4.5 %collective-permute-start.3 = (bf16[32,1,64]{2,1,0:T(2,128)(2,1)S(1)}, bf16[32,1,64]{2,1,0:T(2,128)(2,1)S(1)}, u32[]{:S(2)}, u32[]{:S(2)}) collective-permute-start(bf16[32,1,64]{2,1,0:T(2,128)(2,1)S(1)} %get-tuple-element.95), channel_id=1, source_target_pairs={{32,0},{64,32},{96,64},{128,96},{160,128},{192,160},{224,192},{33,... | collective-permute-start | bytes 12296 | tf_op jit(solution)/shard_map/ppermute | solution.py:94
  242.3 10.4 %copy-start.1 = (bf16[1,1,8,64,1024]{4,3,2,1,0:T(8,128)(2,1)S(1)}, bf16[1,1,8,64,1024]{4,3,2,1,0:T(8,128)(2,1)}, u32[]{:S(2)}) copy-start(bf16[1,1,8,64,1024]{4,3,2,1,0:T(8,128)(2,1)} %param.9) | copy-start | bytes 3145732
  252.0 0.7 copy-start.4
  257.3 17.0 %collective-permute-start.4 = (bf16[2176,128]{1,0:T(8,128)(2,1)}, bf16[2176,128]{1,0:T(8,128)(2,1)}, u32[]{:S(2)}, u32[]{:S(2)}) collective-permute-start(bf16[2176,128]{1,0:T(8,128)(2,1)} %constant_dynamic-slice_fusion), channel_id=1, source_target_pairs={{0,256},{256,0},{1,257},{257,1},{2,258},{258,2},{3,259},{259,3},{4... | collective-permute-start | bytes 1671176 | tf_op jit(solution)/shard_map/ppermute | solution.py:62
  270.1 18.8 %all-to-all-start.5 = ((bf16[8,32,512]{2,1,0:T(8,128)(2,1)}), bf16[8,32,512]{2,1,0:T(8,128)(2,1)S(1)}, u32[]{:S(2)}, u32[]{:S(2)}) async-start(bf16[8,32,512]{2,1,0:T(8,128)(2,1)} %bitcast.37), calls=%async_computation.5 | async-start | bytes 524288 | tf_op jit(solution)/shard_map/all_to_all | solution.py:40
  274.3 29.1 %copy-start.5 = (bf16[288,512]{1,0:T(8,128)(2,1)S(1)}, bf16[288,512]{1,0:T(8,128)(2,1)}, u32[]{:S(2)}) copy-start(bf16[288,512]{1,0:T(8,128)(2,1)} %copy-done.4) | copy-start | bytes 884740
  288.9 21.7 %all-to-all-start.14 = ((bf16[4,544,128]{2,1,0:T(8,128)(2,1)}), bf16[4,544,128]{2,1,0:T(8,128)(2,1)S(1)}, u32[]{:S(2)}, u32[]{:S(2)}) async-start(bf16[4,544,128]{2,1,0:T(8,128)(2,1)} %bitcast.73), calls=%async_computation.14 | async-start | bytes 1114112 | tf_op jit(solution)/shard_map/all_to_all | solution.py:76
  310.6 19.4 %all-to-all-start.12 = ((bf16[4,256,512]{2,1,0:T(8,128)(2,1)}), bf16[4,256,512]{2,1,0:T(8,128)(2,1)S(1)}, u32[]{:S(2)}, u32[]{:S(2)}) async-start(bf16[4,256,512]{2,1,0:T(8,128)(2,1)} %bitcast.68), calls=%async_computation.12 | async-start | bytes 2097152 | tf_op jit(solution)/shard_map/all_to_all | solution.py:38
  315.1 14.8 %collective-permute-start.5 = (bf16[544,128]{1,0:T(8,128)(2,1)S(1)}, bf16[544,128]{1,0:T(8,128)(2,1)S(1)}, u32[]{:S(2)}, u32[]{:S(2)}) collective-permute-start(bf16[544,128]{1,0:T(8,128)(2,1)S(1)} %reduce_sum.207), channel_id=1, source_target_pairs={{0,128},{32,160},{64,192},{96,224},{128,0},{160,32},{192,64},{224,... | collective-permute-start | bytes 417800 | tf_op jit(solution)/shard_map/ppermute | solution.py:78
  330.8 10.6 %all-to-all-start.15 = ((bf16[4,544,128]{2,1,0:T(8,128)(2,1)}), bf16[4,544,128]{2,1,0:T(8,128)(2,1)S(1)}, u32[]{:S(2)}, u32[]{:S(2)}) async-start(bf16[4,544,128]{2,1,0:T(8,128)(2,1)} %broadcast_in_dim.84), calls=%async_computation.15 | async-start | bytes 1114112 | tf_op jit(solution)/shard_map/all_to_all | solution.py:80
  334.3 29.4 %copy-start.11 = (bf16[32,512]{1,0:T(8,128)(2,1)S(1)}, bf16[32,512]{1,0:T(8,128)(2,1)}, u32[]{:S(2)}) copy-start(bf16[32,512]{1,0:T(8,128)(2,1)} %copy-done.10) | copy-start | bytes 98308
  341.4 30.4 %all-to-all-start.13 = ((bf16[8,32,512]{2,1,0:T(8,128)(2,1)}), bf16[8,32,512]{2,1,0:T(8,128)(2,1)S(1)}, u32[]{:S(2)}, u32[]{:S(2)}) async-start(bf16[8,32,512]{2,1,0:T(8,128)(2,1)} %bitcast.69), calls=%async_computation.13 | async-start | bytes 524288 | tf_op jit(solution)/shard_map/all_to_all | solution.py:40
  360.2 4.4 %collective-permute-start.7 = (f32[2,160]{1,0:T(2,128)S(1)}, f32[2,160]{1,0:T(2,128)S(1)}, u32[]{:S(2)}, u32[]{:S(2)}) collective-permute-start(f32[2,160]{1,0:T(2,128)S(1)} %pad_maximum_fusion.5), channel_id=1, source_target_pairs={{0,256},{256,0},{1,257},{257,1},{2,258},{258,2},{3,259},{259,3},{4... | collective-permute-start | bytes 3848 | tf_op jit(solution)/shard_map/ppermute | solution.py:62
  365.1 7.4 %collective-permute-start.6 = (bf16[2176,128]{1,0:T(8,128)(2,1)S(1)}, bf16[2176,128]{1,0:T(8,128)(2,1)S(1)}, u32[]{:S(2)}, u32[]{:S(2)}) collective-permute-start(bf16[2176,128]{1,0:T(8,128)(2,1)S(1)} %bitcast.273), channel_id=1, source_target_pairs={{0,256},{256,0},{1,257},{257,1},{2,258},{258,2},{3,259},{259,3},{4... | collective-permute-start | bytes 1671176 | tf_op jit(solution)/shard_map/ppermute | solution.py:62

commit v2 on v1

v2 whole, which is shorter than its diff:
```python
import functools

import jax
import jax.numpy as jnp
from jax import lax
from jax.experimental import pallas as pl
from jax.experimental.pallas import tpu as pltpu
from jax.sharding import PartitionSpec as P

EPSILON = 1e-05
F32 = jnp.float32
BF16 = jnp.bfloat16
NX = 4
NY = 4
LANES = 128
VMEM_LIMIT = 8 << 20
NT = (((1,), (1,)), ((), ()))
TN = (((0,), (0,)), ((), ()))


def x_groups(n):
    return [[NX * z + i for i in range(NX)] for z in range(n // NX)]


def z_groups(n):
    return [[NX * z + i for z in range(n // NX)] for i in range(NX)]


def y_groups(n):
    return [[NY * z + i for i in range(NY)] for z in range(n // NY)]


def along_x(parts):
    n = lax.axis_size("chan")
    return lax.all_to_all(parts, "chan", 0, 0, axis_index_groups=x_groups(n))


def along_z(parts):
    n = lax.axis_size("chan")
    return lax.all_to_all(parts, "chan", 0, 0, axis_index_groups=z_groups(n))


def along_y(parts):
    n = lax.axis_size("batch")
    return lax.all_to_all(parts, "batch", 0, 0, axis_index_groups=y_groups(n))


def along_batch(parts):
    return lax.all_to_all(parts, "batch", 0, 0)


def copies(value, n):
    return jnp.broadcast_to(value[None], (n,) + value.shape)


def by_xz(array, n):
    block = array.shape[0] // n
    split = array.reshape(n // NX, NX, block, *array.shape[1:])
    return jnp.swapaxes(split, 0, 1).reshape(array.shape)


def after(value, *others):
    return lax.optimization_barrier((value, *others))[0]


def partner(value, axis, step):
    n = lax.axis_size(axis)
    return lax.ppermute(value, axis, [(i, i ^ step) for i in range(n)])


def dot(a, b, dims=None):
    if dims is None:
        return jnp.dot(a, b, preferred_element_type=F32)
    return lax.dot_general(a, b, dims, preferred_element_type=F32)


def call(kernel, outs, arrays, scratch=()):
    vmem = pl.BlockSpec(memory_space=pltpu.VMEM)
    return pl.pallas_call(
        kernel,
        out_shape=tuple(jax.ShapeDtypeStruct(shape, dtype) for shape, dtype in outs),
        in_specs=[vmem] * len(arrays),
        out_specs=(vmem,) * len(outs),
        scratch_shapes=list(scratch),
        compiler_params=pltpu.CompilerParams(vmem_limit_bytes=VMEM_LIMIT),
    )(*arrays)


def lane_of(lanes):
    return lax.broadcasted_iota(jnp.int32, (1, lanes), 1)


def column_tile(first, second, start):
    lane = lane_of(LANES)
    return jnp.where(lane == start, first, jnp.where(lane == start + 1, second, 0.0))


def write_edges(out_ref, value, first, second, columns, me):
    local = value.shape[1]
    lane = lane_of(LANES)
    sums = column_tile(first, second, columns)
    low = jnp.where(lane < columns, value[:, :LANES], sums)
    last = pltpu.roll(value[:, local - LANES :], columns, 1)
    high = jnp.where(lane < columns, last, sums)
    for peer in range(out_ref.shape[0]):
        out_ref[peer] = jnp.where(me > peer, low, high)


def read_edges(in_ref, columns, me):
    count = in_ref.shape[0]
    total = in_ref[0]
    for peer in range(1, count):
        total = total + in_ref[peer]
    beyond = in_ref[jnp.minimum(me + 1, count - 1)]
    before = pltpu.roll(in_ref[jnp.maximum(me - 1, 0)], columns, 1)
    edge = jnp.where(lane_of(LANES) < columns, beyond, before)
    return edge, total[:, columns : columns + 1], total[:, columns + 1 : columns + 2]


def write_rows(out_ref, first, second):
    rows = column_tile(first, second, 0).T[:8]
    for peer in range(out_ref.shape[0]):
        out_ref[peer] = rows


def read_rows(in_ref):
    total = in_ref[0]
    for peer in range(1, in_ref.shape[0]):
        total = total + in_ref[peer]
    square = jnp.concatenate([total, jnp.zeros((LANES - 8, LANES), F32)], 0).T
    return total, square[:, 0:1], square[:, 1:2]


def shifted(value, offset, local):
    if offset != 0:
        value = pltpu.roll(value, (-offset) % value.shape[1], 1)
    return value[:, :local]


def conv_kernel(columns, x_ref, edge_ref, taps_ref, conv_ref, own_ref, pay_ref, part_ref):
    width, local = conv_ref.shape
    channels = x_ref.shape[1]
    part_ref[:, :local] = dot(taps_ref[...], x_ref[...], NT)
    part_ref[:, local:] = dot(taps_ref[...], edge_ref[...], NT)
    row = lax.broadcasted_iota(jnp.int32, (width, channels), 0) + lax.axis_index("chan") * width
    col = lax.broadcasted_iota(jnp.int32, (width, channels), 1)
    own_ref[...] = dot(jnp.where(row == col, 1.0, 0.0).astype(BF16), x_ref[...], NT)
    column = lax.rem(lane_of(local), columns)
    conv = jnp.zeros((width, local), F32)
    for tap in range(9):
        tap_row, tap_col = divmod(tap, 3)
        offset = (tap_row - 1) * columns + tap_col - 1
        piece = shifted(part_ref[tap * width : (tap + 1) * width, :], offset, local)
        if tap_col == 0:
            piece = jnp.where(column > 0, piece, 0.0)
        if tap_col == 2:
            piece = jnp.where(column < columns - 1, piece, 0.0)
        conv = conv + piece
    conv_ref[...] = conv
    first = jnp.sum(conv, 1, keepdims=True)
    second = jnp.sum(conv * conv, 1, keepdims=True)
    write_edges(pay_ref, conv, first, second, columns, lax.axis_index("batch"))


def stream_kernel(
    columns, pixels, conv_ref, own_ref, recv_ref, gain_ref, bias_ref, out_ref, norm_ref, fact_ref
):
    local = conv_ref.shape[1]
    edge, first, second = read_edges(recv_ref, columns, lax.axis_index("batch"))
    mean = first / pixels
    scale = lax.rsqrt(second / pixels - mean * mean + EPSILON)
    norm = (conv_ref[...] - mean) * scale
    norm_ref[:, :local] = norm
    norm_ref[:, local:] = (edge - mean) * scale
    pre = gain_ref[...] * norm + bias_ref[...]
    stream = (own_ref[...] + jnp.maximum(pre, 0.0)).astype(BF16)
    for peer in range(out_ref.shape[0]):
        out_ref[peer] = stream
    fact_ref[...] = jnp.broadcast_to(gain_ref[...] * scale, fact_ref.shape)


def hidden_kernel(full_ref, up_ref, hidden_ref, pay_ref):
    depth = full_ref.shape[1]
    hidden = jnp.zeros(hidden_ref.shape, F32)
    for i in range(NX):
        hidden = hidden + dot(up_ref[:, i * depth : (i + 1) * depth], full_ref[i])
    hidden_ref[...] = hidden
    write_rows(
        pay_ref,
        jnp.sum(hidden, 1, keepdims=True),
        jnp.sum(hidden * hidden, 1, keepdims=True),
    )


def active_kernel(
    pixels, hidden_ref, cotan_ref, recv_ref, gain_ref, bias_ref, cols_ref, rows_ref,
    act_ref, norm_ref, masked_ref, pay_ref, fact_ref, term_ref,
):
    _, first, second = read_rows(recv_ref)
    mean = first / pixels
    scale = lax.rsqrt(second / pixels - mean * mean + EPSILON)
    norm = (hidden_ref[...] - mean) * scale
    pre = gain_ref[...] * norm + bias_ref[...]
    act = jnp.maximum(pre, 0.0).astype(BF16)
    act_ref[...] = act
    masked = jnp.where(pre > 0, dot(cols_ref[...], cotan_ref[...]), 0.0)
    norm_ref[...] = norm
    masked_ref[...] = masked
    fact_ref[...] = jnp.broadcast_to(gain_ref[...] * scale, fact_ref.shape)
    write_rows(
        pay_ref,
        jnp.sum(masked, 1, keepdims=True),
        jnp.sum(masked * norm, 1, keepdims=True),
    )
    depth = term_ref.shape[0] // NX
    for i in range(NX):
        part = slice(i * depth, (i + 1) * depth)
        term_ref[part] = dot(rows_ref[part], act).astype(BF16)


def term_kernel(
    pixels, masked_ref, norm_ref, recv_ref, fact_ref, up_ref, delta_ref, term_ref, sums_ref
):
    total, first, second = read_rows(recv_ref)
    sums_ref[...] = total
    delta = fact_ref[:, 0:1] * (
        masked_ref[...] - first / pixels - norm_ref[...] * second / pixels
    )
    delta = delta.astype(BF16)
    delta_ref[...] = delta
    depth = term_ref.shape[1]
    for i in range(NX):
        part = slice(i * depth, (i + 1) * depth)
        term_ref[i] = dot(up_ref[part], delta).astype(BF16)


def weight_kernel(full_ref, cotan_ref, delta_ref, act_ref, grad_ref):
    depth = full_ref.shape[1]
    for i in range(NX):
        grad_ref[i] = dot(full_ref[i], delta_ref[...], NT).astype(BF16)
        cotan = cotan_ref[i * depth : (i + 1) * depth]
        grad_ref[NX + i] = dot(cotan, act_ref[...], NT).astype(BF16)


def sum_kernel(recv_ref, *refs):
    out_ref = refs[-1]
    rows = recv_ref.shape[1] // out_ref.shape[0]
    for z in range(out_ref.shape[0]):
        part = slice(z * rows, (z + 1) * rows)
        total = recv_ref[0, part].astype(F32)
        for i in range(1, NX):
            total = total + recv_ref[i, part].astype(F32)
        out_ref[z, :rows] = total.astype(BF16)
        for k, ref in enumerate(refs[:-1]):
            out_ref[z, (k + 1) * rows : (k + 2) * rows] = ref[part]


def grad_kernel(
    columns, recv_ref, cotan_ref, norm_ref, gain_ref, bias_ref, grad_ref, masked_ref, pay_ref
):
    width, local = grad_ref.shape
    total = recv_ref[0].astype(F32)
    for z in range(1, recv_ref.shape[0]):
        total = total + recv_ref[z].astype(F32)
    grad = cotan_ref[...].astype(F32) + total
    grad_ref[...] = grad
    norm = norm_ref[:, :local]
    masked = jnp.where(gain_ref[...] * norm + bias_ref[...] > 0, grad, 0.0)
    masked_ref[...] = masked
    first = jnp.sum(masked, 1, keepdims=True)
    second = jnp.sum(masked * norm, 1, keepdims=True)
    write_edges(pay_ref, masked, first, second, columns, lax.axis_index("batch"))


def back_kernel(
    columns, pixels, masked_ref, recv_ref, norm_ref, fact_ref, taps_ref, x_ref, weight_ref,
    term_ref, mine_ref, theirs_ref, sums_ref, win_ref,
):
    width, local = masked_ref.shape
    me = lax.axis_index("batch")
    edge, first, second = read_edges(recv_ref, columns, me)
    sums_ref[...] = column_tile(first, second, 0)
    masked = jnp.concatenate([masked_ref[...], edge], 1)
    delta = fact_ref[:, 0:1] * (masked - first / pixels - norm_ref[...] * second / pixels)
    lane = lane_of(local + LANES)
    beyond = (lane >= local) & (lane < local + columns)
    before = lane >= local + columns
    high = jnp.where(me == recv_ref.shape[0] - 1, 1, 0)
    low = jnp.where(me == 0, 1, 0)
    outside = jnp.where(beyond, high, jnp.where(before, low, 0))
    delta = jnp.where(outside > 0, 0.0, delta).astype(BF16).astype(F32)
    column = lax.rem(lane_of(local), columns)
    for tap in range(9):
        tap_row, tap_col = divmod(tap, 3)
        offset = (1 - tap_row) * columns + 1 - tap_col
        piece = shifted(delta, offset, local)
        if tap_col == 0:
            piece = jnp.where(column < columns - 1, piece, 0.0)
        if tap_col == 2:
            piece = jnp.where(column > 0, piece, 0.0)
        win_ref[tap * width : (tap + 1) * width, :] = piece.astype(BF16)
    depth = term_ref.shape[1]
    step = NX * width
    for z in range(depth // width):
        block = dot(taps_ref[:, z * step : (z + 1) * step], win_ref[...], TN).astype(BF16)
        for i in range(NX):
            term_ref[i, z * width : (z + 1) * width, :] = block[i * width : (i + 1) * width]
    rows = win_ref.shape[0]
    for ref, half in ((mine_ref, lax.axis_index("section")), (theirs_ref, 1 - lax.axis_index("section"))):
        for j in range(NY):
            chunk = half * NY + j
            start = pl.multiple_of(chunk * LANES, LANES)
            ref[j, :rows] = dot(win_ref[...], x_ref[:, pl.ds(start, LANES)]).astype(BF16)
            ref[j, rows:] = weight_ref[chunk]


def finish_kernel(recv_ref, grad_ref, stream_ref, grad_x_ref, out_ref):
    width = grad_ref.shape[0]
    total = recv_ref[0].astype(F32)
    for z in range(1, recv_ref.shape[0]):
        total = total + recv_ref[z].astype(F32)
    grad_x_ref[...] = (grad_ref[...] + total[:width]).astype(BF16)
    out_ref[...] = (stream_ref[0].astype(F32) + total[width:]).astype(BF16)


def spread_kernel(line_ref, rest_ref, taps_ref, up_ref, down_ref, hold_ref):
    rows = taps_ref.shape[0]
    width = rows // 9
    mine = lax.axis_index("section") == 0
    for chunk in range(2 * NY):
        j = chunk % NY
        a, b = line_ref[j], rest_ref[j]
        if chunk < NY:
            part = jnp.where(mine, a.astype(F32), b.astype(F32))
        else:
            part = jnp.where(mine, b.astype(F32), a.astype(F32))
        taps_ref[:, chunk * LANES : (chunk + 1) * LANES] = part[:rows]
        target = up_ref if chunk < NX else hold_ref
        for z in range((part.shape[0] - rows) // width):
            at = (z * NX + chunk % NX) * width
            target[at : at + width] = part[rows + z * width : rows + (z + 1) * width]
    for block in range(hold_ref.shape[0] // LANES):
        part = slice(block * LANES, (block + 1) * LANES)
        down_ref[:, part] = hold_ref[part].T


def body(activations, kernel_a, gain_a, bias_a, w_up, gain_b, bias_b, w_down, grad_out):
    rows, columns, channels = activations.shape[2:]
    width = kernel_a.shape[3]
    units = w_up.shape[1]
    n_chan = lax.axis_size("chan")
    n_batch = lax.axis_size("batch")
    nz = n_chan // NX
    local = rows * columns
    pixels = local * n_batch
    gain_a, bias_a = gain_a[:, None], bias_a[:, None]
    gain_b, bias_b = gain_b[:, None], bias_b[:, None]

    x_rows = activations.reshape(local, channels)
    taps = kernel_a.transpose(0, 1, 3, 2).reshape(9 * width, channels)
    cotan_own = grad_out[0, 0].transpose(2, 0, 1).reshape(width, local)
    cotan_line = along_z(copies(cotan_own, nz)).reshape(nz * width, local)
    cotan_full = lax.all_gather(
        cotan_line, "chan", axis_index_groups=x_groups(n_chan), tiled=True
    )
    up = [(i, i + 1) for i in range(n_batch - 1)]
    down = [(j, i) for i, j in up]
    before = lax.ppermute(x_rows[local - columns :], "batch", up)
    beyond = lax.ppermute(x_rows[:columns], "batch", down)
    edge = jnp.concatenate([beyond, before], 0)
    up_rows = by_xz(w_up, n_chan)
    down_rows = by_xz(w_down.T, n_chan)
    up_cols, down_cols = up_rows.T, down_rows.T

    conv_a, source, pay = call(
        functools.partial(conv_kernel, columns),
        [((width, local), F32), ((width, local), F32), ((n_batch, width, LANES), F32)],
        (x_rows, edge, taps),
        [pltpu.VMEM((9 * width, local + 2 * columns), F32)],
    )
    recv = along_batch(after(pay, cotan_line, up_cols, down_cols))
    stream, norm_a, fact_a = call(
        functools.partial(stream_kernel, columns, pixels),
        [
            ((nz, width, local), BF16),
            ((width, local + LANES), F32),
            ((width, LANES), F32),
        ],
        (conv_a, source, recv, gain_a, bias_a),
    )
    stream_line = along_z(stream)
    depth = nz * width
    full = along_x(copies(stream_line.reshape(depth, local), NX))
    hidden, pay = call(
        hidden_kernel,
        [((units, local), F32), ((n_batch, 8, LANES), F32)],
        (full, up_cols),
    )
    act, norm_b, masked_b, pay, fact_b, down_term = call(
        functools.partial(active_kernel, pixels),
        [
            ((units, local), BF16),
            ((units, local), F32),
            ((units, local), F32),
            ((n_batch, 8, LANES), F32),
            ((units, LANES), F32),
            ((channels, local), BF16),
        ],
        (hidden, cotan_full, along_batch(pay), gain_b, bias_b, down_cols, down_rows),
    )
    down_part = lax.psum_scatter(
        down_term, "chan", axis_index_groups=x_groups(n_chan), tiled=True
    )
    delta_u, term, sums_b = call(
        functools.partial(term_kernel, pixels),
        [((units, local), BF16), ((NX, depth, local), BF16), ((8, LANES), F32)],
        (masked_b, norm_b, along_batch(pay), fact_b, up_rows),
    )
    (weight_grad,) = call(
        weight_kernel, [((2 * NX, depth, units), BF16)], (full, cotan_full, delta_u, act)
    )
    (part,) = call(
        sum_kernel, [((nz, width, local), BF16)], (along_x(term),)
    )
    part = after(part, weight_grad, down_part)
    grad_y, masked_a, pay = call(
        functools.partial(grad_kernel, columns),
        [
            ((width, local), F32),
            ((width, local), F32),
            ((n_batch, width, LANES), F32),
        ],
        (along_z(part), cotan_own, norm_a, gain_a, bias_a),
    )
    taps_rows = 9 * width
    chunk_rows = taps_rows + depth
    term, mine, theirs, sums_a = call(
        functools.partial(back_kernel, columns, pixels),
        [
            ((NX, depth, local), BF16),
            ((NY, chunk_rows, LANES), BF16),
            ((NY, chunk_rows, LANES), BF16),
            ((width, LANES), F32),
        ],
        (masked_a, along_batch(pay), norm_a, fact_a, taps, x_rows, weight_grad),
        [pltpu.VMEM((taps_rows, local), BF16)],
    )
    recv = along_x(term)
    theirs = partner(theirs, "section", 1)
    vectors = jnp.concatenate([sums_a[:, :2].T, sums_b[:2]], 1)
    vectors = vectors + partner(vectors, "section", 1)
    half = (mine.astype(F32) + theirs.astype(F32)).astype(BF16)
    recv = after(recv, half, vectors)
    half = along_y(after(half, recv))
    half = jnp.sum(half.astype(F32), 0).astype(BF16)
    across = partner(half, "batch", NY)
    (part,) = call(sum_kernel, [((nz, 2 * width, local), BF16)], (recv, down_part))
    recv = along_z(after(part, half))
    grad_x, out_own = call(
        finish_kernel,
        [((width, local), BF16), ((width, local), BF16)],
        (recv, grad_y, stream),
    )
    half = (half.astype(F32) + across.astype(F32)).astype(BF16)
    line = along_y(copies(after(half, recv), NY))
    rest = partner(line, "section", 1)
    kernel_total, up_total, down_total = call(
        spread_kernel,
        [((taps_rows, channels), F32), ((channels, units), F32), ((units, channels), F32)],
        (line, rest),
        [pltpu.VMEM((channels, units), F32)],
    )
    kernel_total = kernel_total.reshape(3, 3, width, channels).transpose(0, 1, 3, 2)

    def placed(own):
        return own.reshape(width, rows, columns).transpose(1, 2, 0)[None, None]

    return (
        placed(out_own),
        placed(grad_x),
        kernel_total,
        vectors[1, :width],
        vectors[0, :width],
        up_total,
        vectors[1, width:],
        vectors[0, width:],
        down_total,
    )


def solution(mesh):
    placed = (
        P("section", None, "batch", None, None),
        P(None, None, None, "chan"),
        P("chan"),
        P("chan"),
        P(None, "chan"),
        P("chan"),
        P("chan"),
        P("chan", None),
        P("section", None, "batch", None, "chan"),
    )
    return jax.shard_map(
        body,
        mesh=mesh,
        in_specs=placed,
        out_specs=(
            P("section", None, "batch", None, "chan"),
            P("section", None, "batch", None, "chan"),
            P(None, None, None, "chan"),
            P("chan"),
            P("chan"),
            P(None, "chan"),
            P("chan"),
            P("chan"),
            P("chan", None),
        ),
        check_vma=False,
    )
```

time: 383 us -> 341 us (0.89); the launches traced: 376 us -> 339 us
  blocking collectives: 69.9 us -> 49.7 us
  starting transfers between devices: 139 us -> 123 us
  other arithmetic: 16.7 us -> 2.18 us
  between operations: 1.28 us -> 14.5 us
  waiting for transfers between devices: 104 us -> 117 us
  local copies, waits for them, and re-layouts: 33.9 us -> 21.8 us
  Pallas kernels: 0 us -> 11.9 us
  matrix products: 11.5 us -> 0 us
    all_to_all x12 -> x10, starting transfers between devices: 110 us -> 88.4 us  [the longest x3 38 us: along_z(): return lax.all_to_all(parts, 'chan', 0, 0, axis_index_groups=z_groups(n))]
    all_to_all x4 -> x3, blocking collectives: 69.9 us -> 49.7 us  [the longest x1 22.7 us: along_z(): return lax.all_to_all(parts, 'chan', 0, 0, axis_index_groups=z_groups(n))]
    all_to_all x12 -> x10, waiting for transfers between devices: 84.8 us -> 99.4 us  [the longest x3 39.6 us: along_batch(): return lax.all_to_all(parts, 'batch', 0, 0)]
    pallas_call x0 -> x12, Pallas kernels: none -> 11.9 us  [call(): pl.pallas_call(kernel, out_shape=tuple((jax.ShapeDtypeStruct(shape, dtype...]
    dot_general x9 -> x0, matrix products: 11.5 us -> none  [the longest x1 1.89 us: body(): lax.dot_general(down_rows, cotan_full, (((0,), (0,)), ((), ())), preferre...]
    reduce_sum x13 -> x1, other arithmetic: 6.94 us -> 0.09 us  [body(): half = jnp.sum(half.astype(F32), 0).astype(BF16)]
    ppermute x8 -> x6, starting transfers between devices: 28.3 us -> 34.3 us  [the longest x4 28.2 us: partner(): return lax.ppermute(value, axis, [(i, i ^ step) for i in range(n)])]
    unnamed x64 -> x73, local copies, waits for them, and re-layouts: 8.89 us -> 14.1 us
  transfers between devices with their start and end apart: 20 -> 18, of which waited for: 14 -> 12; matrix products, arithmetic and copies ran while one was open for 10% -> 2% of each run, Pallas kernels for 0% -> 2%
where the time goes in v2:
time: 341 us; the launch traced here: 339 us
  starting transfers between devices  123 us (36%)
  waiting for transfers between devices  117 us (34%)
  blocking collectives  49.7 us (15%)
  local copies, waits for them, and re-layouts  21.8 us (6%)
  between operations  14.5 us (4%)
  Pallas kernels  11.9 us (3%)
    all_to_all x3, waiting for transfers between devices, along_batch(): return lax.all_to_all(parts, 'batch', 0, 0)  39.6 us
    all_to_all x3, starting transfers between devices, along_z(): return lax.all_to_all(parts, 'chan', 0, 0, axis_index_groups=z_groups(n))  38 us
    all_to_all x3, starting transfers between devices, along_batch(): return lax.all_to_all(parts, 'batch', 0, 0)  35.6 us
    ppermute x4, starting transfers between devices, partner(): return lax.ppermute(value, axis, [(i, i ^ step) for i in range(n)])  28.2 us
    all_to_all x3, waiting for transfers between devices, along_x(): return lax.all_to_all(parts, 'chan', 0, 0, axis_index_groups=x_groups(n))  27.7 us
    all_to_all x3, waiting for transfers between devices, along_z(): return lax.all_to_all(parts, 'chan', 0, 0, axis_index_groups=z_groups(n))  26 us
    all_to_all x1, blocking collectives, along_z(): return lax.all_to_all(parts, 'chan', 0, 0, axis_index_groups=z_groups(n))  22.7 us
    all_to_all x1, blocking collectives, along_batch(): return lax.all_to_all(parts, 'batch', 0, 0)  17.2 us
  transfers between devices with their start and end apart: 18, of which 12 were waited for; matrix products, arithmetic and copies ran while one was open for 2% of the time, Pallas kernels for 2%

profile of v2, /device:TPU:1, one launch (start us, length us, event | category | flops | bytes accessed | tf_op | source)
XLA Modules:
  0.0 339.3 jit_solution(15389479824545965217)
XLA Ops:
  7.2 1.0 copy.32
  8.3 0.7 broadcast_in_dim.39
  9.0 13.1 %all-to-all-start = ((bf16[8,32,512]{2,1,0:T(8,128)(2,1)}), bf16[8,32,512]{2,1,0:T(8,128)(2,1)S(1)}, u32[]{:S(2)}, u32[]{:S(2)}) async-start(bf16[8,32,512]{2,1,0:T(8,128)(2,1)} %broadcast_in_dim.39), calls=%async_computation | async-start | bytes 524288 | tf_op jit(solution)/shard_map/all_to_all | solution.py:40
  22.2 1.4 collective-permute-start
  23.6 4.6 %collective-permute-start.1 = (bf16[64,1024]{1,0:T(8,128)(2,1)S(1)}, bf16[64,1024]{1,0:T(8,128)(2,1)}, u32[]{:S(2)}, u32[]{:S(2)}) collective-permute-start(bf16[64,1024]{1,0:T(8,128)(2,1)S(1)} %get-tuple-element.80), channel_id=1, source_target_pairs={{0,32},{32,64},{64,96},{96,128},{128,160},{160,192},{192,224},{1,3... | collective-permute-start | bytes 393224 | tf_op jit(solution)/shard_map/ppermute | solution.py:368
  28.5 1.0 collective-permute-done.1
  29.5 0.9 pad_maximum_fusion.edge_ref
  30.5 1.7 shard_map.160
  32.2 2.1 all-to-all-done
  34.3 23.4 %all-to-all-start.1 = ((f32[8,32,128]{2,1,0:T(8,128)}), f32[8,32,128]{2,1,0:T(8,128)S(1)}, u32[]{:S(2)}, u32[]{:S(2)}) async-start(f32[8,32,128]{2,1,0:T(8,128)} %get-tuple-element.47), calls=%async_computation.1 | async-start | bytes 262144 | tf_op jit(solution)/shard_map/all_to_all | solution.py:49
  57.9 14.0 %all-to-all-done.1.recv_ref = f32[8,32,128]{2,1,0:T(8,128)S(1)} async-done(((f32[8,32,128]{2,1,0:T(8,128)}), f32[8,32,128]{2,1,0:T(8,128)S(1)}, u32[]{:S(2)}, u32[]{:S(2)}) %all-to-all-start.1) | async-done | bytes 131104 | tf_op jit(solution)/shard_map/all_to_all | solution.py:49
  71.9 0.9 shard_map.161
  72.8 17.9 %all-to-all-start.2 = ((bf16[8,32,512]{2,1,0:T(8,128)(2,1)}), bf16[8,32,512]{2,1,0:T(8,128)(2,1)S(1)}, u32[]{:S(2)}, u32[]{:S(2)}) async-start(bf16[8,32,512]{2,1,0:T(8,128)(2,1)} %get-tuple-element.48.stream_ref), calls=%async_computation.2 | async-start | bytes 524288 | tf_op jit(solution)/shard_map/all_to_all | solution.py:40
  90.7 0.7 all-gather.2.cloned.1.call-update
  91.4 11.2 %all-to-all-done.2 = bf16[8,32,512]{2,1,0:T(8,128)(2,1)S(1)} async-done(((bf16[8,32,512]{2,1,0:T(8,128)(2,1)}), bf16[8,32,512]{2,1,0:T(8,128)(2,1)S(1)}, u32[]{:S(2)}, u32[]{:S(2)}) %all-to-all-start.2) | async-done | bytes 262176 | tf_op jit(solution)/shard_map/all_to_all | solution.py:40
  102.6 1.1 broadcast_in_dim.43
  103.7 4.0 %all-to-all-start.3 = ((bf16[4,256,512]{2,1,0:T(8,128)(2,1)}), bf16[4,256,512]{2,1,0:T(8,128)(2,1)S(1)}, u32[]{:S(2)}, u32[]{:S(2)}) async-start(bf16[4,256,512]{2,1,0:T(8,128)(2,1)} %broadcast_in_dim.43), calls=%async_computation.3 | async-start | bytes 2097152 | tf_op jit(solution)/shard_map/all_to_all | solution.py:35
  107.8 17.6 %all-to-all-done.3.full_ref = bf16[4,256,512]{2,1,0:T(8,128)(2,1)S(1)} async-done(((bf16[4,256,512]{2,1,0:T(8,128)(2,1)}), bf16[4,256,512]{2,1,0:T(8,128)(2,1)S(1)}, u32[]{:S(2)}, u32[]{:S(2)}) %all-to-all-start.3) | async-done | bytes 1048608 | tf_op jit(solution)/shard_map/all_to_all | solution.py:35
  125.4 1.0 shard_map.162
  126.5 3.3 all-to-all-start.4
  130.0 0.7 copy.39.gain_ref
  130.8 0.7 copy.40.bias_ref
  131.5 12.1 %all-to-all-done.4.recv_ref = f32[8,8,128]{2,1,0:T(8,128)S(1)} async-done(((f32[8,8,128]{2,1,0:T(8,128)}), f32[8,8,128]{2,1,0:T(8,128)S(1)}, u32[]{:S(2)}, u32[]{:S(2)}) %all-to-all-start.4) | async-done | bytes 32800 | tf_op jit(solution)/shard_map/all_to_all | solution.py:49
  144.2 1.2 copy-done.1
  145.4 0.8 copy-done.13
  146.3 0.8 copy-done.14
  147.1 0.8 copy-done.16
  147.9 0.8 shard_map.163
  148.7 1.0 copy-done.7
  149.7 0.7 copy-done.11
  150.4 0.6 copy-done.17
  152.3 17.2 %all_to_all.65.recv_ref = f32[8,8,128]{2,1,0:T(8,128)S(1)} all-to-all(f32[8,8,128]{2,1,0:T(8,128)} %copy-done.23), channel_id=1, replica_groups=mesh['section'=2,'batch'=8,'chan'=32] {'batch'}, dimensions={0} | all-to-all | bytes 65536 | tf_op jit(solution)/shard_map/all_to_all | solution.py:49
  170.2 1.0 copy-done.9
  171.1 0.7 copy-done.19
  172.4 3.6 %all-to-all-start.6 = ((bf16[4,256,512]{2,1,0:T(8,128)(2,1)}), bf16[4,256,512]{2,1,0:T(8,128)(2,1)S(1)}, u32[]{:S(2)}, u32[]{:S(2)}) async-start(bf16[4,256,512]{2,1,0:T(8,128)(2,1)} %copy-done.9), calls=%async_computation.6 | async-start | bytes 2097152 | tf_op jit(solution)/shard_map/all_to_all | solution.py:35
  176.1 1.2 copy-done.2
  177.3 0.7 shard_map.166.weight_ref
  178.0 0.8 copy-done.5
  178.8 10.1 %all-to-all-done.6.recv_ref = bf16[4,256,512]{2,1,0:T(8,128)(2,1)S(1)} async-done(((bf16[4,256,512]{2,1,0:T(8,128)(2,1)}), bf16[4,256,512]{2,1,0:T(8,128)(2,1)S(1)}, u32[]{:S(2)}, u32[]{:S(2)}) %all-to-all-start.6) | async-done | bytes 1048608 | tf_op jit(solution)/shard_map/all_to_all | solution.py:35
  189.1 22.7 %all_to_all.66.recv_ref = bf16[8,32,512]{2,1,0:T(8,128)(2,1)S(1)} all-to-all(bf16[8,32,512]{2,1,0:T(8,128)(2,1)S(1)} %shard_map.165), channel_id=1, replica_groups={{0,4,8,12,16,20,24,28},{1,5,9,13,17,21,25,29},{2,6,10,14,18,22,26,30},{..., dimensions={0} | all-to-all | bytes 524288 | tf_op jit(solution)/shard_map/all_to_all | solution.py:40
  211.8 0.8 shard_map.167
  212.6 8.9 %all-to-all-start.8 = ((f32[8,32,128]{2,1,0:T(8,128)}), f32[8,32,128]{2,1,0:T(8,128)S(1)}, u32[]{:S(2)}, u32[]{:S(2)}) async-start(f32[8,32,128]{2,1,0:T(8,128)} %get-tuple-element.62), calls=%async_computation.9 | async-start | bytes 262144 | tf_op jit(solution)/shard_map/all_to_all | solution.py:49
  221.5 0.7 slice.35
  222.2 13.6 %all-to-all-done.8.recv_ref = f32[8,32,128]{2,1,0:T(8,128)S(1)} async-done(((f32[8,32,128]{2,1,0:T(8,128)}), f32[8,32,128]{2,1,0:T(8,128)S(1)}, u32[]{:S(2)}, u32[]{:S(2)}) %all-to-all-start.8) | async-done | bytes 131104 | tf_op jit(solution)/shard_map/all_to_all | solution.py:49
  235.8 1.6 shard_map.168
  237.4 1.0 copy-done.8
  238.4 0.8 copy-done.27
  239.2 3.6 %all-to-all-start.9 = ((bf16[4,256,512]{2,1,0:T(8,128)(2,1)}), bf16[4,256,512]{2,1,0:T(8,128)(2,1)S(1)}, u32[]{:S(2)}, u32[]{:S(2)}) async-start(bf16[4,256,512]{2,1,0:T(8,128)(2,1)} %copy-done.8), calls=%async_computation.10 | async-start | bytes 2097152 | tf_op jit(solution)/shard_map/all_to_all | solution.py:35
  242.9 8.9 %collective-permute-start.2 = (bf16[4,544,128]{2,1,0:T(8,128)(2,1)S(1)}, bf16[4,544,128]{2,1,0:T(8,128)(2,1)S(1)}, u32[]{:S(2)}, u32[]{:S(2)}) collective-permute-start(bf16[4,544,128]{2,1,0:T(8,128)(2,1)S(1)} %copy-done.28), channel_id=1, source_target_pairs={{0,256},{256,0},{1,257},{257,1},{2,258},{258,2},{3,259},{259,3},{4... | collective-permute-start | bytes 1671176 | tf_op jit(solution)/shard_map/ppermute | solution.py:68
  252.0 1.9 collective-permute-start.3
  253.9 1.1 collective-permute-done.3
  255.1 1.0 add_convert_fusion
  256.1 3.5 %all-to-all-start.10 = ((bf16[4,544,128]{2,1,0:T(8,128)(2,1)}), bf16[4,544,128]{2,1,0:T(8,128)(2,1)S(1)}, u32[]{:S(2)}, u32[]{:S(2)}) async-start(bf16[4,544,128]{2,1,0:T(8,128)(2,1)} %add_convert_fusion), calls=%async_computation.11 | async-start | bytes 1114112 | tf_op jit(solution)/shard_map/all_to_all | solution.py:45
  259.6 0.9 shard_map.169
  260.5 6.1 %all-to-all-done.10 = bf16[4,544,128]{2,1,0:T(8,128)(2,1)S(1)} async-done(((bf16[4,544,128]{2,1,0:T(8,128)(2,1)}), bf16[4,544,128]{2,1,0:T(8,128)(2,1)S(1)}, u32[]{:S(2)}, u32[]{:S(2)}) %all-to-all-start.10) | async-done | bytes 557088 | tf_op jit(solution)/shard_map/all_to_all | solution.py:45
  266.7 7.0 %all-to-all-start.11 = ((bf16[8,64,512]{2,1,0:T(8,128)(2,1)}), bf16[8,64,512]{2,1,0:T(8,128)(2,1)S(1)}, u32[]{:S(2)}, u32[]{:S(2)}) async-start(bf16[8,64,512]{2,1,0:T(8,128)(2,1)} %shard_map.169), calls=%async_computation.12 | async-start | bytes 1048576 | tf_op jit(solution)/shard_map/all_to_all | solution.py:40
  273.7 1.9 collective-permute-start.4
  275.6 14.2 %collective-permute-done.4 = bf16[544,128]{1,0:T(8,128)(2,1)S(1)} collective-permute-done((bf16[544,128]{1,0:T(8,128)(2,1)S(1)}, bf16[544,128]{1,0:T(8,128)(2,1)S(1)}, u32[]{:S(2)}, u32[]{:S(2)}) %collective-permute-start.4) | collective-permute-done | bytes 139296 | tf_op jit(solution)/shard_map/ppermute | solution.py:68
  289.9 12.7 %all-to-all-done.11.recv_ref = bf16[8,64,512]{2,1,0:T(8,128)(2,1)S(1)} async-done(((bf16[8,64,512]{2,1,0:T(8,128)(2,1)}), bf16[8,64,512]{2,1,0:T(8,128)(2,1)S(1)}, u32[]{:S(2)}, u32[]{:S(2)}) %all-to-all-start.11) | async-done | bytes 524320 | tf_op jit(solution)/shard_map/all_to_all | solution.py:40
  302.7 9.8 %all_to_all.67.line_ref = bf16[4,544,128]{2,1,0:T(8,128)(2,1)S(1)} all-to-all(bf16[4,544,128]{2,1,0:T(8,128)(2,1)S(1)} %broadcast_in_dim.48), channel_id=1, replica_groups={{0,32,64,96},{128,160,192,224},{1,33,65,97},{129,161,193,225},{2,34,66,..., dimensions={0} | all-to-all | bytes 1114112 | tf_op jit(solution)/shard_map/all_to_all | solution.py:45
  312.5 15.5 %collective-permute-start.5 = (bf16[4,544,128]{2,1,0:T(8,128)(2,1)S(1)}, bf16[4,544,128]{2,1,0:T(8,128)(2,1)S(1)}, u32[]{:S(2)}, u32[]{:S(2)}) collective-permute-start(bf16[4,544,128]{2,1,0:T(8,128)(2,1)S(1)} %all_to_all.67.line_ref), channel_id=1, source_target_pairs={{0,256},{256,0},{1,257},{257,1},{2,258},{258,2},{3,259},{259,3},{4... | collective-permute-start | bytes 1671176 | tf_op jit(solution)/shard_map/ppermute | solution.py:68
  329.1 1.0 shard_map.170
  330.3 0.7 copy_bitcast_fusion
  331.0 1.5 shard_map.171
  (90 shorter events, 6.0 us)
Async XLA Ops:
  7.2 14.9 %copy-start = (bf16[1,1,8,64,1024]{4,3,2,1,0:T(8,128)(2,1)S(1)}, bf16[1,1,8,64,1024]{4,3,2,1,0:T(8,128)(2,1)}, u32[]{:S(2)}) copy-start(bf16[1,1,8,64,1024]{4,3,2,1,0:T(8,128)(2,1)} %param.9) | copy-start | bytes 3145732
  7.2 21.0 %copy-start.30 = (bf16[1024,128]{1,0:T(8,128)(2,1)S(1)}, bf16[1024,128]{1,0:T(8,128)(2,1)}, u32[]{:S(2)}) copy-start(bf16[1024,128]{1,0:T(8,128)(2,1)} %param.13) | copy-start | bytes 786436
  7.2 21.1 %copy-start.31 = (bf16[128,1024]{1,0:T(8,128)(2,1)S(1)}, bf16[128,1024]{1,0:T(8,128)(2,1)}, u32[]{:S(2)}) copy-start(bf16[128,1024]{1,0:T(8,128)(2,1)} %param.16) | copy-start | bytes 786436
  9.0 25.3 %all-to-all-start = ((bf16[8,32,512]{2,1,0:T(8,128)(2,1)}), bf16[8,32,512]{2,1,0:T(8,128)(2,1)S(1)}, u32[]{:S(2)}, u32[]{:S(2)}) async-start(bf16[8,32,512]{2,1,0:T(8,128)(2,1)} %broadcast_in_dim.39), calls=%async_computation | async-start | bytes 524288 | tf_op jit(solution)/shard_map/all_to_all | solution.py:40
  22.1 8.3 %copy-start.3 = (bf16[3,3,1024,32]{2,3,1,0:T(8,128)(2,1)S(1)}, bf16[3,3,1024,32]{2,3,1,0:T(8,128)(2,1)}, u32[]{:S(2)}) copy-start(bf16[3,3,1024,32]{2,3,1,0:T(8,128)(2,1)} %param.10) | copy-start | bytes 1769476
  22.2 6.3 %collective-permute-start = (bf16[64,1024]{1,0:T(8,128)(2,1)S(1)}, bf16[64,1024]{1,0:T(8,128)(2,1)S(1)}, u32[]{:S(2)}, u32[]{:S(2)}) collective-permute-start(bf16[64,1024]{1,0:T(8,128)(2,1)S(1)} %get-tuple-element.79), channel_id=1, source_target_pairs={{32,0},{64,32},{96,64},{128,96},{160,128},{192,160},{224,192},{33,... | collective-permute-start | bytes 393224 | tf_op jit(solution)/shard_map/ppermute | solution.py:369
  23.6 5.9 %collective-permute-start.1 = (bf16[64,1024]{1,0:T(8,128)(2,1)S(1)}, bf16[64,1024]{1,0:T(8,128)(2,1)}, u32[]{:S(2)}, u32[]{:S(2)}) collective-permute-start(bf16[64,1024]{1,0:T(8,128)(2,1)S(1)} %get-tuple-element.80), channel_id=1, source_target_pairs={{0,32},{32,64},{64,96},{96,128},{128,160},{160,192},{192,224},{1,3... | collective-permute-start | bytes 393224 | tf_op jit(solution)/shard_map/ppermute | solution.py:368
  30.4 27.3 %copy-start.34 = (f32[32]{0:T(128)S(1)}, f32[32]{0:T(128)}, u32[]{:S(2)}) copy-start(f32[32]{0:T(128)} %param.11) | copy-start | bytes 388
  30.5 27.4 %copy-start.35 = (f32[32]{0:T(128)S(1)}, f32[32]{0:T(128)}, u32[]{:S(2)}) copy-start(f32[32]{0:T(128)} %param.12) | copy-start | bytes 388
  34.3 56.4 %copy-start.29 = (bf16[8,32,512]{2,1,0:T(8,128)(2,1)}, bf16[8,32,512]{2,1,0:T(8,128)(2,1)S(1)}, u32[]{:S(2)}) copy-start(bf16[8,32,512]{2,1,0:T(8,128)(2,1)S(1)} %all-to-all-done) | copy-start | bytes 786436
  34.3 37.6 %all-to-all-start.1 = ((f32[8,32,128]{2,1,0:T(8,128)}), f32[8,32,128]{2,1,0:T(8,128)S(1)}, u32[]{:S(2)}, u32[]{:S(2)}) async-start(f32[8,32,128]{2,1,0:T(8,128)} %get-tuple-element.47), calls=%async_computation.1 | async-start | bytes 262144 | tf_op jit(solution)/shard_map/all_to_all | solution.py:49
  72.8 30.9 %copy-start.24 = (f32[32,128]{1,0:T(8,128)}, f32[32,128]{1,0:T(8,128)S(1)}, u32[]{:S(2)}) copy-start(f32[32,128]{1,0:T(8,128)S(1)} %get-tuple-element.63.fact_ref) | copy-start | bytes 49156
  72.8 29.8 %all-to-all-start.2 = ((bf16[8,32,512]{2,1,0:T(8,128)(2,1)}), bf16[8,32,512]{2,1,0:T(8,128)(2,1)S(1)}, u32[]{:S(2)}, u32[]{:S(2)}) async-start(bf16[8,32,512]{2,1,0:T(8,128)(2,1)} %get-tuple-element.48.stream_ref), calls=%async_computation.2 | async-start | bytes 524288 | tf_op jit(solution)/shard_map/all_to_all | solution.py:40
  90.7 40.8 %all-gather.2.cloned.1.call-start = ((), (), s32[]{:S(2)}) async-start(), calls=%async_computation.14 | async-start | bytes 1310720 | tf_op jit(solution)/shard_map/all_gather | solution.py:363
  103.7 21.8 %all-to-all-start.3 = ((bf16[4,256,512]{2,1,0:T(8,128)(2,1)}), bf16[4,256,512]{2,1,0:T(8,128)(2,1)S(1)}, u32[]{:S(2)}, u32[]{:S(2)}) async-start(bf16[4,256,512]{2,1,0:T(8,128)(2,1)} %broadcast_in_dim.43), calls=%async_computation.3 | async-start | bytes 2097152 | tf_op jit(solution)/shard_map/all_to_all | solution.py:35
  107.7 22.4 %copy-start.32 = (f32[128]{0:T(128)S(1)}, f32[128]{0:T(128)}, u32[]{:S(2)}) copy-start(f32[128]{0:T(128)} %param.14) | copy-start | bytes 1540
  107.8 23.0 %copy-start.33 = (f32[128]{0:T(128)S(1)}, f32[128]{0:T(128)}, u32[]{:S(2)}) copy-start(f32[128]{0:T(128)} %param.15) | copy-start | bytes 1540
  126.5 17.1 %all-to-all-start.4 = ((f32[8,8,128]{2,1,0:T(8,128)}), f32[8,8,128]{2,1,0:T(8,128)S(1)}, u32[]{:S(2)}, u32[]{:S(2)}) async-start(f32[8,8,128]{2,1,0:T(8,128)} %get-tuple-element.50), calls=%async_computation.4 | async-start | bytes 65536 | tf_op jit(solution)/shard_map/all_to_all | solution.py:49
  129.8 59.2 %reduce-scatter.2.cloned.1.call-start = ((), (), s32[]{:S(2)}) async-start(), calls=%async_computation.15 | async-start | bytes 1310720 | tf_op jit(solution)/shard_map/reduce_scatter | solution.py:411
  143.6 0.6 copy-start.15
  144.2 1.2 copy-start.1
  145.4 0.8 copy-start.13
  146.3 0.8 copy-start.14
  147.1 0.8 copy-start.16
  148.7 1.0 copy-start.7
  149.7 0.7 copy-start.11
  150.4 0.6 copy-start.17
  151.0 0.6 copy-start.21
  151.6 0.6 copy-start.23
  152.3 17.2 %copy-start.12 = (f32[128,512]{1,0:T(8,128)S(1)}, f32[128,512]{1,0:T(8,128)}, u32[]{:S(2)}) copy-start(f32[128,512]{1,0:T(8,128)} %copy-done.11) | copy-start | bytes 786436
  152.3 17.2 %copy-start.22 = (f32[128,128]{1,0:T(8,128)S(1)}, f32[128,128]{1,0:T(8,128)}, u32[]{:S(2)}) copy-start(f32[128,128]{1,0:T(8,128)} %copy-done.21) | copy-start | bytes 196612
  170.1 1.0 copy-start.9
  171.1 0.7 copy-start.19
  171.8 0.6 copy-start.26
  172.4 3.7 %copy-start.18 = (bf16[128,512]{1,0:T(8,128)(2,1)S(1)}, bf16[128,512]{1,0:T(8,128)(2,1)}, u32[]{:S(2)}) copy-start(bf16[128,512]{1,0:T(8,128)(2,1)} %copy-done.17) | copy-start | bytes 393220
  172.4 3.7 %copy-start.20 = (bf16[128,512]{1,0:T(8,128)(2,1)S(1)}, bf16[128,512]{1,0:T(8,128)(2,1)}, u32[]{:S(2)}) copy-start(bf16[128,512]{1,0:T(8,128)(2,1)} %copy-done.19) | copy-start | bytes 393220
  172.4 16.5 %all-to-all-start.6 = ((bf16[4,256,512]{2,1,0:T(8,128)(2,1)}), bf16[4,256,512]{2,1,0:T(8,128)(2,1)S(1)}, u32[]{:S(2)}, u32[]{:S(2)}) async-start(bf16[4,256,512]{2,1,0:T(8,128)(2,1)} %copy-done.9), calls=%async_computation.6 | async-start | bytes 2097152 | tf_op jit(solution)/shard_map/all_to_all | solution.py:35
  176.0 1.2 copy-start.2
  178.0 0.8 copy-start.5
  178.8 57.0 %copy-start.4 = (bf16[3,3,1024,32]{2,3,1,0:T(8,128)(2,1)S(1)}, bf16[3,3,1024,32]{2,3,1,0:T(8,128)(2,1)}, u32[]{:S(2)}) copy-start(bf16[3,3,1024,32]{2,3,1,0:T(8,128)(2,1)} %param.10) | copy-start | bytes 1769476
  178.8 57.0 %copy-start.25 = (f32[32,128]{1,0:T(8,128)S(1)}, f32[32,128]{1,0:T(8,128)}, u32[]{:S(2)}) copy-start(f32[32,128]{1,0:T(8,128)} %copy-done.24) | copy-start | bytes 49156
  189.0 46.8 %copy-start.6 = (bf16[8,256,128]{2,1,0:T(8,128)(2,1)S(1)}, bf16[8,256,128]{2,1,0:T(8,128)(2,1)}, u32[]{:S(2)}) copy-start(bf16[8,256,128]{2,1,0:T(8,128)(2,1)} %copy-done.5) | copy-start | bytes 1572868
  212.6 23.1 %all-to-all-start.8 = ((f32[8,32,128]{2,1,0:T(8,128)}), f32[8,32,128]{2,1,0:T(8,128)S(1)}, u32[]{:S(2)}, u32[]{:S(2)}) async-start(f32[8,32,128]{2,1,0:T(8,128)} %get-tuple-element.62), calls=%async_computation.9 | async-start | bytes 262144 | tf_op jit(solution)/shard_map/all_to_all | solution.py:49
  237.4 1.0 copy-start.8
  238.4 0.8 copy-start.27
  239.2 3.7 %copy-start.28 = (bf16[4,544,128]{2,1,0:T(8,128)(2,1)S(1)}, bf16[4,544,128]{2,1,0:T(8,128)(2,1)}, u32[]{:S(2)}) copy-start(bf16[4,544,128]{2,1,0:T(8,128)(2,1)} %copy-done.27) | copy-start | bytes 1671172
  239.2 16.9 %all-to-all-start.9 = ((bf16[4,256,512]{2,1,0:T(8,128)(2,1)}), bf16[4,256,512]{2,1,0:T(8,128)(2,1)S(1)}, u32[]{:S(2)}, u32[]{:S(2)}) async-start(bf16[4,256,512]{2,1,0:T(8,128)(2,1)} %copy-done.8), calls=%async_computation.10 | async-start | bytes 2097152 | tf_op jit(solution)/shard_map/all_to_all | solution.py:35
  242.9 12.2 %collective-permute-start.2 = (bf16[4,544,128]{2,1,0:T(8,128)(2,1)S(1)}, bf16[4,544,128]{2,1,0:T(8,128)(2,1)S(1)}, u32[]{:S(2)}, u32[]{:S(2)}) collective-permute-start(bf16[4,544,128]{2,1,0:T(8,128)(2,1)S(1)} %copy-done.28), channel_id=1, source_target_pairs={{0,256},{256,0},{1,257},{257,1},{2,258},{258,2},{3,259},{259,3},{4... | collective-permute-start | bytes 1671176 | tf_op jit(solution)/shard_map/ppermute | solution.py:68
  252.0 3.0 collective-permute-start.3
  255.1 4.5 %copy-start.10 = (bf16[256,512]{1,0:T(8,128)(2,1)S(1)}, bf16[256,512]{1,0:T(8,128)(2,1)}, u32[]{:S(2)}) copy-start(bf16[256,512]{1,0:T(8,128)(2,1)} %reduce-scatter.2.cloned.1.call-done.refs_0_) | copy-start | bytes 786436
  256.1 10.6 %all-to-all-start.10 = ((bf16[4,544,128]{2,1,0:T(8,128)(2,1)}), bf16[4,544,128]{2,1,0:T(8,128)(2,1)S(1)}, u32[]{:S(2)}, u32[]{:S(2)}) async-start(bf16[4,544,128]{2,1,0:T(8,128)(2,1)} %add_convert_fusion), calls=%async_computation.11 | async-start | bytes 1114112 | tf_op jit(solution)/shard_map/all_to_all | solution.py:45
  266.7 35.9 %all-to-all-start.11 = ((bf16[8,64,512]{2,1,0:T(8,128)(2,1)}), bf16[8,64,512]{2,1,0:T(8,128)(2,1)S(1)}, u32[]{:S(2)}, u32[]{:S(2)}) async-start(bf16[8,64,512]{2,1,0:T(8,128)(2,1)} %shard_map.169), calls=%async_computation.12 | async-start | bytes 1048576 | tf_op jit(solution)/shard_map/all_to_all | solution.py:40
  273.7 16.1 %collective-permute-start.4 = (bf16[544,128]{1,0:T(8,128)(2,1)S(1)}, bf16[544,128]{1,0:T(8,128)(2,1)S(1)}, u32[]{:S(2)}, u32[]{:S(2)}) collective-permute-start(bf16[544,128]{1,0:T(8,128)(2,1)S(1)} %reduce_sum.12), channel_id=1, source_target_pairs={{0,128},{32,160},{64,192},{96,224},{128,0},{160,32},{192,64},{224,... | collective-permute-start | bytes 417800 | tf_op jit(solution)/shard_map/ppermute | solution.py:68
  312.5 18.5 %collective-permute-start.5 = (bf16[4,544,128]{2,1,0:T(8,128)(2,1)S(1)}, bf16[4,544,128]{2,1,0:T(8,128)(2,1)S(1)}, u32[]{:S(2)}, u32[]{:S(2)}) collective-permute-start(bf16[4,544,128]{2,1,0:T(8,128)(2,1)S(1)} %all_to_all.67.line_ref), channel_id=1, source_target_pairs={{0,256},{256,0},{1,257},{257,1},{2,258},{258,2},{3,259},{259,3},{4... | collective-permute-start | bytes 1671176 | tf_op jit(solution)/shard_map/ppermute | solution.py:68
Sparse Core Ops, SparseCore 0:
  94.2 34.7 all-gather.1
  152.4 33.2 reduce-scatter.1

commit v3 on v2

--- a/solution.py
+++ b/solution.py
@@ -13,7 +13,8 @@
 NX = 4
 NY = 4
 LANES = 128
-VMEM_LIMIT = 8 << 20
+VMEM_LIMIT = 12 << 20
+FAR_LIMIT = 56 << 20
 NT = (((1,), (1,)), ((), ()))
 TN = (((0,), (0,)), ((), ()))
 
@@ -74,15 +75,57 @@
     return lax.dot_general(a, b, dims, preferred_element_type=F32)
 
 
-def call(kernel, outs, arrays, scratch=()):
+def call(kernel, outs, arrays, scratch=(), far_in=(), far_out=()):
+    n_in, n_out, n_scratch = len(arrays), len(outs), len(scratch)
     vmem = pl.BlockSpec(memory_space=pltpu.VMEM)
+    far = pl.BlockSpec(memory_space=pl.ANY)
+    held = [pltpu.VMEM(arrays[k].shape, arrays[k].dtype) for k in far_in]
+    held += [pltpu.VMEM(*outs[k]) for k in far_out]
+    scratch = list(scratch) + held
+    n_far = len(held)
+    if n_far:
+        scratch.append(pltpu.SemaphoreType.DMA((n_far,)))
+
+    def run(*refs):
+        near = list(refs[: n_in + n_out])
+        if not n_far:
+            kernel(*refs)
+            return
+        buffers, sems = refs[n_in + n_out + n_scratch : -1], refs[-1]
+        moves = []
+        for i, k in enumerate(far_in):
+            moves.append(pltpu.make_async_copy(refs[k], buffers[i], sems.at[i]))
+            near[k] = buffers[i]
+        flights = {}
+        for i, k in enumerate(far_out, len(far_in)):
+            flights[k] = pltpu.make_async_copy(buffers[i], refs[n_in + k], sems.at[i])
+            near[n_in + k] = buffers[i]
+        for move in moves:
+            move.start()
+        for move in moves:
+            move.wait()
+        started = []
+
+        def flush(k):
+            flights[k].start()
+            started.append(k)
+
+        kernel(*near, *refs[n_in + n_out : n_in + n_out + n_scratch], flush=flush)
+        for k in far_out:
+            if k not in started:
+                flush(k)
+        for k in far_out:
+            flights[k].wait()
+
     return pl.pallas_call(
-        kernel,
+        run,
         out_shape=tuple(jax.ShapeDtypeStruct(shape, dtype) for shape, dtype in outs),
-        in_specs=[vmem] * len(arrays),
-        out_specs=(vmem,) * len(outs),
-        scratch_shapes=list(scratch),
-        compiler_params=pltpu.CompilerParams(vmem_limit_bytes=VMEM_LIMIT),
+        in_specs=[far if k in far_in else vmem for k in range(n_in)],
+        out_specs=tuple(far if k in far_out else vmem for k in range(n_out)),
+        scratch_shapes=scratch,
+        compiler_params=pltpu.CompilerParams(
+            vmem_limit_bytes=FAR_LIMIT if n_far else VMEM_LIMIT
+        ),
     )(*arrays)
 
 
@@ -194,7 +237,7 @@
 
 def active_kernel(
     pixels, hidden_ref, cotan_ref, recv_ref, gain_ref, bias_ref, cols_ref, rows_ref,
-    act_ref, norm_ref, masked_ref, pay_ref, fact_ref, term_ref,
+    act_ref, norm_ref, masked_ref, pay_ref, fact_ref, term_ref, flush,
 ):
     _, first, second = read_rows(recv_ref)
     mean = first / pixels
@@ -203,10 +246,14 @@
     pre = gain_ref[...] * norm + bias_ref[...]
     act = jnp.maximum(pre, 0.0).astype(BF16)
     act_ref[...] = act
+    flush(0)
     masked = jnp.where(pre > 0, dot(cols_ref[...], cotan_ref[...]), 0.0)
     norm_ref[...] = norm
+    flush(1)
     masked_ref[...] = masked
+    flush(2)
     fact_ref[...] = jnp.broadcast_to(gain_ref[...] * scale, fact_ref.shape)
+    flush(4)
     write_rows(
         pay_ref,
         jnp.sum(masked, 1, keepdims=True),
@@ -407,6 +454,8 @@
             ((channels, local), BF16),
         ],
         (hidden, cotan_full, along_batch(pay), gain_b, bias_b, down_cols, down_rows),
+        far_in=(0, 1, 5, 6),
+        far_out=(0, 1, 2, 4, 5),
     )
     down_part = lax.psum_scatter(
         down_term, "chan", axis_index_groups=x_groups(n_chan), tiled=True

time: 341 us -> 340 us (level)
  local copies, waits for them, and re-layouts: 21.8 us -> 16.4 us
  Pallas kernels: 11.9 us -> 16.5 us
    unnamed x73 -> x59, local copies, waits for them, and re-layouts: 14.1 us -> 7.32 us
    pallas_call x12, Pallas kernels: 11.9 us -> 16.5 us  [call(): pl.pallas_call(run, out_shape=tuple((jax.ShapeDtypeStruct(shape, dtype) f...]
  transfers between devices with their start and end apart: 18 -> 18, of which waited for: 12 -> 12; matrix products, arithmetic and copies ran while one was open for 2% -> 3% of each run, Pallas kernels for 2% -> 2%
where the time goes in v3:
time: 340 us; the launch traced here: 338 us
  starting transfers between devices  124 us (36%)
  waiting for transfers between devices  116 us (34%)
  blocking collectives  49.1 us (14%)
  Pallas kernels  16.5 us (5%)
  local copies, waits for them, and re-layouts  16.4 us (5%)
  between operations  14.4 us (4%)
    all_to_all x3, waiting for transfers between devices, along_batch(): return lax.all_to_all(parts, 'batch', 0, 0)  38.9 us
    all_to_all x3, starting transfers between devices, along_z(): return lax.all_to_all(parts, 'chan', 0, 0, axis_index_groups=z_groups(n))  37.9 us
    all_to_all x3, starting transfers between devices, along_batch(): return lax.all_to_all(parts, 'batch', 0, 0)  36.8 us
    all_to_all x3, waiting for transfers between devices, along_x(): return lax.all_to_all(parts, 'chan', 0, 0, axis_index_groups=x_groups(n))  28.5 us
    ppermute x4, starting transfers between devices, partner(): return lax.ppermute(value, axis, [(i, i ^ step) for i in range(n)])  28.2 us
    all_to_all x3, waiting for transfers between devices, along_z(): return lax.all_to_all(parts, 'chan', 0, 0, axis_index_groups=z_groups(n))  25.1 us
    all_to_all x1, blocking collectives, along_z(): return lax.all_to_all(parts, 'chan', 0, 0, axis_index_groups=z_groups(n))  22.1 us
    all_to_all x1, blocking collectives, along_batch(): return lax.all_to_all(parts, 'batch', 0, 0)  17.2 us
  transfers between devices with their start and end apart: 18, of which 12 were waited for; matrix products, arithmetic and copies ran while one was open for 3% of the time, Pallas kernels for 2%

profile of v3, /device:TPU:1, one launch (start us, length us, event | category | flops | bytes accessed | tf_op | source)
XLA Modules:
  0.0 338.3 jit_solution(2329634867434485895)
XLA Ops:
  7.2 1.0 copy.32
  8.3 0.7 broadcast_in_dim.39
  9.0 13.1 %all-to-all-start = ((bf16[8,32,512]{2,1,0:T(8,128)(2,1)}), bf16[8,32,512]{2,1,0:T(8,128)(2,1)S(1)}, u32[]{:S(2)}, u32[]{:S(2)}) async-start(bf16[8,32,512]{2,1,0:T(8,128)(2,1)} %broadcast_in_dim.39), calls=%async_computation | async-start | bytes 524288 | tf_op jit(solution)/shard_map/all_to_all | solution.py:41
  22.1 0.7 slice_bitcast_fusion.1
  22.8 1.4 collective-permute-start
  24.3 4.6 %collective-permute-start.1 = (bf16[64,1024]{1,0:T(8,128)(2,1)}, bf16[64,1024]{1,0:T(8,128)(2,1)}, u32[]{:S(2)}, u32[]{:S(2)}) collective-permute-start(bf16[64,1024]{1,0:T(8,128)(2,1)} %get-tuple-element.80), channel_id=1, source_target_pairs={{0,32},{32,64},{64,96},{96,128},{128,160},{160,192},{192,224},{1,3... | collective-permute-start | bytes 393224 | tf_op jit(solution)/shard_map/ppermute | solution.py:415
  29.2 1.3 collective-permute-done.1
  30.5 0.9 pad_maximum_fusion.refs_1_
  31.5 1.7 shard_map.160
  33.2 1.1 all-to-all-done
  34.3 24.3 %all-to-all-start.1 = ((f32[8,32,128]{2,1,0:T(8,128)}), f32[8,32,128]{2,1,0:T(8,128)S(1)}, u32[]{:S(2)}, u32[]{:S(2)}) async-start(f32[8,32,128]{2,1,0:T(8,128)} %get-tuple-element.47), calls=%async_computation.1 | async-start | bytes 262144 | tf_op jit(solution)/shard_map/all_to_all | solution.py:50
  58.8 14.0 %all-to-all-done.1.refs_2_ = f32[8,32,128]{2,1,0:T(8,128)S(1)} async-done(((f32[8,32,128]{2,1,0:T(8,128)}), f32[8,32,128]{2,1,0:T(8,128)S(1)}, u32[]{:S(2)}, u32[]{:S(2)}) %all-to-all-start.1) | async-done | bytes 131104 | tf_op jit(solution)/shard_map/all_to_all | solution.py:50
  72.8 0.9 shard_map.161
  73.7 17.9 %all-to-all-start.2 = ((bf16[8,32,512]{2,1,0:T(8,128)(2,1)}), bf16[8,32,512]{2,1,0:T(8,128)(2,1)S(1)}, u32[]{:S(2)}, u32[]{:S(2)}) async-start(bf16[8,32,512]{2,1,0:T(8,128)(2,1)} %get-tuple-element.48.refs_2_), calls=%async_computation.2 | async-start | bytes 524288 | tf_op jit(solution)/shard_map/all_to_all | solution.py:41
  91.6 0.7 all-gather.2.cloned.1.call-update
  92.3 11.2 %all-to-all-done.2 = bf16[8,32,512]{2,1,0:T(8,128)(2,1)S(1)} async-done(((bf16[8,32,512]{2,1,0:T(8,128)(2,1)}), bf16[8,32,512]{2,1,0:T(8,128)(2,1)S(1)}, u32[]{:S(2)}, u32[]{:S(2)}) %all-to-all-start.2) | async-done | bytes 262176 | tf_op jit(solution)/shard_map/all_to_all | solution.py:41
  103.5 1.1 broadcast_in_dim.43
  104.5 4.0 %all-to-all-start.3 = ((bf16[4,256,512]{2,1,0:T(8,128)(2,1)}), bf16[4,256,512]{2,1,0:T(8,128)(2,1)S(1)}, u32[]{:S(2)}, u32[]{:S(2)}) async-start(bf16[4,256,512]{2,1,0:T(8,128)(2,1)} %broadcast_in_dim.43), calls=%async_computation.3 | async-start | bytes 2097152 | tf_op jit(solution)/shard_map/all_to_all | solution.py:36
  108.7 19.2 %all-to-all-done.3.refs_0_ = bf16[4,256,512]{2,1,0:T(8,128)(2,1)S(1)} async-done(((bf16[4,256,512]{2,1,0:T(8,128)(2,1)}), bf16[4,256,512]{2,1,0:T(8,128)(2,1)S(1)}, u32[]{:S(2)}, u32[]{:S(2)}) %all-to-all-start.3) | async-done | bytes 1048608 | tf_op jit(solution)/shard_map/all_to_all | solution.py:36
  127.9 1.0 shard_map.162
  128.9 0.7 copy-done.8
  129.6 3.3 all-to-all-start.4
  133.0 0.8 copy.41.refs_5_
  133.9 0.7 copy.39.refs_3_
  134.6 0.7 copy.40.refs_4_
  135.4 11.4 %all-to-all-done.4.refs_2_ = f32[8,8,128]{2,1,0:T(8,128)S(1)} async-done(((f32[8,8,128]{2,1,0:T(8,128)}), f32[8,8,128]{2,1,0:T(8,128)S(1)}, u32[]{:S(2)}, u32[]{:S(2)}) %all-to-all-start.4) | async-done | bytes 32800 | tf_op jit(solution)/shard_map/all_to_all | solution.py:50
  146.7 0.6 copy-done.24
  147.3 4.8 %shard_map.163 = (bf16[128,512]{1,0:T(8,128)(2,1)}, f32[128,512]{1,0:T(8,128)}, f32[128,512]{1,0:T(8,128)}, f32[8,8,128]{2,1,0:T(8,128)}, f32[128,128]{1,0:T(8,128)}, /*index=5*/bf16[1024,512]{1,0:T(8,128)(2,1)}) custom-call(f32[128,512]{1,0:T(8,128)} %copy-done.8, bf16[1024,512]{1,0:T(8,128)(2,1)} %all-gather.2.cloned.1.call-done.refs_1_, ...), custom_call_target="tpu_custom_call" | custom-call | tf_op jit(solution)/shard_map/pallas_call | solution.py:120
  152.2 17.2 %all_to_all.65.refs_2_ = f32[8,8,128]{2,1,0:T(8,128)S(1)} all-to-all(f32[8,8,128]{2,1,0:T(8,128)} %get-tuple-element.53), channel_id=1, replica_groups=mesh['section'=2,'batch'=8,'chan'=32] {'batch'}, dimensions={0} | all-to-all | bytes 65536 | tf_op jit(solution)/shard_map/all_to_all | solution.py:50
  169.4 0.6 shard_map.164
  170.1 1.0 copy-done.6
  171.0 0.7 copy-done.12
  171.7 0.6 copy-done.17
  172.3 3.5 %all-to-all-start.6 = ((bf16[4,256,512]{2,1,0:T(8,128)(2,1)}), bf16[4,256,512]{2,1,0:T(8,128)(2,1)S(1)}, u32[]{:S(2)}, u32[]{:S(2)}) async-start(bf16[4,256,512]{2,1,0:T(8,128)(2,1)} %copy-done.6), calls=%async_computation.6 | async-start | bytes 2097152 | tf_op jit(solution)/shard_map/all_to_all | solution.py:36
  175.8 1.2 copy-done.1
  177.1 0.7 shard_map.166.refs_6_
  177.8 0.8 copy-done.4
  178.6 9.4 %all-to-all-done.6.refs_0_ = bf16[4,256,512]{2,1,0:T(8,128)(2,1)S(1)} async-done(((bf16[4,256,512]{2,1,0:T(8,128)(2,1)}), bf16[4,256,512]{2,1,0:T(8,128)(2,1)S(1)}, u32[]{:S(2)}, u32[]{:S(2)}) %all-to-all-start.6) | async-done | bytes 1048608 | tf_op jit(solution)/shard_map/all_to_all | solution.py:36
  188.1 22.1 %all_to_all.66.refs_0_ = bf16[8,32,512]{2,1,0:T(8,128)(2,1)S(1)} all-to-all(bf16[8,32,512]{2,1,0:T(8,128)(2,1)S(1)} %shard_map.165), channel_id=1, replica_groups={{0,4,8,12,16,20,24,28},{1,5,9,13,17,21,25,29},{2,6,10,14,18,22,26,30},{..., dimensions={0} | all-to-all | bytes 524288 | tf_op jit(solution)/shard_map/all_to_all | solution.py:41
  210.2 0.8 shard_map.167
  211.0 9.1 %all-to-all-start.8 = ((f32[8,32,128]{2,1,0:T(8,128)}), f32[8,32,128]{2,1,0:T(8,128)S(1)}, u32[]{:S(2)}, u32[]{:S(2)}) async-start(f32[8,32,128]{2,1,0:T(8,128)} %get-tuple-element.62), calls=%async_computation.9 | async-start | bytes 262144 | tf_op jit(solution)/shard_map/all_to_all | solution.py:50
  220.2 0.7 slice.35
  220.9 13.6 %all-to-all-done.8.refs_1_ = f32[8,32,128]{2,1,0:T(8,128)S(1)} async-done(((f32[8,32,128]{2,1,0:T(8,128)}), f32[8,32,128]{2,1,0:T(8,128)S(1)}, u32[]{:S(2)}, u32[]{:S(2)}) %all-to-all-start.8) | async-done | bytes 131104 | tf_op jit(solution)/shard_map/all_to_all | solution.py:50
  234.4 0.7 copy-done.16
  235.2 2.3 shard_map.168
  237.4 0.8 copy-done.18
  238.2 3.6 %all-to-all-start.9 = ((bf16[4,256,512]{2,1,0:T(8,128)(2,1)}), bf16[4,256,512]{2,1,0:T(8,128)(2,1)S(1)}, u32[]{:S(2)}, u32[]{:S(2)}) async-start(bf16[4,256,512]{2,1,0:T(8,128)(2,1)} %get-tuple-element.64), calls=%async_computation.10 | async-start | bytes 2097152 | tf_op jit(solution)/shard_map/all_to_all | solution.py:36
  241.9 8.9 %collective-permute-start.2 = (bf16[4,544,128]{2,1,0:T(8,128)(2,1)S(1)}, bf16[4,544,128]{2,1,0:T(8,128)(2,1)S(1)}, u32[]{:S(2)}, u32[]{:S(2)}) collective-permute-start(bf16[4,544,128]{2,1,0:T(8,128)(2,1)S(1)} %copy-done.19), channel_id=1, source_target_pairs={{0,256},{256,0},{1,257},{257,1},{2,258},{258,2},{3,259},{259,3},{4... | collective-permute-start | bytes 1671176 | tf_op jit(solution)/shard_map/ppermute | solution.py:69
  251.0 1.9 collective-permute-start.3
  253.0 1.1 collective-permute-done.3
  254.2 1.0 add_convert_fusion
  255.1 3.5 %all-to-all-start.10 = ((bf16[4,544,128]{2,1,0:T(8,128)(2,1)}), bf16[4,544,128]{2,1,0:T(8,128)(2,1)S(1)}, u32[]{:S(2)}, u32[]{:S(2)}) async-start(bf16[4,544,128]{2,1,0:T(8,128)(2,1)} %add_convert_fusion), calls=%async_computation.11 | async-start | bytes 1114112 | tf_op jit(solution)/shard_map/all_to_all | solution.py:46
  258.6 0.9 shard_map.169
  259.5 6.1 %all-to-all-done.10 = bf16[4,544,128]{2,1,0:T(8,128)(2,1)S(1)} async-done(((bf16[4,544,128]{2,1,0:T(8,128)(2,1)}), bf16[4,544,128]{2,1,0:T(8,128)(2,1)S(1)}, u32[]{:S(2)}, u32[]{:S(2)}) %all-to-all-start.10) | async-done | bytes 557088 | tf_op jit(solution)/shard_map/all_to_all | solution.py:46
  265.8 6.9 %all-to-all-start.11 = ((bf16[8,64,512]{2,1,0:T(8,128)(2,1)}), bf16[8,64,512]{2,1,0:T(8,128)(2,1)S(1)}, u32[]{:S(2)}, u32[]{:S(2)}) async-start(bf16[8,64,512]{2,1,0:T(8,128)(2,1)} %shard_map.169), calls=%async_computation.12 | async-start | bytes 1048576 | tf_op jit(solution)/shard_map/all_to_all | solution.py:41
  272.7 1.9 collective-permute-start.4
  274.6 14.2 %collective-permute-done.4 = bf16[544,128]{1,0:T(8,128)(2,1)S(1)} collective-permute-done((bf16[544,128]{1,0:T(8,128)(2,1)S(1)}, bf16[544,128]{1,0:T(8,128)(2,1)S(1)}, u32[]{:S(2)}, u32[]{:S(2)}) %collective-permute-start.4) | collective-permute-done | bytes 139296 | tf_op jit(solution)/shard_map/ppermute | solution.py:69
  288.8 12.8 %all-to-all-done.11.refs_0_ = bf16[8,64,512]{2,1,0:T(8,128)(2,1)S(1)} async-done(((bf16[8,64,512]{2,1,0:T(8,128)(2,1)}), bf16[8,64,512]{2,1,0:T(8,128)(2,1)S(1)}, u32[]{:S(2)}, u32[]{:S(2)}) %all-to-all-start.11) | async-done | bytes 524320 | tf_op jit(solution)/shard_map/all_to_all | solution.py:41
  301.7 9.8 %all_to_all.67.refs_0_ = bf16[4,544,128]{2,1,0:T(8,128)(2,1)S(1)} all-to-all(bf16[4,544,128]{2,1,0:T(8,128)(2,1)S(1)} %broadcast_in_dim.48), channel_id=1, replica_groups={{0,32,64,96},{128,160,192,224},{1,33,65,97},{129,161,193,225},{2,34,66,..., dimensions={0} | all-to-all | bytes 1114112 | tf_op jit(solution)/shard_map/all_to_all | solution.py:46
  311.5 15.4 %collective-permute-start.5 = (bf16[4,544,128]{2,1,0:T(8,128)(2,1)S(1)}, bf16[4,544,128]{2,1,0:T(8,128)(2,1)S(1)}, u32[]{:S(2)}, u32[]{:S(2)}) collective-permute-start(bf16[4,544,128]{2,1,0:T(8,128)(2,1)S(1)} %all_to_all.67.refs_0_), channel_id=1, source_target_pairs={{0,256},{256,0},{1,257},{257,1},{2,258},{258,2},{3,259},{259,3},{4... | collective-permute-start | bytes 1671176 | tf_op jit(solution)/shard_map/ppermute | solution.py:69
  327.4 0.6 slice_bitcast_fusion.3
  328.0 1.0 shard_map.170
  329.3 0.7 copy_bitcast_fusion
  329.9 1.5 shard_map.171
  (76 shorter events, 2.2 us)
Async XLA Ops:
  7.2 14.9 %copy-start = (bf16[1,1,8,64,1024]{4,3,2,1,0:T(8,128)(2,1)S(1)}, bf16[1,1,8,64,1024]{4,3,2,1,0:T(8,128)(2,1)}, u32[]{:S(2)}) copy-start(bf16[1,1,8,64,1024]{4,3,2,1,0:T(8,128)(2,1)} %param.9) | copy-start | bytes 3145732
  7.2 21.7 %copy-start.22 = (bf16[1024,128]{1,0:T(8,128)(2,1)S(1)}, bf16[1024,128]{1,0:T(8,128)(2,1)}, u32[]{:S(2)}) copy-start(bf16[1024,128]{1,0:T(8,128)(2,1)} %param.13) | copy-start | bytes 786436
  7.2 21.7 %copy-start.23 = (bf16[128,1024]{1,0:T(8,128)(2,1)S(1)}, bf16[128,1024]{1,0:T(8,128)(2,1)}, u32[]{:S(2)}) copy-start(bf16[128,1024]{1,0:T(8,128)(2,1)} %param.16) | copy-start | bytes 786436
  9.0 25.3 %all-to-all-start = ((bf16[8,32,512]{2,1,0:T(8,128)(2,1)}), bf16[8,32,512]{2,1,0:T(8,128)(2,1)S(1)}, u32[]{:S(2)}, u32[]{:S(2)}) async-start(bf16[8,32,512]{2,1,0:T(8,128)(2,1)} %broadcast_in_dim.39), calls=%async_computation | async-start | bytes 524288 | tf_op jit(solution)/shard_map/all_to_all | solution.py:41
  22.8 8.6 %copy-start.2 = (bf16[3,3,1024,32]{2,3,1,0:T(8,128)(2,1)S(1)}, bf16[3,3,1024,32]{2,3,1,0:T(8,128)(2,1)}, u32[]{:S(2)}) copy-start(bf16[3,3,1024,32]{2,3,1,0:T(8,128)(2,1)} %param.10) | copy-start | bytes 1769476
  22.8 6.3 %collective-permute-start = (bf16[64,1024]{1,0:T(8,128)(2,1)}, bf16[64,1024]{1,0:T(8,128)(2,1)S(1)}, u32[]{:S(2)}, u32[]{:S(2)}) collective-permute-start(bf16[64,1024]{1,0:T(8,128)(2,1)} %get-tuple-element.79), channel_id=1, source_target_pairs={{32,0},{64,32},{96,64},{128,96},{160,128},{192,160},{224,192},{33,... | collective-permute-start | bytes 393224 | tf_op jit(solution)/shard_map/ppermute | solution.py:416
  24.3 6.2 %collective-permute-start.1 = (bf16[64,1024]{1,0:T(8,128)(2,1)}, bf16[64,1024]{1,0:T(8,128)(2,1)}, u32[]{:S(2)}, u32[]{:S(2)}) collective-permute-start(bf16[64,1024]{1,0:T(8,128)(2,1)} %get-tuple-element.80), channel_id=1, source_target_pairs={{0,32},{32,64},{64,96},{96,128},{128,160},{160,192},{192,224},{1,3... | collective-permute-start | bytes 393224 | tf_op jit(solution)/shard_map/ppermute | solution.py:415
  29.1 103.9 %copy-start.20 = (bf16[4,8,32,128]{3,2,1,0:T(8,128)(2,1)}, bf16[4,8,32,128]{3,2,1,0:T(8,128)(2,1)S(1)}, u32[]{:S(2)}) copy-start(bf16[4,8,32,128]{3,2,1,0:T(8,128)(2,1)S(1)} %copy.35) | copy-start | bytes 786436
  31.4 27.2 %copy-start.27 = (f32[32]{0:T(128)S(1)}, f32[32]{0:T(128)}, u32[]{:S(2)}) copy-start(f32[32]{0:T(128)} %param.11) | copy-start | bytes 388
  31.4 27.3 %copy-start.28 = (f32[32]{0:T(128)S(1)}, f32[32]{0:T(128)}, u32[]{:S(2)}) copy-start(f32[32]{0:T(128)} %param.12) | copy-start | bytes 388
  34.3 57.3 %copy-start.21 = (bf16[8,32,512]{2,1,0:T(8,128)(2,1)}, bf16[8,32,512]{2,1,0:T(8,128)(2,1)S(1)}, u32[]{:S(2)}) copy-start(bf16[8,32,512]{2,1,0:T(8,128)(2,1)S(1)} %all-to-all-done) | copy-start | bytes 786436
  34.3 38.4 %all-to-all-start.1 = ((f32[8,32,128]{2,1,0:T(8,128)}), f32[8,32,128]{2,1,0:T(8,128)S(1)}, u32[]{:S(2)}, u32[]{:S(2)}) async-start(f32[8,32,128]{2,1,0:T(8,128)} %get-tuple-element.47), calls=%async_computation.1 | async-start | bytes 262144 | tf_op jit(solution)/shard_map/all_to_all | solution.py:50
  73.7 30.9 %copy-start.15 = (f32[32,128]{1,0:T(8,128)}, f32[32,128]{1,0:T(8,128)S(1)}, u32[]{:S(2)}) copy-start(f32[32,128]{1,0:T(8,128)S(1)} %get-tuple-element.63.refs_3_) | copy-start | bytes 49156
  73.7 29.8 %all-to-all-start.2 = ((bf16[8,32,512]{2,1,0:T(8,128)(2,1)}), bf16[8,32,512]{2,1,0:T(8,128)(2,1)S(1)}, u32[]{:S(2)}, u32[]{:S(2)}) async-start(bf16[8,32,512]{2,1,0:T(8,128)(2,1)} %get-tuple-element.48.refs_2_), calls=%async_computation.2 | async-start | bytes 524288 | tf_op jit(solution)/shard_map/all_to_all | solution.py:41
  91.6 43.8 %all-gather.2.cloned.1.call-start = ((), (), s32[]{:S(2)}) async-start(), calls=%async_computation.14 | async-start | bytes 1310720 | tf_op jit(solution)/shard_map/all_gather | solution.py:410
  104.5 23.4 %all-to-all-start.3 = ((bf16[4,256,512]{2,1,0:T(8,128)(2,1)}), bf16[4,256,512]{2,1,0:T(8,128)(2,1)S(1)}, u32[]{:S(2)}, u32[]{:S(2)}) async-start(bf16[4,256,512]{2,1,0:T(8,128)(2,1)} %broadcast_in_dim.43), calls=%async_computation.3 | async-start | bytes 2097152 | tf_op jit(solution)/shard_map/all_to_all | solution.py:36
  108.6 25.3 %copy-start.25 = (f32[128]{0:T(128)S(1)}, f32[128]{0:T(128)}, u32[]{:S(2)}) copy-start(f32[128]{0:T(128)} %param.14) | copy-start | bytes 1540
  108.7 25.9 %copy-start.26 = (f32[128]{0:T(128)S(1)}, f32[128]{0:T(128)}, u32[]{:S(2)}) copy-start(f32[128]{0:T(128)} %param.15) | copy-start | bytes 1540
  128.9 0.7 copy-start.8
  129.6 17.1 %all-to-all-start.4 = ((f32[8,8,128]{2,1,0:T(8,128)}), f32[8,8,128]{2,1,0:T(8,128)S(1)}, u32[]{:S(2)}, u32[]{:S(2)}) async-start(f32[8,8,128]{2,1,0:T(8,128)} %get-tuple-element.50), calls=%async_computation.4 | async-start | bytes 65536 | tf_op jit(solution)/shard_map/all_to_all | solution.py:50
  133.0 55.1 %reduce-scatter.2.cloned.1.call-start = ((), (), s32[]{:S(2)}) async-start(), calls=%async_computation.15 | async-start | bytes 1310720 | tf_op jit(solution)/shard_map/reduce_scatter | solution.py:460
  146.7 0.6 copy-start.24
  152.1 17.3 %copy-start.9 = (f32[128,512]{1,0:T(8,128)S(1)}, f32[128,512]{1,0:T(8,128)}, u32[]{:S(2)}) copy-start(f32[128,512]{1,0:T(8,128)} %get-tuple-element.52.refs_1_) | copy-start | bytes 786436
  152.1 17.3 %copy-start.10 = (f32[128,512]{1,0:T(8,128)S(1)}, f32[128,512]{1,0:T(8,128)}, u32[]{:S(2)}) copy-start(f32[128,512]{1,0:T(8,128)} %get-tuple-element.51.refs_0_) | copy-start | bytes 786436
  152.1 17.3 %copy-start.14 = (f32[128,128]{1,0:T(8,128)S(1)}, f32[128,128]{1,0:T(8,128)}, u32[]{:S(2)}) copy-start(f32[128,128]{1,0:T(8,128)} %get-tuple-element.54.refs_3_) | copy-start | bytes 196612
  170.0 1.0 copy-start.6
  171.0 0.7 copy-start.12
  171.7 0.6 copy-start.17
  171.7 4.1 %copy-start.11 = (bf16[128,512]{1,0:T(8,128)(2,1)S(1)}, bf16[128,512]{1,0:T(8,128)(2,1)}, u32[]{:S(2)}) copy-start(bf16[128,512]{1,0:T(8,128)(2,1)} %get-tuple-element.57.refs_3_) | copy-start | bytes 393220
  171.7 4.1 %copy-start.13 = (bf16[128,512]{1,0:T(8,128)(2,1)S(1)}, bf16[128,512]{1,0:T(8,128)(2,1)}, u32[]{:S(2)}) copy-start(bf16[128,512]{1,0:T(8,128)(2,1)} %copy-done.12) | copy-start | bytes 393220
  172.3 15.7 %all-to-all-start.6 = ((bf16[4,256,512]{2,1,0:T(8,128)(2,1)}), bf16[4,256,512]{2,1,0:T(8,128)(2,1)S(1)}, u32[]{:S(2)}, u32[]{:S(2)}) async-start(bf16[4,256,512]{2,1,0:T(8,128)(2,1)} %copy-done.6), calls=%async_computation.6 | async-start | bytes 2097152 | tf_op jit(solution)/shard_map/all_to_all | solution.py:36
  175.8 1.2 copy-start.1
  177.8 0.8 copy-start.4
  178.6 55.9 %copy-start.3 = (bf16[3,3,1024,32]{2,3,1,0:T(8,128)(2,1)S(1)}, bf16[3,3,1024,32]{2,3,1,0:T(8,128)(2,1)}, u32[]{:S(2)}) copy-start(bf16[3,3,1024,32]{2,3,1,0:T(8,128)(2,1)} %param.10) | copy-start | bytes 1769476
  188.1 46.4 %copy-start.5 = (bf16[8,256,128]{2,1,0:T(8,128)(2,1)S(1)}, bf16[8,256,128]{2,1,0:T(8,128)(2,1)}, u32[]{:S(2)}) copy-start(bf16[8,256,128]{2,1,0:T(8,128)(2,1)} %copy-done.4) | copy-start | bytes 1572868
  211.0 23.4 %all-to-all-start.8 = ((f32[8,32,128]{2,1,0:T(8,128)}), f32[8,32,128]{2,1,0:T(8,128)S(1)}, u32[]{:S(2)}, u32[]{:S(2)}) async-start(f32[8,32,128]{2,1,0:T(8,128)} %get-tuple-element.62), calls=%async_computation.9 | async-start | bytes 262144 | tf_op jit(solution)/shard_map/all_to_all | solution.py:50
  234.4 0.7 copy-start.16
  237.4 0.8 copy-start.18
  238.2 3.7 %copy-start.19 = (bf16[4,544,128]{2,1,0:T(8,128)(2,1)S(1)}, bf16[4,544,128]{2,1,0:T(8,128)(2,1)}, u32[]{:S(2)}) copy-start(bf16[4,544,128]{2,1,0:T(8,128)(2,1)} %copy-done.18) | copy-start | bytes 1671172
  238.2 16.9 %all-to-all-start.9 = ((bf16[4,256,512]{2,1,0:T(8,128)(2,1)}), bf16[4,256,512]{2,1,0:T(8,128)(2,1)S(1)}, u32[]{:S(2)}, u32[]{:S(2)}) async-start(bf16[4,256,512]{2,1,0:T(8,128)(2,1)} %get-tuple-element.64), calls=%async_computation.10 | async-start | bytes 2097152 | tf_op jit(solution)/shard_map/all_to_all | solution.py:36
  241.9 12.2 %collective-permute-start.2 = (bf16[4,544,128]{2,1,0:T(8,128)(2,1)S(1)}, bf16[4,544,128]{2,1,0:T(8,128)(2,1)S(1)}, u32[]{:S(2)}, u32[]{:S(2)}) collective-permute-start(bf16[4,544,128]{2,1,0:T(8,128)(2,1)S(1)} %copy-done.19), channel_id=1, source_target_pairs={{0,256},{256,0},{1,257},{257,1},{2,258},{258,2},{3,259},{259,3},{4... | collective-permute-start | bytes 1671176 | tf_op jit(solution)/shard_map/ppermute | solution.py:69
  251.0 3.0 collective-permute-start.3
  254.2 4.4 %copy-start.7 = (bf16[256,512]{1,0:T(8,128)(2,1)S(1)}, bf16[256,512]{1,0:T(8,128)(2,1)}, u32[]{:S(2)}) copy-start(bf16[256,512]{1,0:T(8,128)(2,1)} %reduce-scatter.2.cloned.1.call-done.refs_1_) | copy-start | bytes 786436
  255.1 10.6 %all-to-all-start.10 = ((bf16[4,544,128]{2,1,0:T(8,128)(2,1)}), bf16[4,544,128]{2,1,0:T(8,128)(2,1)S(1)}, u32[]{:S(2)}, u32[]{:S(2)}) async-start(bf16[4,544,128]{2,1,0:T(8,128)(2,1)} %add_convert_fusion), calls=%async_computation.11 | async-start | bytes 1114112 | tf_op jit(solution)/shard_map/all_to_all | solution.py:46
  265.8 35.9 %all-to-all-start.11 = ((bf16[8,64,512]{2,1,0:T(8,128)(2,1)}), bf16[8,64,512]{2,1,0:T(8,128)(2,1)S(1)}, u32[]{:S(2)}, u32[]{:S(2)}) async-start(bf16[8,64,512]{2,1,0:T(8,128)(2,1)} %shard_map.169), calls=%async_computation.12 | async-start | bytes 1048576 | tf_op jit(solution)/shard_map/all_to_all | solution.py:41
  272.7 16.1 %collective-permute-start.4 = (bf16[544,128]{1,0:T(8,128)(2,1)S(1)}, bf16[544,128]{1,0:T(8,128)(2,1)S(1)}, u32[]{:S(2)}, u32[]{:S(2)}) collective-permute-start(bf16[544,128]{1,0:T(8,128)(2,1)S(1)} %reduce_sum.12), channel_id=1, source_target_pairs={{0,128},{32,160},{64,192},{96,224},{128,0},{160,32},{192,64},{224,... | collective-permute-start | bytes 417800 | tf_op jit(solution)/shard_map/ppermute | solution.py:69
  311.5 18.4 %collective-permute-start.5 = (bf16[4,544,128]{2,1,0:T(8,128)(2,1)S(1)}, bf16[4,544,128]{2,1,0:T(8,128)(2,1)S(1)}, u32[]{:S(2)}, u32[]{:S(2)}) collective-permute-start(bf16[4,544,128]{2,1,0:T(8,128)(2,1)S(1)} %all_to_all.67.refs_0_), channel_id=1, source_target_pairs={{0,256},{256,0},{1,257},{257,1},{2,258},{258,2},{3,259},{259,3},{4... | collective-permute-start | bytes 1671176 | tf_op jit(solution)/shard_map/ppermute | solution.py:69
Sparse Core Ops, SparseCore 0:
  94.5 35.1 all-gather.1
  152.3 31.2 reduce-scatter.1

commit v4 on v3

--- a/solution.py
+++ b/solution.py
@@ -138,26 +138,37 @@
     return jnp.where(lane == start, first, jnp.where(lane == start + 1, second, 0.0))
 
 
+def square_of(rows):
+    pad = jnp.zeros((LANES - rows.shape[0], LANES), F32)
+    return jnp.concatenate([rows, pad], 0).T
+
+
 def write_edges(out_ref, value, first, second, columns, me):
-    local = value.shape[1]
-    lane = lane_of(LANES)
-    sums = column_tile(first, second, columns)
-    low = jnp.where(lane < columns, value[:, :LANES], sums)
-    last = pltpu.roll(value[:, local - LANES :], columns, 1)
-    high = jnp.where(lane < columns, last, sums)
+    width, local = value.shape
+    half = width // 2
+    left = lane_of(LANES) < columns
+    sums = square_of(column_tile(first, second, 0))[:8]
+    head, last = value[:, :LANES], value[:, local - LANES :]
+    low = jnp.where(left, head[:half], pltpu.roll(head[half:], columns, 1))
+    high = jnp.where(left, pltpu.roll(last[:half], columns, 1), last[half:])
     for peer in range(out_ref.shape[0]):
-        out_ref[peer] = jnp.where(me > peer, low, high)
+        out_ref[peer, :half] = jnp.where(me > peer, low, high)
+        out_ref[peer, half:] = sums
 
 
 def read_edges(in_ref, columns, me):
-    count = in_ref.shape[0]
-    total = in_ref[0]
+    count, rows = in_ref.shape[:2]
+    half = rows - 8
+    total = in_ref[0, half:]
     for peer in range(1, count):
-        total = total + in_ref[peer]
-    beyond = in_ref[jnp.minimum(me + 1, count - 1)]
-    before = pltpu.roll(in_ref[jnp.maximum(me - 1, 0)], columns, 1)
-    edge = jnp.where(lane_of(LANES) < columns, beyond, before)
-    return edge, total[:, columns : columns + 1], total[:, columns + 1 : columns + 2]
+        total = total + in_ref[peer, half:]
+    beyond = in_ref[jnp.minimum(me + 1, count - 1)][:half]
+    before = in_ref[jnp.maximum(me - 1, 0)][:half]
+    left = lane_of(LANES) < columns
+    top = jnp.where(left, beyond, pltpu.roll(before, columns, 1))
+    low = jnp.where(left, pltpu.roll(beyond, columns, 1), before)
+    square = square_of(total)[: 2 * half]
+    return jnp.concatenate([top, low], 0), square[:, 0:1], square[:, 1:2]
 
 
 def write_rows(out_ref, first, second):
@@ -421,7 +432,7 @@
 
     conv_a, source, pay = call(
         functools.partial(conv_kernel, columns),
-        [((width, local), F32), ((width, local), F32), ((n_batch, width, LANES), F32)],
+        [((width, local), F32), ((width, local), F32), ((n_batch, width // 2 + 8, LANES), F32)],
         (x_rows, edge, taps),
         [pltpu.VMEM((9 * width, local + 2 * columns), F32)],
     )
@@ -477,7 +488,7 @@
         [
             ((width, local), F32),
             ((width, local), F32),
-            ((n_batch, width, LANES), F32),
+            ((n_batch, width // 2 + 8, LANES), F32),
         ],
         (along_z(part), cotan_own, norm_a, gain_a, bias_a),
     )

time: 340 us -> 339 us (level)
  no operation moved by 1% of the time
where the time goes in v4:
time: 339 us; the launch traced here: 338 us
  starting transfers between devices  124 us (37%)
  waiting for transfers between devices  115 us (34%)
  blocking collectives  49.4 us (15%)
  Pallas kernels  16.5 us (5%)
  local copies, waits for them, and re-layouts  16.4 us (5%)
  between operations  14.4 us (4%)
    all_to_all x3, waiting for transfers between devices, along_batch(): return lax.all_to_all(parts, 'batch', 0, 0)  38.6 us
    all_to_all x3, starting transfers between devices, along_z(): return lax.all_to_all(parts, 'chan', 0, 0, axis_index_groups=z_groups(n))  37.9 us
    all_to_all x3, starting transfers between devices, along_batch(): return lax.all_to_all(parts, 'batch', 0, 0)  36.9 us
    all_to_all x3, waiting for transfers between devices, along_x(): return lax.all_to_all(parts, 'chan', 0, 0, axis_index_groups=x_groups(n))  28.1 us
    ppermute x4, starting transfers between devices, partner(): return lax.ppermute(value, axis, [(i, i ^ step) for i in range(n)])  28.1 us
    all_to_all x3, waiting for transfers between devices, along_z(): return lax.all_to_all(parts, 'chan', 0, 0, axis_index_groups=z_groups(n))  25.2 us
    all_to_all x1, blocking collectives, along_z(): return lax.all_to_all(parts, 'chan', 0, 0, axis_index_groups=z_groups(n))  22.4 us
    all_to_all x1, blocking collectives, along_batch(): return lax.all_to_all(parts, 'batch', 0, 0)  17.2 us
  transfers between devices with their start and end apart: 18, of which 12 were waited for; matrix products, arithmetic and copies ran while one was open for 3% of the time, Pallas kernels for 2%

profile of v4, /device:TPU:1, one launch (start us, length us, event | category | flops | bytes accessed | tf_op | source)
XLA Modules:
  0.0 337.9 jit_solution(13861292930601683903)
XLA Ops:
  7.2 1.0 copy.32
  8.3 0.7 broadcast_in_dim.39
  9.0 13.1 %all-to-all-start = ((bf16[8,32,512]{2,1,0:T(8,128)(2,1)}), bf16[8,32,512]{2,1,0:T(8,128)(2,1)S(1)}, u32[]{:S(2)}, u32[]{:S(2)}) async-start(bf16[8,32,512]{2,1,0:T(8,128)(2,1)} %broadcast_in_dim.39), calls=%async_computation | async-start | bytes 524288 | tf_op jit(solution)/shard_map/all_to_all | solution.py:41
  22.1 0.7 slice_bitcast_fusion.1
  22.8 1.4 collective-permute-start
  24.3 4.6 %collective-permute-start.1 = (bf16[64,1024]{1,0:T(8,128)(2,1)}, bf16[64,1024]{1,0:T(8,128)(2,1)}, u32[]{:S(2)}, u32[]{:S(2)}) collective-permute-start(bf16[64,1024]{1,0:T(8,128)(2,1)} %get-tuple-element.80), channel_id=1, source_target_pairs={{0,32},{32,64},{64,96},{96,128},{128,160},{160,192},{192,224},{1,3... | collective-permute-start | bytes 393224 | tf_op jit(solution)/shard_map/ppermute | solution.py:426
  29.2 1.3 collective-permute-done.1
  30.5 0.9 pad_maximum_fusion.refs_1_
  31.5 1.7 shard_map.160
  33.2 1.1 all-to-all-done
  34.3 24.3 %all-to-all-start.1 = ((f32[8,24,128]{2,1,0:T(8,128)}), f32[8,24,128]{2,1,0:T(8,128)S(1)}, u32[]{:S(2)}, u32[]{:S(2)}) async-start(f32[8,24,128]{2,1,0:T(8,128)} %get-tuple-element.47), calls=%async_computation.1 | async-start | bytes 196608 | tf_op jit(solution)/shard_map/all_to_all | solution.py:50
  58.8 13.8 %all-to-all-done.1.refs_2_ = f32[8,24,128]{2,1,0:T(8,128)S(1)} async-done(((f32[8,24,128]{2,1,0:T(8,128)}), f32[8,24,128]{2,1,0:T(8,128)S(1)}, u32[]{:S(2)}, u32[]{:S(2)}) %all-to-all-start.1) | async-done | bytes 98336 | tf_op jit(solution)/shard_map/all_to_all | solution.py:50
  72.6 1.0 shard_map.161
  73.6 17.9 %all-to-all-start.2 = ((bf16[8,32,512]{2,1,0:T(8,128)(2,1)}), bf16[8,32,512]{2,1,0:T(8,128)(2,1)S(1)}, u32[]{:S(2)}, u32[]{:S(2)}) async-start(bf16[8,32,512]{2,1,0:T(8,128)(2,1)} %get-tuple-element.48.refs_2_), calls=%async_computation.2 | async-start | bytes 524288 | tf_op jit(solution)/shard_map/all_to_all | solution.py:41
  91.6 0.7 all-gather.2.cloned.1.call-update
  92.2 11.2 %all-to-all-done.2 = bf16[8,32,512]{2,1,0:T(8,128)(2,1)S(1)} async-done(((bf16[8,32,512]{2,1,0:T(8,128)(2,1)}), bf16[8,32,512]{2,1,0:T(8,128)(2,1)S(1)}, u32[]{:S(2)}, u32[]{:S(2)}) %all-to-all-start.2) | async-done | bytes 262176 | tf_op jit(solution)/shard_map/all_to_all | solution.py:41
  103.4 1.1 broadcast_in_dim.43
  104.5 4.0 %all-to-all-start.3 = ((bf16[4,256,512]{2,1,0:T(8,128)(2,1)}), bf16[4,256,512]{2,1,0:T(8,128)(2,1)S(1)}, u32[]{:S(2)}, u32[]{:S(2)}) async-start(bf16[4,256,512]{2,1,0:T(8,128)(2,1)} %broadcast_in_dim.43), calls=%async_computation.3 | async-start | bytes 2097152 | tf_op jit(solution)/shard_map/all_to_all | solution.py:36
  108.7 19.0 %all-to-all-done.3.refs_0_ = bf16[4,256,512]{2,1,0:T(8,128)(2,1)S(1)} async-done(((bf16[4,256,512]{2,1,0:T(8,128)(2,1)}), bf16[4,256,512]{2,1,0:T(8,128)(2,1)S(1)}, u32[]{:S(2)}, u32[]{:S(2)}) %all-to-all-start.3) | async-done | bytes 1048608 | tf_op jit(solution)/shard_map/all_to_all | solution.py:36
  127.6 1.0 shard_map.162
  128.7 0.7 copy-done.8
  129.4 3.3 all-to-all-start.4
  132.8 0.8 copy.41.refs_5_
  133.7 0.7 copy.39.refs_3_
  134.4 0.7 copy.40.refs_4_
  135.1 11.4 %all-to-all-done.4.refs_2_ = f32[8,8,128]{2,1,0:T(8,128)S(1)} async-done(((f32[8,8,128]{2,1,0:T(8,128)}), f32[8,8,128]{2,1,0:T(8,128)S(1)}, u32[]{:S(2)}, u32[]{:S(2)}) %all-to-all-start.4) | async-done | bytes 32800 | tf_op jit(solution)/shard_map/all_to_all | solution.py:50
  146.5 0.6 copy-done.24
  147.1 4.8 %shard_map.163 = (bf16[128,512]{1,0:T(8,128)(2,1)}, f32[128,512]{1,0:T(8,128)}, f32[128,512]{1,0:T(8,128)}, f32[8,8,128]{2,1,0:T(8,128)}, f32[128,128]{1,0:T(8,128)}, /*index=5*/bf16[1024,512]{1,0:T(8,128)(2,1)}) custom-call(f32[128,512]{1,0:T(8,128)} %copy-done.8, bf16[1024,512]{1,0:T(8,128)(2,1)} %all-gather.2.cloned.1.call-done.refs_1_, ...), custom_call_target="tpu_custom_call" | custom-call | tf_op jit(solution)/shard_map/pallas_call | solution.py:120
  151.9 17.2 %all_to_all.65.refs_2_ = f32[8,8,128]{2,1,0:T(8,128)S(1)} all-to-all(f32[8,8,128]{2,1,0:T(8,128)} %get-tuple-element.53), channel_id=1, replica_groups=mesh['section'=2,'batch'=8,'chan'=32] {'batch'}, dimensions={0} | all-to-all | bytes 65536 | tf_op jit(solution)/shard_map/all_to_all | solution.py:50
  169.2 0.6 shard_map.164
  169.8 1.0 copy-done.6
  170.8 0.7 copy-done.12
  171.5 0.6 copy-done.17
  172.0 3.5 %all-to-all-start.6 = ((bf16[4,256,512]{2,1,0:T(8,128)(2,1)}), bf16[4,256,512]{2,1,0:T(8,128)(2,1)S(1)}, u32[]{:S(2)}, u32[]{:S(2)}) async-start(bf16[4,256,512]{2,1,0:T(8,128)(2,1)} %copy-done.6), calls=%async_computation.6 | async-start | bytes 2097152 | tf_op jit(solution)/shard_map/all_to_all | solution.py:36
  175.6 1.2 copy-done.1
  176.8 0.7 shard_map.166.refs_6_
  177.5 0.8 copy-done.4
  178.3 9.1 %all-to-all-done.6.refs_0_ = bf16[4,256,512]{2,1,0:T(8,128)(2,1)S(1)} async-done(((bf16[4,256,512]{2,1,0:T(8,128)(2,1)}), bf16[4,256,512]{2,1,0:T(8,128)(2,1)S(1)}, u32[]{:S(2)}, u32[]{:S(2)}) %all-to-all-start.6) | async-done | bytes 1048608 | tf_op jit(solution)/shard_map/all_to_all | solution.py:36
  187.6 22.4 %all_to_all.66.refs_0_ = bf16[8,32,512]{2,1,0:T(8,128)(2,1)S(1)} all-to-all(bf16[8,32,512]{2,1,0:T(8,128)(2,1)S(1)} %shard_map.165), channel_id=1, replica_groups={{0,4,8,12,16,20,24,28},{1,5,9,13,17,21,25,29},{2,6,10,14,18,22,26,30},{..., dimensions={0} | all-to-all | bytes 524288 | tf_op jit(solution)/shard_map/all_to_all | solution.py:41
  210.0 0.9 shard_map.167
  210.9 9.2 %all-to-all-start.8 = ((f32[8,24,128]{2,1,0:T(8,128)}), f32[8,24,128]{2,1,0:T(8,128)S(1)}, u32[]{:S(2)}, u32[]{:S(2)}) async-start(f32[8,24,128]{2,1,0:T(8,128)} %get-tuple-element.62), calls=%async_computation.9 | async-start | bytes 196608 | tf_op jit(solution)/shard_map/all_to_all | solution.py:50
  220.1 0.7 slice.35
  220.8 13.4 %all-to-all-done.8.refs_1_ = f32[8,24,128]{2,1,0:T(8,128)S(1)} async-done(((f32[8,24,128]{2,1,0:T(8,128)}), f32[8,24,128]{2,1,0:T(8,128)S(1)}, u32[]{:S(2)}, u32[]{:S(2)}) %all-to-all-start.8) | async-done | bytes 98336 | tf_op jit(solution)/shard_map/all_to_all | solution.py:50
  234.2 0.7 copy-done.16
  234.9 2.2 shard_map.168
  237.1 0.8 copy-done.18
  237.9 3.6 %all-to-all-start.9 = ((bf16[4,256,512]{2,1,0:T(8,128)(2,1)}), bf16[4,256,512]{2,1,0:T(8,128)(2,1)S(1)}, u32[]{:S(2)}, u32[]{:S(2)}) async-start(bf16[4,256,512]{2,1,0:T(8,128)(2,1)} %get-tuple-element.64), calls=%async_computation.10 | async-start | bytes 2097152 | tf_op jit(solution)/shard_map/all_to_all | solution.py:36
  241.5 9.0 %collective-permute-start.2 = (bf16[4,544,128]{2,1,0:T(8,128)(2,1)S(1)}, bf16[4,544,128]{2,1,0:T(8,128)(2,1)S(1)}, u32[]{:S(2)}, u32[]{:S(2)}) collective-permute-start(bf16[4,544,128]{2,1,0:T(8,128)(2,1)S(1)} %copy-done.19), channel_id=1, source_target_pairs={{0,256},{256,0},{1,257},{257,1},{2,258},{258,2},{3,259},{259,3},{4... | collective-permute-start | bytes 1671176 | tf_op jit(solution)/shard_map/ppermute | solution.py:69
  250.7 1.9 collective-permute-start.3
  252.6 1.1 collective-permute-done.3
  253.8 1.0 add_convert_fusion
  254.8 3.5 %all-to-all-start.10 = ((bf16[4,544,128]{2,1,0:T(8,128)(2,1)}), bf16[4,544,128]{2,1,0:T(8,128)(2,1)S(1)}, u32[]{:S(2)}, u32[]{:S(2)}) async-start(bf16[4,544,128]{2,1,0:T(8,128)(2,1)} %add_convert_fusion), calls=%async_computation.11 | async-start | bytes 1114112 | tf_op jit(solution)/shard_map/all_to_all | solution.py:46
  258.2 0.9 shard_map.169
  259.2 6.1 %all-to-all-done.10 = bf16[4,544,128]{2,1,0:T(8,128)(2,1)S(1)} async-done(((bf16[4,544,128]{2,1,0:T(8,128)(2,1)}), bf16[4,544,128]{2,1,0:T(8,128)(2,1)S(1)}, u32[]{:S(2)}, u32[]{:S(2)}) %all-to-all-start.10) | async-done | bytes 557088 | tf_op jit(solution)/shard_map/all_to_all | solution.py:46
  265.4 6.9 %all-to-all-start.11 = ((bf16[8,64,512]{2,1,0:T(8,128)(2,1)}), bf16[8,64,512]{2,1,0:T(8,128)(2,1)S(1)}, u32[]{:S(2)}, u32[]{:S(2)}) async-start(bf16[8,64,512]{2,1,0:T(8,128)(2,1)} %shard_map.169), calls=%async_computation.12 | async-start | bytes 1048576 | tf_op jit(solution)/shard_map/all_to_all | solution.py:41
  272.3 1.9 collective-permute-start.4
  274.2 14.2 %collective-permute-done.4 = bf16[544,128]{1,0:T(8,128)(2,1)S(1)} collective-permute-done((bf16[544,128]{1,0:T(8,128)(2,1)S(1)}, bf16[544,128]{1,0:T(8,128)(2,1)S(1)}, u32[]{:S(2)}, u32[]{:S(2)}) %collective-permute-start.4) | collective-permute-done | bytes 139296 | tf_op jit(solution)/shard_map/ppermute | solution.py:69
  288.5 12.9 %all-to-all-done.11.refs_0_ = bf16[8,64,512]{2,1,0:T(8,128)(2,1)S(1)} async-done(((bf16[8,64,512]{2,1,0:T(8,128)(2,1)}), bf16[8,64,512]{2,1,0:T(8,128)(2,1)S(1)}, u32[]{:S(2)}, u32[]{:S(2)}) %all-to-all-start.11) | async-done | bytes 524320 | tf_op jit(solution)/shard_map/all_to_all | solution.py:41
  301.5 9.8 %all_to_all.67.refs_0_ = bf16[4,544,128]{2,1,0:T(8,128)(2,1)S(1)} all-to-all(bf16[4,544,128]{2,1,0:T(8,128)(2,1)S(1)} %broadcast_in_dim.48), channel_id=1, replica_groups={{0,32,64,96},{128,160,192,224},{1,33,65,97},{129,161,193,225},{2,34,66,..., dimensions={0} | all-to-all | bytes 1114112 | tf_op jit(solution)/shard_map/all_to_all | solution.py:46
  311.2 15.3 %collective-permute-start.5 = (bf16[4,544,128]{2,1,0:T(8,128)(2,1)S(1)}, bf16[4,544,128]{2,1,0:T(8,128)(2,1)S(1)}, u32[]{:S(2)}, u32[]{:S(2)}) collective-permute-start(bf16[4,544,128]{2,1,0:T(8,128)(2,1)S(1)} %all_to_all.67.refs_0_), channel_id=1, source_target_pairs={{0,256},{256,0},{1,257},{257,1},{2,258},{258,2},{3,259},{259,3},{4... | collective-permute-start | bytes 1671176 | tf_op jit(solution)/shard_map/ppermute | solution.py:69
  327.1 0.6 slice_bitcast_fusion.3
  327.6 1.0 shard_map.170
  328.9 0.7 copy_bitcast_fusion
  329.6 1.5 shard_map.171
  (76 shorter events, 2.2 us)
Async XLA Ops:
  7.2 14.9 %copy-start = (bf16[1,1,8,64,1024]{4,3,2,1,0:T(8,128)(2,1)S(1)}, bf16[1,1,8,64,1024]{4,3,2,1,0:T(8,128)(2,1)}, u32[]{:S(2)}) copy-start(bf16[1,1,8,64,1024]{4,3,2,1,0:T(8,128)(2,1)} %param.9) | copy-start | bytes 3145732
  7.2 21.7 %copy-start.22 = (bf16[1024,128]{1,0:T(8,128)(2,1)S(1)}, bf16[1024,128]{1,0:T(8,128)(2,1)}, u32[]{:S(2)}) copy-start(bf16[1024,128]{1,0:T(8,128)(2,1)} %param.13) | copy-start | bytes 786436
  7.2 21.7 %copy-start.23 = (bf16[128,1024]{1,0:T(8,128)(2,1)S(1)}, bf16[128,1024]{1,0:T(8,128)(2,1)}, u32[]{:S(2)}) copy-start(bf16[128,1024]{1,0:T(8,128)(2,1)} %param.16) | copy-start | bytes 786436
  9.0 25.3 %all-to-all-start = ((bf16[8,32,512]{2,1,0:T(8,128)(2,1)}), bf16[8,32,512]{2,1,0:T(8,128)(2,1)S(1)}, u32[]{:S(2)}, u32[]{:S(2)}) async-start(bf16[8,32,512]{2,1,0:T(8,128)(2,1)} %broadcast_in_dim.39), calls=%async_computation | async-start | bytes 524288 | tf_op jit(solution)/shard_map/all_to_all | solution.py:41
  22.8 8.6 %copy-start.2 = (bf16[3,3,1024,32]{2,3,1,0:T(8,128)(2,1)S(1)}, bf16[3,3,1024,32]{2,3,1,0:T(8,128)(2,1)}, u32[]{:S(2)}) copy-start(bf16[3,3,1024,32]{2,3,1,0:T(8,128)(2,1)} %param.10) | copy-start | bytes 1769476
  22.8 6.3 %collective-permute-start = (bf16[64,1024]{1,0:T(8,128)(2,1)}, bf16[64,1024]{1,0:T(8,128)(2,1)S(1)}, u32[]{:S(2)}, u32[]{:S(2)}) collective-permute-start(bf16[64,1024]{1,0:T(8,128)(2,1)} %get-tuple-element.79), channel_id=1, source_target_pairs={{32,0},{64,32},{96,64},{128,96},{160,128},{192,160},{224,192},{33,... | collective-permute-start | bytes 393224 | tf_op jit(solution)/shard_map/ppermute | solution.py:427
  24.3 6.2 %collective-permute-start.1 = (bf16[64,1024]{1,0:T(8,128)(2,1)}, bf16[64,1024]{1,0:T(8,128)(2,1)}, u32[]{:S(2)}, u32[]{:S(2)}) collective-permute-start(bf16[64,1024]{1,0:T(8,128)(2,1)} %get-tuple-element.80), channel_id=1, source_target_pairs={{0,32},{32,64},{64,96},{96,128},{128,160},{160,192},{192,224},{1,3... | collective-permute-start | bytes 393224 | tf_op jit(solution)/shard_map/ppermute | solution.py:426
  29.1 103.7 %copy-start.20 = (bf16[4,8,32,128]{3,2,1,0:T(8,128)(2,1)}, bf16[4,8,32,128]{3,2,1,0:T(8,128)(2,1)S(1)}, u32[]{:S(2)}) copy-start(bf16[4,8,32,128]{3,2,1,0:T(8,128)(2,1)S(1)} %copy.35) | copy-start | bytes 786436
  31.4 27.2 %copy-start.27 = (f32[32]{0:T(128)S(1)}, f32[32]{0:T(128)}, u32[]{:S(2)}) copy-start(f32[32]{0:T(128)} %param.11) | copy-start | bytes 388
  31.4 27.3 %copy-start.28 = (f32[32]{0:T(128)S(1)}, f32[32]{0:T(128)}, u32[]{:S(2)}) copy-start(f32[32]{0:T(128)} %param.12) | copy-start | bytes 388
  34.3 57.2 %copy-start.21 = (bf16[8,32,512]{2,1,0:T(8,128)(2,1)}, bf16[8,32,512]{2,1,0:T(8,128)(2,1)S(1)}, u32[]{:S(2)}) copy-start(bf16[8,32,512]{2,1,0:T(8,128)(2,1)S(1)} %all-to-all-done) | copy-start | bytes 786436
  34.3 38.3 %all-to-all-start.1 = ((f32[8,24,128]{2,1,0:T(8,128)}), f32[8,24,128]{2,1,0:T(8,128)S(1)}, u32[]{:S(2)}, u32[]{:S(2)}) async-start(f32[8,24,128]{2,1,0:T(8,128)} %get-tuple-element.47), calls=%async_computation.1 | async-start | bytes 196608 | tf_op jit(solution)/shard_map/all_to_all | solution.py:50
  73.6 30.9 %copy-start.15 = (f32[32,128]{1,0:T(8,128)}, f32[32,128]{1,0:T(8,128)S(1)}, u32[]{:S(2)}) copy-start(f32[32,128]{1,0:T(8,128)S(1)} %get-tuple-element.63.refs_3_) | copy-start | bytes 49156
  73.6 29.8 %all-to-all-start.2 = ((bf16[8,32,512]{2,1,0:T(8,128)(2,1)}), bf16[8,32,512]{2,1,0:T(8,128)(2,1)S(1)}, u32[]{:S(2)}, u32[]{:S(2)}) async-start(bf16[8,32,512]{2,1,0:T(8,128)(2,1)} %get-tuple-element.48.refs_2_), calls=%async_computation.2 | async-start | bytes 524288 | tf_op jit(solution)/shard_map/all_to_all | solution.py:41
  91.5 43.6 %all-gather.2.cloned.1.call-start = ((), (), s32[]{:S(2)}) async-start(), calls=%async_computation.14 | async-start | bytes 1310720 | tf_op jit(solution)/shard_map/all_gather | solution.py:421
  104.5 23.2 %all-to-all-start.3 = ((bf16[4,256,512]{2,1,0:T(8,128)(2,1)}), bf16[4,256,512]{2,1,0:T(8,128)(2,1)S(1)}, u32[]{:S(2)}, u32[]{:S(2)}) async-start(bf16[4,256,512]{2,1,0:T(8,128)(2,1)} %broadcast_in_dim.43), calls=%async_computation.3 | async-start | bytes 2097152 | tf_op jit(solution)/shard_map/all_to_all | solution.py:36
  108.5 25.2 %copy-start.25 = (f32[128]{0:T(128)S(1)}, f32[128]{0:T(128)}, u32[]{:S(2)}) copy-start(f32[128]{0:T(128)} %param.14) | copy-start | bytes 1540
  108.7 25.7 %copy-start.26 = (f32[128]{0:T(128)S(1)}, f32[128]{0:T(128)}, u32[]{:S(2)}) copy-start(f32[128]{0:T(128)} %param.15) | copy-start | bytes 1540
  128.7 0.7 copy-start.8
  129.4 17.1 %all-to-all-start.4 = ((f32[8,8,128]{2,1,0:T(8,128)}), f32[8,8,128]{2,1,0:T(8,128)S(1)}, u32[]{:S(2)}, u32[]{:S(2)}) async-start(f32[8,8,128]{2,1,0:T(8,128)} %get-tuple-element.50), calls=%async_computation.4 | async-start | bytes 65536 | tf_op jit(solution)/shard_map/all_to_all | solution.py:50
  132.7 54.9 %reduce-scatter.2.cloned.1.call-start = ((), (), s32[]{:S(2)}) async-start(), calls=%async_computation.15 | async-start | bytes 1310720 | tf_op jit(solution)/shard_map/reduce_scatter | solution.py:471
  146.5 0.6 copy-start.24
  151.9 17.3 %copy-start.9 = (f32[128,512]{1,0:T(8,128)S(1)}, f32[128,512]{1,0:T(8,128)}, u32[]{:S(2)}) copy-start(f32[128,512]{1,0:T(8,128)} %get-tuple-element.52.refs_1_) | copy-start | bytes 786436
  151.9 17.3 %copy-start.10 = (f32[128,512]{1,0:T(8,128)S(1)}, f32[128,512]{1,0:T(8,128)}, u32[]{:S(2)}) copy-start(f32[128,512]{1,0:T(8,128)} %get-tuple-element.51.refs_0_) | copy-start | bytes 786436
  151.9 17.3 %copy-start.14 = (f32[128,128]{1,0:T(8,128)S(1)}, f32[128,128]{1,0:T(8,128)}, u32[]{:S(2)}) copy-start(f32[128,128]{1,0:T(8,128)} %get-tuple-element.54.refs_3_) | copy-start | bytes 196612
  169.8 1.0 copy-start.6
  170.8 0.7 copy-start.12
  171.4 0.6 copy-start.17
  171.4 4.1 %copy-start.11 = (bf16[128,512]{1,0:T(8,128)(2,1)S(1)}, bf16[128,512]{1,0:T(8,128)(2,1)}, u32[]{:S(2)}) copy-start(bf16[128,512]{1,0:T(8,128)(2,1)} %get-tuple-element.57.refs_3_) | copy-start | bytes 393220
  171.5 4.1 %copy-start.13 = (bf16[128,512]{1,0:T(8,128)(2,1)S(1)}, bf16[128,512]{1,0:T(8,128)(2,1)}, u32[]{:S(2)}) copy-start(bf16[128,512]{1,0:T(8,128)(2,1)} %copy-done.12) | copy-start | bytes 393220
  172.0 15.4 %all-to-all-start.6 = ((bf16[4,256,512]{2,1,0:T(8,128)(2,1)}), bf16[4,256,512]{2,1,0:T(8,128)(2,1)S(1)}, u32[]{:S(2)}, u32[]{:S(2)}) async-start(bf16[4,256,512]{2,1,0:T(8,128)(2,1)} %copy-done.6), calls=%async_computation.6 | async-start | bytes 2097152 | tf_op jit(solution)/shard_map/all_to_all | solution.py:36
  175.6 1.2 copy-start.1
  177.5 0.8 copy-start.4
  178.3 55.8 %copy-start.3 = (bf16[3,3,1024,32]{2,3,1,0:T(8,128)(2,1)S(1)}, bf16[3,3,1024,32]{2,3,1,0:T(8,128)(2,1)}, u32[]{:S(2)}) copy-start(bf16[3,3,1024,32]{2,3,1,0:T(8,128)(2,1)} %param.10) | copy-start | bytes 1769476
  187.6 46.6 %copy-start.5 = (bf16[8,256,128]{2,1,0:T(8,128)(2,1)S(1)}, bf16[8,256,128]{2,1,0:T(8,128)(2,1)}, u32[]{:S(2)}) copy-start(bf16[8,256,128]{2,1,0:T(8,128)(2,1)} %copy-done.4) | copy-start | bytes 1572868
  210.9 23.3 %all-to-all-start.8 = ((f32[8,24,128]{2,1,0:T(8,128)}), f32[8,24,128]{2,1,0:T(8,128)S(1)}, u32[]{:S(2)}, u32[]{:S(2)}) async-start(f32[8,24,128]{2,1,0:T(8,128)} %get-tuple-element.62), calls=%async_computation.9 | async-start | bytes 196608 | tf_op jit(solution)/shard_map/all_to_all | solution.py:50
  234.2 0.7 copy-start.16
  237.1 0.8 copy-start.18
  237.9 3.7 %copy-start.19 = (bf16[4,544,128]{2,1,0:T(8,128)(2,1)S(1)}, bf16[4,544,128]{2,1,0:T(8,128)(2,1)}, u32[]{:S(2)}) copy-start(bf16[4,544,128]{2,1,0:T(8,128)(2,1)} %copy-done.18) | copy-start | bytes 1671172
  237.9 16.9 %all-to-all-start.9 = ((bf16[4,256,512]{2,1,0:T(8,128)(2,1)}), bf16[4,256,512]{2,1,0:T(8,128)(2,1)S(1)}, u32[]{:S(2)}, u32[]{:S(2)}) async-start(bf16[4,256,512]{2,1,0:T(8,128)(2,1)} %get-tuple-element.64), calls=%async_computation.10 | async-start | bytes 2097152 | tf_op jit(solution)/shard_map/all_to_all | solution.py:36
  241.5 12.2 %collective-permute-start.2 = (bf16[4,544,128]{2,1,0:T(8,128)(2,1)S(1)}, bf16[4,544,128]{2,1,0:T(8,128)(2,1)S(1)}, u32[]{:S(2)}, u32[]{:S(2)}) collective-permute-start(bf16[4,544,128]{2,1,0:T(8,128)(2,1)S(1)} %copy-done.19), channel_id=1, source_target_pairs={{0,256},{256,0},{1,257},{257,1},{2,258},{258,2},{3,259},{259,3},{4... | collective-permute-start | bytes 1671176 | tf_op jit(solution)/shard_map/ppermute | solution.py:69
  250.7 3.0 collective-permute-start.3
  253.8 4.4 %copy-start.7 = (bf16[256,512]{1,0:T(8,128)(2,1)S(1)}, bf16[256,512]{1,0:T(8,128)(2,1)}, u32[]{:S(2)}) copy-start(bf16[256,512]{1,0:T(8,128)(2,1)} %reduce-scatter.2.cloned.1.call-done.refs_1_) | copy-start | bytes 786436
  254.8 10.6 %all-to-all-start.10 = ((bf16[4,544,128]{2,1,0:T(8,128)(2,1)}), bf16[4,544,128]{2,1,0:T(8,128)(2,1)S(1)}, u32[]{:S(2)}, u32[]{:S(2)}) async-start(bf16[4,544,128]{2,1,0:T(8,128)(2,1)} %add_convert_fusion), calls=%async_computation.11 | async-start | bytes 1114112 | tf_op jit(solution)/shard_map/all_to_all | solution.py:46
  265.4 36.0 %all-to-all-start.11 = ((bf16[8,64,512]{2,1,0:T(8,128)(2,1)}), bf16[8,64,512]{2,1,0:T(8,128)(2,1)S(1)}, u32[]{:S(2)}, u32[]{:S(2)}) async-start(bf16[8,64,512]{2,1,0:T(8,128)(2,1)} %shard_map.169), calls=%async_computation.12 | async-start | bytes 1048576 | tf_op jit(solution)/shard_map/all_to_all | solution.py:41
  272.3 16.1 %collective-permute-start.4 = (bf16[544,128]{1,0:T(8,128)(2,1)S(1)}, bf16[544,128]{1,0:T(8,128)(2,1)S(1)}, u32[]{:S(2)}, u32[]{:S(2)}) collective-permute-start(bf16[544,128]{1,0:T(8,128)(2,1)S(1)} %reduce_sum.12), channel_id=1, source_target_pairs={{0,128},{32,160},{64,192},{96,224},{128,0},{160,32},{192,64},{224,... | collective-permute-start | bytes 417800 | tf_op jit(solution)/shard_map/ppermute | solution.py:69
  311.2 18.3 %collective-permute-start.5 = (bf16[4,544,128]{2,1,0:T(8,128)(2,1)S(1)}, bf16[4,544,128]{2,1,0:T(8,128)(2,1)S(1)}, u32[]{:S(2)}, u32[]{:S(2)}) collective-permute-start(bf16[4,544,128]{2,1,0:T(8,128)(2,1)S(1)} %all_to_all.67.refs_0_), channel_id=1, source_target_pairs={{0,256},{256,0},{1,257},{257,1},{2,258},{258,2},{3,259},{259,3},{4... | collective-permute-start | bytes 1671176 | tf_op jit(solution)/shard_map/ppermute | solution.py:69
Sparse Core Ops, SparseCore 0:
  94.4 35.2 all-gather.1
  152.1 31.3 reduce-scatter.1

commit v5 on v3

--- a/solution.py
+++ b/solution.py
@@ -425,7 +425,7 @@
         (x_rows, edge, taps),
         [pltpu.VMEM((9 * width, local + 2 * columns), F32)],
     )
-    recv = along_batch(after(pay, cotan_line, up_cols, down_cols))
+    recv = along_batch(after(pay, cotan_line))
     stream, norm_a, fact_a = call(
         functools.partial(stream_kernel, columns, pixels),
         [

time: 340 us -> 339 us (level)
    unnamed x59 -> x55, local copies, waits for them, and re-layouts: 7.32 us -> 6.7 us
  transfers between devices with their start and end apart: 18 -> 18, of which waited for: 12 -> 13; matrix products, arithmetic and copies ran while one was open for 3% -> 2% of each run, Pallas kernels for 2% -> 2%
where the time goes in v5:
time: 339 us; the launch traced here: 337 us
  starting transfers between devices  121 us (36%)
  waiting for transfers between devices  119 us (35%)
  blocking collectives  49.2 us (15%)
  Pallas kernels  16.5 us (5%)
  local copies, waits for them, and re-layouts  15.1 us (4%)
  between operations  14.4 us (4%)
    all_to_all x3, starting transfers between devices, along_z(): return lax.all_to_all(parts, 'chan', 0, 0, axis_index_groups=z_groups(n))  38.9 us
    all_to_all x3, waiting for transfers between devices, along_batch(): return lax.all_to_all(parts, 'batch', 0, 0)  38.9 us
    all_to_all x3, starting transfers between devices, along_batch(): return lax.all_to_all(parts, 'batch', 0, 0)  34.8 us
    all_to_all x3, waiting for transfers between devices, along_x(): return lax.all_to_all(parts, 'chan', 0, 0, axis_index_groups=x_groups(n))  28.8 us
    ppermute x4, starting transfers between devices, partner(): return lax.ppermute(value, axis, [(i, i ^ step) for i in range(n)])  27.6 us
    all_to_all x3, waiting for transfers between devices, along_z(): return lax.all_to_all(parts, 'chan', 0, 0, axis_index_groups=z_groups(n))  27.4 us
    all_to_all x1, blocking collectives, along_z(): return lax.all_to_all(parts, 'chan', 0, 0, axis_index_groups=z_groups(n))  22.3 us
    all_to_all x1, blocking collectives, along_batch(): return lax.all_to_all(parts, 'batch', 0, 0)  17.2 us
  transfers between devices with their start and end apart: 18, of which 13 were waited for; matrix products, arithmetic and copies ran while one was open for 2% of the time, Pallas kernels for 2%

profile of v5, /device:TPU:1, one launch (start us, length us, event | category | flops | bytes accessed | tf_op | source)
XLA Modules:
  0.0 337.3 jit_solution(9872318509068389882)
XLA Ops:
  7.2 1.0 copy.32
  8.3 0.7 broadcast_in_dim.39
  9.0 13.1 %all-to-all-start = ((bf16[8,32,512]{2,1,0:T(8,128)(2,1)}), bf16[8,32,512]{2,1,0:T(8,128)(2,1)S(1)}, u32[]{:S(2)}, u32[]{:S(2)}) async-start(bf16[8,32,512]{2,1,0:T(8,128)(2,1)} %broadcast_in_dim.39), calls=%async_computation | async-start | bytes 524288 | tf_op jit(solution)/shard_map/all_to_all | solution.py:41
  22.1 1.3 collective-permute-start
  23.4 4.0 %collective-permute-start.1 = (bf16[64,1024]{1,0:T(8,128)(2,1)S(1)}, bf16[64,1024]{1,0:T(8,128)(2,1)S(1)}, u32[]{:S(2)}, u32[]{:S(2)}) collective-permute-start(bf16[64,1024]{1,0:T(8,128)(2,1)S(1)} %get-tuple-element.80), channel_id=1, source_target_pairs={{0,32},{32,64},{64,96},{96,128},{128,160},{160,192},{192,224},{1,3... | collective-permute-start | bytes 393224 | tf_op jit(solution)/shard_map/ppermute | solution.py:415
  27.4 0.7 collective-permute-done
  28.1 1.2 collective-permute-done.1
  29.4 1.7 shard_map.160
  31.1 3.2 all-to-all-done
  34.3 22.3 %all-to-all-start.1 = ((f32[8,32,128]{2,1,0:T(8,128)}), f32[8,32,128]{2,1,0:T(8,128)S(1)}, u32[]{:S(2)}, u32[]{:S(2)}) async-start(f32[8,32,128]{2,1,0:T(8,128)} %get-tuple-element.47), calls=%async_computation.1 | async-start | bytes 262144 | tf_op jit(solution)/shard_map/all_to_all | solution.py:50
  56.8 14.0 %all-to-all-done.1.refs_2_ = f32[8,32,128]{2,1,0:T(8,128)S(1)} async-done(((f32[8,32,128]{2,1,0:T(8,128)}), f32[8,32,128]{2,1,0:T(8,128)S(1)}, u32[]{:S(2)}, u32[]{:S(2)}) %all-to-all-start.1) | async-done | bytes 131104 | tf_op jit(solution)/shard_map/all_to_all | solution.py:50
  70.7 0.9 shard_map.161
  71.6 17.9 %all-to-all-start.2 = ((bf16[8,32,512]{2,1,0:T(8,128)(2,1)}), bf16[8,32,512]{2,1,0:T(8,128)(2,1)S(1)}, u32[]{:S(2)}, u32[]{:S(2)}) async-start(bf16[8,32,512]{2,1,0:T(8,128)(2,1)} %get-tuple-element.48.refs_2_), calls=%async_computation.2 | async-start | bytes 524288 | tf_op jit(solution)/shard_map/all_to_all | solution.py:41
  89.6 0.7 all-gather.2.cloned.1.call-update
  90.3 11.2 %all-to-all-done.2 = bf16[8,32,512]{2,1,0:T(8,128)(2,1)S(1)} async-done(((bf16[8,32,512]{2,1,0:T(8,128)(2,1)}), bf16[8,32,512]{2,1,0:T(8,128)(2,1)S(1)}, u32[]{:S(2)}, u32[]{:S(2)}) %all-to-all-start.2) | async-done | bytes 262176 | tf_op jit(solution)/shard_map/all_to_all | solution.py:41
  101.4 1.1 broadcast_in_dim.43
  102.5 4.1 %all-to-all-start.3 = ((bf16[4,256,512]{2,1,0:T(8,128)(2,1)}), bf16[4,256,512]{2,1,0:T(8,128)(2,1)S(1)}, u32[]{:S(2)}, u32[]{:S(2)}) async-start(bf16[4,256,512]{2,1,0:T(8,128)(2,1)} %broadcast_in_dim.43), calls=%async_computation.3 | async-start | bytes 2097152 | tf_op jit(solution)/shard_map/all_to_all | solution.py:36
  106.9 19.4 %all-to-all-done.3.refs_0_ = bf16[4,256,512]{2,1,0:T(8,128)(2,1)S(1)} async-done(((bf16[4,256,512]{2,1,0:T(8,128)(2,1)}), bf16[4,256,512]{2,1,0:T(8,128)(2,1)S(1)}, u32[]{:S(2)}, u32[]{:S(2)}) %all-to-all-start.3) | async-done | bytes 1048608 | tf_op jit(solution)/shard_map/all_to_all | solution.py:36
  126.3 1.0 shard_map.162
  127.3 0.7 copy-done.8
  128.0 3.3 all-to-all-start.4
  131.5 0.7 copy.39.refs_3_
  132.2 0.7 copy.40.refs_4_
  132.9 0.2 copy.37
  133.2 0.9 copy.41.refs_5_
  134.0 11.1 %all-to-all-done.4.refs_2_ = f32[8,8,128]{2,1,0:T(8,128)S(1)} async-done(((f32[8,8,128]{2,1,0:T(8,128)}), f32[8,8,128]{2,1,0:T(8,128)S(1)}, u32[]{:S(2)}, u32[]{:S(2)}) %all-to-all-start.4) | async-done | bytes 32800 | tf_op jit(solution)/shard_map/all_to_all | solution.py:50
  145.2 0.6 copy-done.22
  145.8 4.8 %shard_map.163 = (bf16[128,512]{1,0:T(8,128)(2,1)}, f32[128,512]{1,0:T(8,128)}, f32[128,512]{1,0:T(8,128)}, f32[8,8,128]{2,1,0:T(8,128)}, f32[128,128]{1,0:T(8,128)}, /*index=5*/bf16[1024,512]{1,0:T(8,128)(2,1)}) custom-call(f32[128,512]{1,0:T(8,128)} %copy-done.8, bf16[1024,512]{1,0:T(8,128)(2,1)} %all-gather.2.cloned.1.call-done.refs_1_, ...), custom_call_target="tpu_custom_call" | custom-call | tf_op jit(solution)/shard_map/pallas_call | solution.py:120
  150.6 17.2 %all_to_all.65.refs_2_ = f32[8,8,128]{2,1,0:T(8,128)S(1)} all-to-all(f32[8,8,128]{2,1,0:T(8,128)} %get-tuple-element.53), channel_id=1, replica_groups=mesh['section'=2,'batch'=8,'chan'=32] {'batch'}, dimensions={0} | all-to-all | bytes 65536 | tf_op jit(solution)/shard_map/all_to_all | solution.py:50
  167.8 0.6 shard_map.164
  168.5 1.0 copy-done.6
  169.4 0.6 copy-done.15
  170.0 3.5 %all-to-all-start.6 = ((bf16[4,256,512]{2,1,0:T(8,128)(2,1)}), bf16[4,256,512]{2,1,0:T(8,128)(2,1)S(1)}, u32[]{:S(2)}, u32[]{:S(2)}) async-start(bf16[4,256,512]{2,1,0:T(8,128)(2,1)} %copy-done.6), calls=%async_computation.6 | async-start | bytes 2097152 | tf_op jit(solution)/shard_map/all_to_all | solution.py:36
  173.6 1.2 copy-done.1
  174.8 0.7 shard_map.166.refs_6_
  175.5 0.8 copy-done.4
  176.3 9.4 %all-to-all-done.6.refs_0_ = bf16[4,256,512]{2,1,0:T(8,128)(2,1)S(1)} async-done(((bf16[4,256,512]{2,1,0:T(8,128)(2,1)}), bf16[4,256,512]{2,1,0:T(8,128)(2,1)S(1)}, u32[]{:S(2)}, u32[]{:S(2)}) %all-to-all-start.6) | async-done | bytes 1048608 | tf_op jit(solution)/shard_map/all_to_all | solution.py:36
  185.8 22.3 %all_to_all.66.refs_0_ = bf16[8,32,512]{2,1,0:T(8,128)(2,1)S(1)} all-to-all(bf16[8,32,512]{2,1,0:T(8,128)(2,1)S(1)} %shard_map.165), channel_id=1, replica_groups={{0,4,8,12,16,20,24,28},{1,5,9,13,17,21,25,29},{2,6,10,14,18,22,26,30},{..., dimensions={0} | all-to-all | bytes 524288 | tf_op jit(solution)/shard_map/all_to_all | solution.py:41
  208.1 0.8 shard_map.167
  208.9 9.2 %all-to-all-start.8 = ((f32[8,32,128]{2,1,0:T(8,128)}), f32[8,32,128]{2,1,0:T(8,128)S(1)}, u32[]{:S(2)}, u32[]{:S(2)}) async-start(f32[8,32,128]{2,1,0:T(8,128)} %get-tuple-element.62), calls=%async_computation.9 | async-start | bytes 262144 | tf_op jit(solution)/shard_map/all_to_all | solution.py:50
  218.1 0.7 slice.35
  218.8 13.8 %all-to-all-done.8.refs_1_ = f32[8,32,128]{2,1,0:T(8,128)S(1)} async-done(((f32[8,32,128]{2,1,0:T(8,128)}), f32[8,32,128]{2,1,0:T(8,128)S(1)}, u32[]{:S(2)}, u32[]{:S(2)}) %all-to-all-start.8) | async-done | bytes 131104 | tf_op jit(solution)/shard_map/all_to_all | solution.py:50
  232.6 0.7 copy-done.14
  233.3 2.3 shard_map.168
  235.6 0.8 copy-done.16
  236.4 3.6 %all-to-all-start.9 = ((bf16[4,256,512]{2,1,0:T(8,128)(2,1)}), bf16[4,256,512]{2,1,0:T(8,128)(2,1)S(1)}, u32[]{:S(2)}, u32[]{:S(2)}) async-start(bf16[4,256,512]{2,1,0:T(8,128)(2,1)} %get-tuple-element.64), calls=%async_computation.10 | async-start | bytes 2097152 | tf_op jit(solution)/shard_map/all_to_all | solution.py:36
  240.1 8.7 %collective-permute-start.2 = (bf16[4,544,128]{2,1,0:T(8,128)(2,1)S(1)}, bf16[4,544,128]{2,1,0:T(8,128)(2,1)S(1)}, u32[]{:S(2)}, u32[]{:S(2)}) collective-permute-start(bf16[4,544,128]{2,1,0:T(8,128)(2,1)S(1)} %copy-done.17), channel_id=1, source_target_pairs={{0,256},{256,0},{1,257},{257,1},{2,258},{258,2},{3,259},{259,3},{4... | collective-permute-start | bytes 1671176 | tf_op jit(solution)/shard_map/ppermute | solution.py:69
  249.0 1.9 collective-permute-start.3
  250.9 1.1 collective-permute-done.3
  252.1 1.0 add_convert_fusion
  253.1 3.5 %all-to-all-start.10 = ((bf16[4,544,128]{2,1,0:T(8,128)(2,1)}), bf16[4,544,128]{2,1,0:T(8,128)(2,1)S(1)}, u32[]{:S(2)}, u32[]{:S(2)}) async-start(bf16[4,544,128]{2,1,0:T(8,128)(2,1)} %add_convert_fusion), calls=%async_computation.11 | async-start | bytes 1114112 | tf_op jit(solution)/shard_map/all_to_all | solution.py:46
  256.6 0.9 shard_map.169
  257.5 6.1 %all-to-all-done.10 = bf16[4,544,128]{2,1,0:T(8,128)(2,1)S(1)} async-done(((bf16[4,544,128]{2,1,0:T(8,128)(2,1)}), bf16[4,544,128]{2,1,0:T(8,128)(2,1)S(1)}, u32[]{:S(2)}, u32[]{:S(2)}) %all-to-all-start.10) | async-done | bytes 557088 | tf_op jit(solution)/shard_map/all_to_all | solution.py:46
  263.7 8.0 %all-to-all-start.11 = ((bf16[8,64,512]{2,1,0:T(8,128)(2,1)}), bf16[8,64,512]{2,1,0:T(8,128)(2,1)S(1)}, u32[]{:S(2)}, u32[]{:S(2)}) async-start(bf16[8,64,512]{2,1,0:T(8,128)(2,1)} %shard_map.169), calls=%async_computation.12 | async-start | bytes 1048576 | tf_op jit(solution)/shard_map/all_to_all | solution.py:41
  271.7 1.9 collective-permute-start.4
  273.6 14.3 %collective-permute-done.4 = bf16[544,128]{1,0:T(8,128)(2,1)S(1)} collective-permute-done((bf16[544,128]{1,0:T(8,128)(2,1)S(1)}, bf16[544,128]{1,0:T(8,128)(2,1)S(1)}, u32[]{:S(2)}, u32[]{:S(2)}) %collective-permute-start.4) | collective-permute-done | bytes 139296 | tf_op jit(solution)/shard_map/ppermute | solution.py:69
  288.0 13.0 %all-to-all-done.11.refs_0_ = bf16[8,64,512]{2,1,0:T(8,128)(2,1)S(1)} async-done(((bf16[8,64,512]{2,1,0:T(8,128)(2,1)}), bf16[8,64,512]{2,1,0:T(8,128)(2,1)S(1)}, u32[]{:S(2)}, u32[]{:S(2)}) %all-to-all-start.11) | async-done | bytes 524320 | tf_op jit(solution)/shard_map/all_to_all | solution.py:41
  301.1 9.8 %all_to_all.67.refs_0_ = bf16[4,544,128]{2,1,0:T(8,128)(2,1)S(1)} all-to-all(bf16[4,544,128]{2,1,0:T(8,128)(2,1)S(1)} %broadcast_in_dim.48), channel_id=1, replica_groups={{0,32,64,96},{128,160,192,224},{1,33,65,97},{129,161,193,225},{2,34,66,..., dimensions={0} | all-to-all | bytes 1114112 | tf_op jit(solution)/shard_map/all_to_all | solution.py:46
  310.9 15.1 %collective-permute-start.5 = (bf16[4,544,128]{2,1,0:T(8,128)(2,1)S(1)}, bf16[4,544,128]{2,1,0:T(8,128)(2,1)S(1)}, u32[]{:S(2)}, u32[]{:S(2)}) collective-permute-start(bf16[4,544,128]{2,1,0:T(8,128)(2,1)S(1)} %all_to_all.67.refs_0_), channel_id=1, source_target_pairs={{0,256},{256,0},{1,257},{257,1},{2,258},{258,2},{3,259},{259,3},{4... | collective-permute-start | bytes 1671176 | tf_op jit(solution)/shard_map/ppermute | solution.py:69
  325.9 0.5 slice_bitcast_fusion.5
  326.5 0.6 slice_bitcast_fusion.3
  327.0 1.0 shard_map.170
  328.3 0.7 copy_bitcast_fusion
  329.0 1.5 shard_map.171
  (72 shorter events, 1.5 us)
Async XLA Ops:
  7.2 14.9 %copy-start = (bf16[1,1,8,64,1024]{4,3,2,1,0:T(8,128)(2,1)S(1)}, bf16[1,1,8,64,1024]{4,3,2,1,0:T(8,128)(2,1)}, u32[]{:S(2)}) copy-start(bf16[1,1,8,64,1024]{4,3,2,1,0:T(8,128)(2,1)} %param.9) | copy-start | bytes 3145732
  7.2 22.2 %copy-start.2 = (bf16[3,3,1024,32]{2,3,1,0:T(8,128)(2,1)S(1)}, bf16[3,3,1024,32]{2,3,1,0:T(8,128)(2,1)}, u32[]{:S(2)}) copy-start(bf16[3,3,1024,32]{2,3,1,0:T(8,128)(2,1)} %param.10) | copy-start | bytes 1769476
  9.0 25.3 %all-to-all-start = ((bf16[8,32,512]{2,1,0:T(8,128)(2,1)}), bf16[8,32,512]{2,1,0:T(8,128)(2,1)S(1)}, u32[]{:S(2)}, u32[]{:S(2)}) async-start(bf16[8,32,512]{2,1,0:T(8,128)(2,1)} %broadcast_in_dim.39), calls=%async_computation | async-start | bytes 524288 | tf_op jit(solution)/shard_map/all_to_all | solution.py:41
  22.1 6.0 %collective-permute-start = (bf16[64,1024]{1,0:T(8,128)(2,1)S(1)}, bf16[64,1024]{1,0:T(8,128)(2,1)S(1)}, u32[]{:S(2)}, u32[]{:S(2)}) collective-permute-start(bf16[64,1024]{1,0:T(8,128)(2,1)S(1)} %get-tuple-element.79), channel_id=1, source_target_pairs={{32,0},{64,32},{96,64},{128,96},{160,128},{192,160},{224,192},{33,... | collective-permute-start | bytes 393224 | tf_op jit(solution)/shard_map/ppermute | solution.py:416
  23.4 5.9 %collective-permute-start.1 = (bf16[64,1024]{1,0:T(8,128)(2,1)S(1)}, bf16[64,1024]{1,0:T(8,128)(2,1)S(1)}, u32[]{:S(2)}, u32[]{:S(2)}) collective-permute-start(bf16[64,1024]{1,0:T(8,128)(2,1)S(1)} %get-tuple-element.80), channel_id=1, source_target_pairs={{0,32},{32,64},{64,96},{96,128},{128,160},{160,192},{192,224},{1,3... | collective-permute-start | bytes 393224 | tf_op jit(solution)/shard_map/ppermute | solution.py:415
  29.4 27.2 %copy-start.25 = (f32[32]{0:T(128)S(1)}, f32[32]{0:T(128)}, u32[]{:S(2)}) copy-start(f32[32]{0:T(128)} %param.11) | copy-start | bytes 388
  29.4 27.3 %copy-start.26 = (f32[32]{0:T(128)S(1)}, f32[32]{0:T(128)}, u32[]{:S(2)}) copy-start(f32[32]{0:T(128)} %param.12) | copy-start | bytes 388
  34.3 55.3 %copy-start.19 = (bf16[8,32,512]{2,1,0:T(8,128)(2,1)}, bf16[8,32,512]{2,1,0:T(8,128)(2,1)S(1)}, u32[]{:S(2)}) copy-start(bf16[8,32,512]{2,1,0:T(8,128)(2,1)S(1)} %all-to-all-done) | copy-start | bytes 786436
  34.3 36.4 %all-to-all-start.1 = ((f32[8,32,128]{2,1,0:T(8,128)}), f32[8,32,128]{2,1,0:T(8,128)S(1)}, u32[]{:S(2)}, u32[]{:S(2)}) async-start(f32[8,32,128]{2,1,0:T(8,128)} %get-tuple-element.47), calls=%async_computation.1 | async-start | bytes 262144 | tf_op jit(solution)/shard_map/all_to_all | solution.py:50
  71.6 30.9 %copy-start.13 = (f32[32,128]{1,0:T(8,128)}, f32[32,128]{1,0:T(8,128)S(1)}, u32[]{:S(2)}) copy-start(f32[32,128]{1,0:T(8,128)S(1)} %get-tuple-element.63.refs_3_) | copy-start | bytes 49156
  71.6 29.8 %all-to-all-start.2 = ((bf16[8,32,512]{2,1,0:T(8,128)(2,1)}), bf16[8,32,512]{2,1,0:T(8,128)(2,1)S(1)}, u32[]{:S(2)}, u32[]{:S(2)}) async-start(bf16[8,32,512]{2,1,0:T(8,128)(2,1)} %get-tuple-element.48.refs_2_), calls=%async_computation.2 | async-start | bytes 524288 | tf_op jit(solution)/shard_map/all_to_all | solution.py:41
  89.5 44.5 %all-gather.2.cloned.1.call-start = ((), (), s32[]{:S(2)}) async-start(), calls=%async_computation.14 | async-start | bytes 1310720 | tf_op jit(solution)/shard_map/all_gather | solution.py:410
  102.5 4.2 %copy-start.20 = (bf16[1024,128]{1,0:T(8,128)(2,1)S(1)}, bf16[1024,128]{1,0:T(8,128)(2,1)}, u32[]{:S(2)}) copy-start(bf16[1024,128]{1,0:T(8,128)(2,1)} %param.13) | copy-start | bytes 786436
  102.5 23.8 %all-to-all-start.3 = ((bf16[4,256,512]{2,1,0:T(8,128)(2,1)}), bf16[4,256,512]{2,1,0:T(8,128)(2,1)S(1)}, u32[]{:S(2)}, u32[]{:S(2)}) async-start(bf16[4,256,512]{2,1,0:T(8,128)(2,1)} %broadcast_in_dim.43), calls=%async_computation.3 | async-start | bytes 2097152 | tf_op jit(solution)/shard_map/all_to_all | solution.py:36
  106.7 24.8 %copy-start.23 = (f32[128]{0:T(128)S(1)}, f32[128]{0:T(128)}, u32[]{:S(2)}) copy-start(f32[128]{0:T(128)} %param.14) | copy-start | bytes 1540
  106.7 25.5 %copy-start.24 = (f32[128]{0:T(128)S(1)}, f32[128]{0:T(128)}, u32[]{:S(2)}) copy-start(f32[128]{0:T(128)} %param.15) | copy-start | bytes 1540
  106.7 26.2 %copy-start.21 = (bf16[128,1024]{1,0:T(8,128)(2,1)S(1)}, bf16[128,1024]{1,0:T(8,128)(2,1)}, u32[]{:S(2)}) copy-start(bf16[128,1024]{1,0:T(8,128)(2,1)} %param.16) | copy-start | bytes 786436
  127.3 0.7 copy-start.8
  128.0 17.1 %all-to-all-start.4 = ((f32[8,8,128]{2,1,0:T(8,128)}), f32[8,8,128]{2,1,0:T(8,128)S(1)}, u32[]{:S(2)}, u32[]{:S(2)}) async-start(f32[8,8,128]{2,1,0:T(8,128)} %get-tuple-element.50), calls=%async_computation.4 | async-start | bytes 65536 | tf_op jit(solution)/shard_map/all_to_all | solution.py:50
  131.4 54.4 %reduce-scatter.2.cloned.1.call-start = ((), (), s32[]{:S(2)}) async-start(), calls=%async_computation.15 | async-start | bytes 1310720 | tf_op jit(solution)/shard_map/reduce_scatter | solution.py:460
  133.1 12.0 %copy-start.18 = (bf16[4,8,32,128]{3,2,1,0:T(8,128)(2,1)}, bf16[4,8,32,128]{3,2,1,0:T(8,128)(2,1)S(1)}, u32[]{:S(2)}) copy-start(bf16[4,8,32,128]{3,2,1,0:T(8,128)(2,1)S(1)} %copy.38) | copy-start | bytes 786436
  145.1 0.6 copy-start.22
  150.5 17.3 %copy-start.9 = (f32[128,512]{1,0:T(8,128)S(1)}, f32[128,512]{1,0:T(8,128)}, u32[]{:S(2)}) copy-start(f32[128,512]{1,0:T(8,128)} %get-tuple-element.52.refs_1_) | copy-start | bytes 786436
  150.5 17.3 %copy-start.10 = (f32[128,512]{1,0:T(8,128)S(1)}, f32[128,512]{1,0:T(8,128)}, u32[]{:S(2)}) copy-start(f32[128,512]{1,0:T(8,128)} %get-tuple-element.51.refs_0_) | copy-start | bytes 786436
  150.5 17.2 %copy-start.12 = (f32[128,128]{1,0:T(8,128)S(1)}, f32[128,128]{1,0:T(8,128)}, u32[]{:S(2)}) copy-start(f32[128,128]{1,0:T(8,128)} %get-tuple-element.54.refs_3_) | copy-start | bytes 196612
  168.4 1.0 copy-start.6
  169.4 0.6 copy-start.15
  169.4 4.1 %copy-start.11 = (bf16[128,512]{1,0:T(8,128)(2,1)S(1)}, bf16[128,512]{1,0:T(8,128)(2,1)}, u32[]{:S(2)}) copy-start(bf16[128,512]{1,0:T(8,128)(2,1)} %get-tuple-element.57.refs_3_) | copy-start | bytes 393220
  170.0 15.6 %all-to-all-start.6 = ((bf16[4,256,512]{2,1,0:T(8,128)(2,1)}), bf16[4,256,512]{2,1,0:T(8,128)(2,1)S(1)}, u32[]{:S(2)}, u32[]{:S(2)}) async-start(bf16[4,256,512]{2,1,0:T(8,128)(2,1)} %copy-done.6), calls=%async_computation.6 | async-start | bytes 2097152 | tf_op jit(solution)/shard_map/all_to_all | solution.py:36
  173.6 1.2 copy-start.1
  175.5 0.8 copy-start.4
  176.3 56.3 %copy-start.3 = (bf16[3,3,1024,32]{2,3,1,0:T(8,128)(2,1)S(1)}, bf16[3,3,1024,32]{2,3,1,0:T(8,128)(2,1)}, u32[]{:S(2)}) copy-start(bf16[3,3,1024,32]{2,3,1,0:T(8,128)(2,1)} %param.10) | copy-start | bytes 1769476
  185.8 46.8 %copy-start.5 = (bf16[8,256,128]{2,1,0:T(8,128)(2,1)S(1)}, bf16[8,256,128]{2,1,0:T(8,128)(2,1)}, u32[]{:S(2)}) copy-start(bf16[8,256,128]{2,1,0:T(8,128)(2,1)} %copy-done.4) | copy-start | bytes 1572868
  208.9 23.7 %all-to-all-start.8 = ((f32[8,32,128]{2,1,0:T(8,128)}), f32[8,32,128]{2,1,0:T(8,128)S(1)}, u32[]{:S(2)}, u32[]{:S(2)}) async-start(f32[8,32,128]{2,1,0:T(8,128)} %get-tuple-element.62), calls=%async_computation.9 | async-start | bytes 262144 | tf_op jit(solution)/shard_map/all_to_all | solution.py:50
  232.6 0.7 copy-start.14
  235.6 0.8 copy-start.16
  236.4 3.7 %copy-start.17 = (bf16[4,544,128]{2,1,0:T(8,128)(2,1)S(1)}, bf16[4,544,128]{2,1,0:T(8,128)(2,1)}, u32[]{:S(2)}) copy-start(bf16[4,544,128]{2,1,0:T(8,128)(2,1)} %copy-done.16) | copy-start | bytes 1671172
  236.4 16.6 %all-to-all-start.9 = ((bf16[4,256,512]{2,1,0:T(8,128)(2,1)}), bf16[4,256,512]{2,1,0:T(8,128)(2,1)S(1)}, u32[]{:S(2)}, u32[]{:S(2)}) async-start(bf16[4,256,512]{2,1,0:T(8,128)(2,1)} %get-tuple-element.64), calls=%async_computation.10 | async-start | bytes 2097152 | tf_op jit(solution)/shard_map/all_to_all | solution.py:36
  240.1 12.0 %collective-permute-start.2 = (bf16[4,544,128]{2,1,0:T(8,128)(2,1)S(1)}, bf16[4,544,128]{2,1,0:T(8,128)(2,1)S(1)}, u32[]{:S(2)}, u32[]{:S(2)}) collective-permute-start(bf16[4,544,128]{2,1,0:T(8,128)(2,1)S(1)} %copy-done.17), channel_id=1, source_target_pairs={{0,256},{256,0},{1,257},{257,1},{2,258},{258,2},{3,259},{259,3},{4... | collective-permute-start | bytes 1671176 | tf_op jit(solution)/shard_map/ppermute | solution.py:69
  249.0 3.0 collective-permute-start.3
  252.1 4.5 %copy-start.7 = (bf16[256,512]{1,0:T(8,128)(2,1)S(1)}, bf16[256,512]{1,0:T(8,128)(2,1)}, u32[]{:S(2)}) copy-start(bf16[256,512]{1,0:T(8,128)(2,1)} %reduce-scatter.2.cloned.1.call-done.refs_1_) | copy-start | bytes 786436
  253.1 10.6 %all-to-all-start.10 = ((bf16[4,544,128]{2,1,0:T(8,128)(2,1)}), bf16[4,544,128]{2,1,0:T(8,128)(2,1)S(1)}, u32[]{:S(2)}, u32[]{:S(2)}) async-start(bf16[4,544,128]{2,1,0:T(8,128)(2,1)} %add_convert_fusion), calls=%async_computation.11 | async-start | bytes 1114112 | tf_op jit(solution)/shard_map/all_to_all | solution.py:46
  263.7 37.3 %all-to-all-start.11 = ((bf16[8,64,512]{2,1,0:T(8,128)(2,1)}), bf16[8,64,512]{2,1,0:T(8,128)(2,1)S(1)}, u32[]{:S(2)}, u32[]{:S(2)}) async-start(bf16[8,64,512]{2,1,0:T(8,128)(2,1)} %shard_map.169), calls=%async_computation.12 | async-start | bytes 1048576 | tf_op jit(solution)/shard_map/all_to_all | solution.py:41
  271.7 16.2 %collective-permute-start.4 = (bf16[544,128]{1,0:T(8,128)(2,1)S(1)}, bf16[544,128]{1,0:T(8,128)(2,1)S(1)}, u32[]{:S(2)}, u32[]{:S(2)}) collective-permute-start(bf16[544,128]{1,0:T(8,128)(2,1)S(1)} %reduce_sum.12), channel_id=1, source_target_pairs={{0,128},{32,160},{64,192},{96,224},{128,0},{160,32},{192,64},{224,... | collective-permute-start | bytes 417800 | tf_op jit(solution)/shard_map/ppermute | solution.py:69
  310.9 18.1 %collective-permute-start.5 = (bf16[4,544,128]{2,1,0:T(8,128)(2,1)S(1)}, bf16[4,544,128]{2,1,0:T(8,128)(2,1)S(1)}, u32[]{:S(2)}, u32[]{:S(2)}) collective-permute-start(bf16[4,544,128]{2,1,0:T(8,128)(2,1)S(1)} %all_to_all.67.refs_0_), channel_id=1, source_target_pairs={{0,256},{256,0},{1,257},{257,1},{2,258},{258,2},{3,259},{259,3},{4... | collective-permute-start | bytes 1671176 | tf_op jit(solution)/shard_map/ppermute | solution.py:69
Sparse Core Ops, SparseCore 0:
  92.5 35.2 all-gather.1
  150.7 31.1 reduce-scatter.1
